TPU v7x, 32 devices: a whole 2x2x4 slice. The times are simulated.
32 devices in a mesh: dp: 2 (over y), expert: 4 (over x, core), tensor: 4 (over z).
Axes of the slice: x: 2, y: 2, z: 4, core: 2. Of those that a mesh axis runs over, the one named last changes fastest.
Arguments:
- hidden: bfloat16 [1024, 2048], P(('dp', 'expert')), may hold values from -6 to 6
- out_grad: bfloat16 [1024, 7168], P(('dp', 'expert'), 'tensor'), may hold values from -6 to 6
- w_down: bfloat16 [4, 2048, 7168], P('expert', None, 'tensor'), may hold values from -0.125 to 0.125
- routes: int32 [1024, 1], P(('dp', 'expert')), may hold values from 0 to 3; in each aligned block of 128 rows (0 to 127, 128 to 255, ...) at most 64 rows name the same one
- placement: int32 [4], replicated, may hold values from 0 to 3, as said below
Outputs:
- output: bfloat16 [1024, 7168], P(('dp', 'expert'), 'tensor')
- d_hidden: bfloat16 [1024, 2048], P(('dp', 'expert'), 'tensor')
- d_weight: bfloat16 [4, 2048, 7168], P('expert', 'dp', 'tensor')
Inputs may be any that keep to these rules, and one draw needn't show every extreme that they name: `routes`: among the 128 tokens of one index pair of dp and expert, no expert is named more than 64 times, a bound that some block reaches. `placement`: each expert is held at exactly one index.
All inputs are finite; a program needn't handle non-finite values.
Results may differ from a plain program's by a relative error of at most 0.009.
Values may be sent and summed in bfloat16 or wider, within the bound.
No kernel may reach another device: no remote copies, remote signals or barrier semaphores. Data moves between devices by JAX's collectives and lax.ppermute only.
A program may use at most 64 MiB of HBM per device.

v0:
```python
import jax
import jax.numpy as jnp
from jax import lax
from jax.sharding import PartitionSpec as P


def shards(hidden, out_grad, w_down, routes, placement):
    experts = lax.axis_size("expert")
    tok = hidden.shape[0]
    width = hidden.shape[1]
    cols = out_grad.shape[1]
    cap = 2 * tok // experts
    slots = experts * cap
    chosen = routes == jnp.arange(placement.shape[0], dtype=jnp.int32)[None, :]
    target = jnp.sum(jnp.where(chosen, placement[None, :], 0), axis=1)
    landing = target[:, None] == jnp.arange(experts, dtype=jnp.int32)[None, :]
    counted = jnp.cumsum(landing.astype(jnp.int32), axis=0) - 1
    within = jnp.sum(jnp.where(landing, counted, 0), axis=1)
    position = target * cap + within
    picker = (jnp.arange(slots, dtype=jnp.int32)[:, None] == position[None, :]).astype(jnp.bfloat16)
    send_hidden = jnp.dot(picker, hidden, preferred_element_type=jnp.float32).astype(jnp.bfloat16)
    send_grad = jnp.dot(picker, out_grad, preferred_element_type=jnp.float32).astype(jnp.bfloat16)
    recv_hidden, recv_grad = (
        lax.all_to_all(
            send_hidden.reshape(experts, cap, -1), "expert", split_axis=0, concat_axis=0, tiled=True
        ),
        lax.all_to_all(
            send_grad.reshape(experts, cap, cols), "expert", split_axis=0, concat_axis=0, tiled=True
        ),
    )
    slot_hidden = recv_hidden.reshape(slots, -1)
    slot_grad = recv_grad.reshape(slots, cols)
    weight = w_down[0]
    out_rows = jnp.dot(slot_hidden, weight, preferred_element_type=jnp.float32).astype(jnp.bfloat16)
    partial_value = lax.dot_general(
        slot_grad, weight, (((1,), (1,)), ((), ())), preferred_element_type=jnp.float32
    )
    hidden_grad = lax.psum_scatter(partial_value, "tensor", scatter_dimension=1, tiled=True).astype(
        jnp.bfloat16
    )
    back_out, back_grad = (
        lax.all_to_all(
            out_rows.reshape(experts, cap, cols), "expert", split_axis=0, concat_axis=0, tiled=True
        ),
        lax.all_to_all(
            hidden_grad.reshape(experts, cap, -1), "expert", split_axis=0, concat_axis=0, tiled=True
        ),
    )
    output = jnp.einsum(
        "rt,rd->td", picker, back_out.reshape(slots, cols), preferred_element_type=jnp.float32
    ).astype(jnp.bfloat16)
    d_hidden = jnp.einsum(
        "rt,rd->td", picker, back_grad.reshape(slots, -1), preferred_element_type=jnp.float32
    ).astype(jnp.bfloat16)
    share = width // lax.axis_size("dp")
    mine = lax.axis_index("dp") * share
    part_h = lax.dynamic_slice_in_dim(
        lax.all_gather(slot_hidden, "dp", axis=0, tiled=True), mine, share, 1
    ).reshape(-1, slots, share)
    part_g = lax.all_gather(slot_grad, "dp", axis=0, tiled=True).reshape(-1, slots, cols)
    terms = jnp.einsum("krf,krd->kfd", part_h, part_g, preferred_element_type=jnp.float32)
    rounded = lax.optimization_barrier(terms.astype(jnp.bfloat16))
    summed = jnp.sum(rounded.astype(jnp.float32), axis=0)
    d_weight = summed.astype(jnp.bfloat16)[None]
    return (output, d_hidden, d_weight)


def solution(mesh):
    in_specs = (
        P(("dp", "expert"), None),
        P(("dp", "expert"), "tensor"),
        P("expert", None, "tensor"),
        P(("dp", "expert"), None),
        P(),
    )
    out_specs = (
        P(("dp", "expert"), "tensor"),
        P(("dp", "expert"), "tensor"),
        P("expert", "dp", "tensor"),
    )
    return jax.shard_map(shards, mesh=mesh, in_specs=in_specs, out_specs=out_specs, check_vma=False)
```

profile of v0, /device:TPU:0, one launch (start us, length us, event | category | flops | bytes accessed | tf_op | source)
XLA Modules:
  0.0 123.1 jit_solution(1672511632533310575)
XLA Ops:
  8.0 0.0 all-gather.3.cloned.1.call-start
  8.1 0.9 select_reduce_fusion.1
  9.0 0.1 fusion.11
  9.1 0.2 reduce_window_sum.11
  9.3 0.2 select_reduce_fusion
  9.5 0.4 convolution_convert_fusion.2
  9.9 18.6 %all_to_all.20 = bf16[4,64,2048]{2,1,0:T(8,128)(2,1)} all-to-all(bf16[4,64,2048]{2,1,0:T(8,128)(2,1)S(1)} %bitcast.30), channel_id=1, replica_groups=mesh['dp'=2,'expert'=4,'tensor'=4] {'expert'}, dimensions={0} | all-to-all | bytes 2097152 | tf_op jit(solution)/shard_map/all_to_all | solution.py:24
  28.5 0.0 reduce-scatter.2.cloned.1.call-start
  28.6 0.4 convolution_convert_fusion.1
  29.0 15.5 %all_to_all.21 = bf16[4,64,1792]{2,1,0:T(8,128)(2,1)S(1)} all-to-all(bf16[4,64,1792]{2,1,0:T(8,128)(2,1)S(1)} %bitcast.34), channel_id=1, replica_groups=mesh['dp'=2,'expert'=4,'tensor'=4] {'expert'}, dimensions={0} | all-to-all | bytes 1835008 | tf_op jit(solution)/shard_map/all_to_all | solution.py:27
  44.4 6.9 %fusion = f32[256,2048]{1,0:T(8,128)} fusion(bf16[256,1792]{1,0:T(8,128)(2,1)S(1)} %bitcast.31, bf16[1,2048,1792]{2,1,0:T(8,128)(2,1)} %param.7), kind=kOutput, calls=%fused_computation | convolution fusion | flops 1879048192 | bytes 10354688 | tf_op jit(solution)/shard_map/dot_general | solution.py:35
  51.3 0.0 all-gather.5.cloned.1.call-start
  51.4 0.7 all-gather.5.cloned.1.call-update
  52.1 6.1 %fusion.4 = bf16[256,1792]{1,0:T(8,128)(2,1)} fusion(bf16[256,2048]{1,0:T(8,128)(2,1)S(1)} %bitcast.29, bf16[1,2048,1792]{2,1,0:T(8,128)(2,1)} %param.7), kind=kOutput, calls=%fused_computation.5 | convolution fusion | flops 1879506944 | bytes 9306112 | tf_op jit(solution)/shard_map/dot_general | solution.py:34
  58.2 3.5 %all-to-all-start.1 = ((bf16[4,64,1792]{2,1,0:T(8,128)(2,1)}), bf16[4,64,1792]{2,1,0:T(8,128)(2,1)S(1)}, u32[]{:S(2)}, u32[]{:S(2)}) async-start(bf16[4,64,1792]{2,1,0:T(8,128)(2,1)} %bitcast.4), calls=%async_computation.1 | async-start | bytes 1835008 | tf_op jit(solution)/shard_map/all_to_all | solution.py:42
  61.7 13.0 %all-to-all-done.1 = bf16[4,64,1792]{2,1,0:T(8,128)(2,1)S(1)} async-done(((bf16[4,64,1792]{2,1,0:T(8,128)(2,1)}), bf16[4,64,1792]{2,1,0:T(8,128)(2,1)S(1)}, u32[]{:S(2)}, u32[]{:S(2)}) %all-to-all-start.1) | async-done | bytes 917536 | tf_op jit(solution)/shard_map/all_to_all | solution.py:42
  74.7 1.1 convolution_convert_fusion.3
  75.8 1.3 %constant_dynamic-slice_fusion = bf16[512,1024]{1,0:T(8,128)(2,1)S(1)} fusion(bf16[512,2048]{1,0:T(8,128)(2,1)} %all-gather.3.cloned.1.call-done, s32[]{:T(128)S(6)} %select_n.13), kind=kLoop, calls=%fused_computation.21 | loop fusion | bytes 2097156 | tf_op jit(solution)/shard_map/dynamic_slice | solution.py:57
  77.1 18.6 %reduce-scatter.2.cloned.1.call-done = f32[256,512]{1,0:T(8,128)} async-done(((f32[256,2048]{1,0:T(8,128)}), f32[256,512]{1,0:T(8,128)}) %reduce-scatter.2.cloned.1.call-update) | async-done | bytes 524304 | tf_op jit(solution)/shard_map/reduce_scatter | solution.py:38
  95.8 1.8 %convert_element_type.32 = bf16[256,512]{1,0:T(8,128)(2,1)} convert(f32[256,512]{1,0:T(8,128)} %reduce-scatter.2.cloned.1.call-done) | non-fusion elementwise | flops 131072 | bytes 786432 | tf_op jit(solution)/shard_map/convert_element_type | solution.py:38
  97.6 3.4 %all-to-all-start.3 = ((bf16[4,64,512]{2,1,0:T(8,128)(2,1)}), bf16[4,64,512]{2,1,0:T(8,128)(2,1)S(1)}, u32[]{:S(2)}, u32[]{:S(2)}) async-start(bf16[4,64,512]{2,1,0:T(8,128)(2,1)} %bitcast.8), calls=%async_computation.4 | async-start | bytes 524288 | tf_op jit(solution)/shard_map/all_to_all | solution.py:45
  101.0 6.6 %convolution_convert_fusion = bf16[2,1024,1792]{2,1,0:T(8,128)(2,1)} fusion(bf16[2,256,1024]{2,1,0:T(8,128)(2,1)S(1)} %bitcast.27, bf16[2,256,1792]{2,1,0:T(8,128)(2,1)} %bitcast.36), kind=kOutput, calls=%fused_computation.4 | convolution fusion | flops 1882718208 | bytes 10223616 | tf_op jit(solution)/shard_map/krf,krd->kfd/dot_general | solution.py:61
  107.6 7.1 %reduce_sum.32 = bf16[1024,1792]{1,0:T(8,128)(2,1)} reduce(bf16[2,1024,1792]{2,1,0:T(8,128)(2,1)} %convolution_convert_fusion, bf16[]{:T(256)} %constant.22.clone.1), dimensions={0}, to_apply=%region_4.5 | reduce | flops 1835008 | bytes 11010050 | tf_op jit(solution)/shard_map/reduce_sum | solution.py:63
  114.7 0.9 convolution_convert_fusion.4
  (14 shorter events, 0.1 us)
Async XLA Ops:
  8.0 1.5 %copy-start = (bf16[128,2048]{1,0:T(8,128)(2,1)S(1)}, bf16[128,2048]{1,0:T(8,128)(2,1)}, u32[]{:S(2)}) copy-start(bf16[128,2048]{1,0:T(8,128)(2,1)} %param.5) | copy-start | bytes 1572868
  8.0 20.5 %copy-start.3 = (bf16[128,1792]{1,0:T(8,128)(2,1)S(1)}, bf16[128,1792]{1,0:T(8,128)(2,1)}, u32[]{:S(2)}) copy-start(bf16[128,1792]{1,0:T(8,128)(2,1)} %param.6) | copy-start | bytes 1376260
  8.0 67.8 %all-gather.3.cloned.1.call-start = ((), (), s32[]{:S(2)}) async-start(), calls=%async_computation.6 | async-start | bytes 3145728 | tf_op jit(solution)/shard_map/all_gather | solution.py:58
  28.5 67.3 %reduce-scatter.2.cloned.1.call-start = ((), (), s32[]{:S(2)}) async-start(), calls=%async_computation.5 | async-start | bytes 2621440 | tf_op jit(solution)/shard_map/reduce_scatter | solution.py:38
  44.4 6.9 %copy-start.2 = (bf16[4,64,1792]{2,1,0:T(8,128)(2,1)}, bf16[4,64,1792]{2,1,0:T(8,128)(2,1)S(1)}, u32[]{:S(2)}) copy-start(bf16[4,64,1792]{2,1,0:T(8,128)(2,1)S(1)} %all_to_all.21) | copy-start | bytes 2752516
  44.4 7.7 %copy-start.1 = (bf16[4,64,2048]{2,1,0:T(8,128)(2,1)S(1)}, bf16[4,64,2048]{2,1,0:T(8,128)(2,1)}, u32[]{:S(2)}) copy-start(bf16[4,64,2048]{2,1,0:T(8,128)(2,1)} %all_to_all.20) | copy-start | bytes 3145732
  51.3 49.7 %all-gather.5.cloned.1.call-start = ((), (), s32[]{:S(2)}) async-start(), calls=%async_computation.7 | async-start | bytes 2752512 | tf_op jit(solution)/shard_map/all_gather | solution.py:60
  58.2 16.5 %all-to-all-start.1 = ((bf16[4,64,1792]{2,1,0:T(8,128)(2,1)}), bf16[4,64,1792]{2,1,0:T(8,128)(2,1)S(1)}, u32[]{:S(2)}, u32[]{:S(2)}) async-start(bf16[4,64,1792]{2,1,0:T(8,128)(2,1)} %bitcast.4), calls=%async_computation.1 | async-start | bytes 1835008 | tf_op jit(solution)/shard_map/all_to_all | solution.py:42
  97.6 17.2 %all-to-all-start.3 = ((bf16[4,64,512]{2,1,0:T(8,128)(2,1)}), bf16[4,64,512]{2,1,0:T(8,128)(2,1)S(1)}, u32[]{:S(2)}, u32[]{:S(2)}) async-start(bf16[4,64,512]{2,1,0:T(8,128)(2,1)} %bitcast.8), calls=%async_computation.4 | async-start | bytes 524288 | tf_op jit(solution)/shard_map/all_to_all | solution.py:45
Sparse Core Ops, SparseCore 0:
  28.6 33.9 all-gather.2
  64.2 30.1 all-gather.4
Sparse Core Ops, SparseCore 1:
  51.4 44.3 reduce-scatter.1
where the time goes:
time: 124 us; the launch traced here: 123 us
  blocking collectives  34.1 us (28%)
  waiting for transfers between devices  32.4 us (26%)
  matrix products  22.4 us (18%)
  between operations  15.6 us (13%)
  other arithmetic  10.3 us (8%)
  starting transfers between devices  7.03 us (6%)
  local copies, waits for them, and re-layouts  1.34 us (1%)
    reduce_scatter x1, waiting for transfers between devices, shards(): lax.psum_scatter(partial_value, 'tensor', scatter_dimension=1, tiled=True)  18.6 us
    all_to_all x1, blocking collectives, shards(): lax.all_to_all(send_hidden.reshape(experts, cap, -1), 'expert', split_axi...  18.6 us
    all_to_all x1, blocking collectives, shards(): lax.all_to_all(send_grad.reshape(experts, cap, cols), 'expert', split_axi...  15.5 us
    all_to_all x1, waiting for transfers between devices, shards(): lax.all_to_all(out_rows.reshape(experts, cap, cols), 'expert', split_axis...  13 us
    reduce_sum x1, other arithmetic, shards(): summed = jnp.sum(rounded.astype(jnp.float32), axis=0)  7.14 us
    dot_general x1, matrix products, shards(): lax.dot_general(slot_grad, weight, (((1,), (1,)), ((), ())), preferred_el...  6.89 us
    dot_general x1, matrix products, shards(): jnp.einsum('krf,krd->kfd', part_h, part_g, preferred_element_type=jnp.flo...  6.59 us
    dot_general x1, matrix products, shards(): jnp.dot(slot_hidden, weight, preferred_element_type=jnp.float32)  6.07 us
  transfers between devices with their start and end apart: 5, of which 2 were waited for; matrix products, arithmetic and copies ran while one was open for 25% of the time, Pallas kernels for 0%

commit v1 on v0

v1 whole, which is shorter than its diff:
```python
import jax
import jax.numpy as jnp
from jax import lax
from jax.sharding import PartitionSpec as P


def swap(value, axis, offset):
    size = lax.axis_size(axis)
    return lax.ppermute(value, axis, [(i, i ^ offset) for i in range(size)])


def route(routes, placement, experts, cap):
    chosen = routes == jnp.arange(placement.shape[0], dtype=jnp.int32)[None, :]
    target = jnp.sum(jnp.where(chosen, placement[None, :], 0), axis=1)
    landing = target[:, None] == jnp.arange(experts, dtype=jnp.int32)[None, :]
    counted = jnp.cumsum(landing.astype(jnp.int32), axis=0) - 1
    within = jnp.sum(jnp.where(landing, counted, 0), axis=1)
    return target, within


def few(hidden, out_grad, w_down, routes, placement):
    experts = lax.axis_size("expert")
    tensors = lax.axis_size("tensor")
    tok, width = hidden.shape
    cols = out_grad.shape[1]
    cap = 2 * tok // experts
    slots = experts * cap
    near = experts // 2 * cap
    target, within = route(routes, placement, experts, cap)
    me = lax.axis_index("expert")
    position = jnp.bitwise_xor(target, me) * cap + within
    picker = (jnp.arange(slots, dtype=jnp.int32)[:, None] == position[None, :]).astype(jnp.bfloat16)
    send_grad = jnp.dot(picker, out_grad, preferred_element_type=jnp.float32).astype(jnp.bfloat16)
    send_hidden = jnp.dot(picker, hidden, preferred_element_type=jnp.float32).astype(jnp.bfloat16)

    def exchange(value):
        blocks = [value[k * cap : (k + 1) * cap] for k in range(experts)]
        return [blocks[0]] + [swap(blocks[k], "expert", k) for k in range(1, experts)]

    grad = exchange(send_grad)
    hid = exchange(send_hidden)
    weight = w_down[0]
    half = experts // 2
    share = width // lax.axis_size("dp")
    column = width // tensors
    mine = lax.axis_index("dp") * share
    z = lax.axis_index("tensor")
    outs, backs, rows_h, rows_g = [], [], [], []
    for group in range(2):
        g = jnp.concatenate(grad[group * half : (group + 1) * half], axis=0)
        h = jnp.concatenate(hid[group * half : (group + 1) * half], axis=0)
        partial = lax.dot_general(g, weight, (((1,), (1,)), ((), ())), preferred_element_type=jnp.float32)
        partial = partial.astype(jnp.bfloat16)
        total = lax.dynamic_slice_in_dim(partial, z * column, column, 1).astype(jnp.float32)
        for k in range(1, tensors):
            piece = lax.dynamic_slice_in_dim(partial, jnp.bitwise_xor(z, k) * column, column, 1)
            total = total + swap(piece, "tensor", k).astype(jnp.float32)
        total = total.astype(jnp.bfloat16)
        out = jnp.dot(h, weight, preferred_element_type=jnp.float32).astype(jnp.bfloat16)
        for k in range(half):
            offset = group * half + k
            for value, into in ((out, outs), (total, backs)):
                block = value[k * cap : (k + 1) * cap]
                into.append(swap(block, "expert", offset) if offset else block)
        rows_h.append(lax.dynamic_slice_in_dim(h, mine, share, 1))
        rows_g.append(g)
        for k in range(1, lax.axis_size("dp")):
            other = jnp.bitwise_xor(lax.axis_index("dp"), k) * share
            rows_h.append(swap(lax.dynamic_slice_in_dim(h, other, share, 1), "dp", k))
            rows_g.append(swap(g, "dp", k))

    def place(blocks):
        return jnp.einsum(
            "rt,rd->td", picker, jnp.concatenate(blocks, axis=0), preferred_element_type=jnp.float32
        ).astype(jnp.bfloat16)

    d_weight = lax.dot_general(
        jnp.concatenate(rows_h, axis=0),
        jnp.concatenate(rows_g, axis=0),
        (((0,), (0,)), ((), ())),
        preferred_element_type=jnp.float32,
    ).astype(jnp.bfloat16)[None]
    return place(outs), place(backs), d_weight


def many(hidden, out_grad, w_down, routes, placement):
    experts = lax.axis_size("expert")
    tok = hidden.shape[0]
    width = hidden.shape[1]
    cols = out_grad.shape[1]
    cap = 2 * tok // experts
    slots = experts * cap
    target, within = route(routes, placement, experts, cap)
    position = target * cap + within
    picker = (jnp.arange(slots, dtype=jnp.int32)[:, None] == position[None, :]).astype(jnp.bfloat16)
    send_hidden = jnp.dot(picker, hidden, preferred_element_type=jnp.float32).astype(jnp.bfloat16)
    send_grad = jnp.dot(picker, out_grad, preferred_element_type=jnp.float32).astype(jnp.bfloat16)

    def exchange(value):
        return lax.all_to_all(
            value.reshape(experts, cap, -1), "expert", split_axis=0, concat_axis=0, tiled=True
        ).reshape(slots, -1)

    slot_hidden, slot_grad = exchange(send_hidden), exchange(send_grad)
    weight = w_down[0]
    out_rows = jnp.dot(slot_hidden, weight, preferred_element_type=jnp.float32).astype(jnp.bfloat16)
    partial_value = lax.dot_general(
        slot_grad, weight, (((1,), (1,)), ((), ())), preferred_element_type=jnp.float32
    )
    hidden_grad = lax.psum_scatter(partial_value, "tensor", scatter_dimension=1, tiled=True).astype(
        jnp.bfloat16
    )

    def place(rows):
        return jnp.einsum("rt,rd->td", picker, rows, preferred_element_type=jnp.float32).astype(jnp.bfloat16)

    output, d_hidden = place(exchange(out_rows)), place(exchange(hidden_grad))
    share = width // lax.axis_size("dp")
    mine = lax.axis_index("dp") * share
    part_h = lax.dynamic_slice_in_dim(
        lax.all_gather(slot_hidden, "dp", axis=0, tiled=True), mine, share, 1
    ).reshape(-1, slots, share)
    part_g = lax.all_gather(slot_grad, "dp", axis=0, tiled=True).reshape(-1, slots, cols)
    terms = jnp.einsum("krf,krd->kfd", part_h, part_g, preferred_element_type=jnp.float32)
    rounded = lax.optimization_barrier(terms.astype(jnp.bfloat16))
    summed = jnp.sum(rounded.astype(jnp.float32), axis=0)
    return output, d_hidden, summed.astype(jnp.bfloat16)[None]


def solution(mesh):
    in_specs = (
        P(("dp", "expert"), None),
        P(("dp", "expert"), "tensor"),
        P("expert", None, "tensor"),
        P(("dp", "expert"), None),
        P(),
    )
    out_specs = (
        P(("dp", "expert"), "tensor"),
        P(("dp", "expert"), "tensor"),
        P("expert", "dp", "tensor"),
    )
    small = all(mesh.shape[a] in (2, 4) for a in ("dp", "expert", "tensor"))
    shards = few if small else many
    return jax.shard_map(shards, mesh=mesh, in_specs=in_specs, out_specs=out_specs, check_vma=False)
```

time: 124 us -> 76.3 us (0.62)
  blocking collectives: 34.1 us -> 0 us
  starting transfers between devices: 7.03 us -> 22.8 us
  between operations: 15.6 us -> 0.94 us
  other arithmetic: 10.3 us -> 1.58 us
  waiting for transfers between devices: 32.4 us -> 27.9 us
    all_to_all x2 -> x0, blocking collectives: 34.1 us -> none  [the longest x1 18.6 us: shards(): lax.all_to_all(send_hidden.reshape(experts, cap, -1), 'expert', split_axi...]
    ppermute x0 -> x22, waiting for transfers between devices: none -> 27.9 us  [swap(): return lax.ppermute(value, axis, [(i, i ^ offset) for i in range(size)])]
    ppermute x0 -> x22, starting transfers between devices: none -> 22.8 us  [swap(): return lax.ppermute(value, axis, [(i, i ^ offset) for i in range(size)])]
    reduce_scatter x1 -> x0, waiting for transfers between devices: 18.6 us -> none  [shards(): lax.psum_scatter(partial_value, 'tensor', scatter_dimension=1, tiled=True)]
    all_to_all x2 -> x0, waiting for transfers between devices: 13 us -> none  [the longest x1 13 us: shards(): lax.all_to_all(out_rows.reshape(experts, cap, cols), 'expert', split_axis...]
    reduce_sum x3 -> x2, other arithmetic: 8.23 us -> 1.07 us  [the longest x1 0.9 us: route(): target = jnp.sum(jnp.where(chosen, placement[None, :], 0), axis=1)]
    all_to_all x2 -> x0, starting transfers between devices: 6.91 us -> none  [the longest x1 3.5 us: shards(): lax.all_to_all(out_rows.reshape(experts, cap, cols), 'expert', split_axis...]
    convert_element_type x2 -> x3, other arithmetic: 1.89 us -> 0.26 us  [the longest x2 0.17 us: few(): total = total.astype(jnp.bfloat16)]
  transfers between devices with their start and end apart: 5 -> 22, of which waited for: 2 -> 9; matrix products, arithmetic and copies ran while one was open for 25% -> 22% of each run, Pallas kernels for 0% -> 0%
where the time goes in v1:
time: 76.3 us; the launch traced here: 76.1 us
  waiting for transfers between devices  27.9 us (37%)
  starting transfers between devices  22.8 us (30%)
  matrix products  21.5 us (28%)
  other arithmetic  1.58 us (2%)
  local copies, waits for them, and re-layouts  1.32 us (2%)
  between operations  0.94 us (1%)
    ppermute x22, waiting for transfers between devices, swap(): return lax.ppermute(value, axis, [(i, i ^ offset) for i in range(size)])  27.9 us
    ppermute x22, starting transfers between devices, swap(): return lax.ppermute(value, axis, [(i, i ^ offset) for i in range(size)])  22.8 us
    dot_general x2, matrix products, few(): lax.dot_general(g, weight, (((1,), (1,)), ((), ())), preferred_element_ty...  8.18 us
    dot_general x2, matrix products, few(): jnp.dot(h, weight, preferred_element_type=jnp.float32).astype(jnp.bfloat16)  5.52 us
    dot_general x1, matrix products, few(): lax.dot_general(jnp.concatenate(rows_h, axis=0), jnp.concatenate(rows_g,...  3.98 us
    dot_general x2, matrix products, place(): jnp.einsum('rt,rd->td', picker, jnp.concatenate(blocks, axis=0), preferre...  1.99 us
  transfers between devices with their start and end apart: 22, of which 9 were waited for; matrix products, arithmetic and copies ran while one was open for 22% of the time, Pallas kernels for 0%

profile of v1, /device:TPU:0, one launch (start us, length us, event | category | flops | bytes accessed | tf_op | source)
XLA Modules:
  0.0 76.1 jit_solution(16960191136819998837)
XLA Ops:
  2.0 1.4 %convolution_convert_fusion.1 = bf16[256,1792]{1,0:T(8,128)(2,1)S(1)} fusion(bf16[128,1792]{1,0:T(8,128)(2,1)} %param.6, s32[128]{0:T(128)S(1)} %multiply_add_fusion), kind=kOutput, calls=%fused_computation.10 | convolution fusion | flops 117932032 | bytes 1376768 | tf_op jit(solution)/shard_map/dot_general | solution.py:33
  5.3 2.7 %collective-permute-start.3 = (bf16[64,2048]{1,0:T(8,128)(2,1)S(1)}, bf16[64,2048]{1,0:T(8,128)(2,1)S(1)}, u32[]{:S(2)}, u32[]{:S(2)}) collective-permute-start(bf16[64,2048]{1,0:T(8,128)(2,1)S(1)} %get-tuple-element.4), channel_id=1, source_target_pairs={{0,12},{4,8},{8,4},{12,0},{1,13},{5,9},{9,5},{13,1},{2,14},{6,10},... | collective-permute-start | bytes 786440 | tf_op jit(solution)/shard_map/ppermute | solution.py:9
  8.1 2.0 %collective-permute-start.12 = (bf16[64,1792]{1,0:T(8,128)(2,1)S(1)}, bf16[64,1792]{1,0:T(8,128)(2,1)S(1)}, u32[]{:S(2)}, u32[]{:S(2)}) collective-permute-start(bf16[64,1792]{1,0:T(8,128)(2,1)S(1)} %get-tuple-element.8), channel_id=1, source_target_pairs={{0,12},{4,8},{8,4},{12,0},{1,13},{5,9},{9,5},{13,1},{2,14},{6,10},... | collective-permute-start | bytes 688136 | tf_op jit(solution)/shard_map/ppermute | solution.py:9
  10.1 5.7 %fusion.15 = bf16[128,2048]{1,0:T(8,128)(2,1)S(1)} fusion(bf16[1,2048,1792]{2,1,0:T(8,128)(2,1)} %param.7, bf16[64,1792]{1,0:T(8,128)(2,1)S(1)} %collective-permute-done.6, bf16[64,1792]{1,0:T(8,128)(2,1)S(1)} %get-tuple-element.11), kind=kOutput, calls=%fused_computation.14 | convolution fusion | flops 940703744 | bytes 8323072 | tf_op jit(solution)/shard_map/dot_general | solution.py:52
  15.8 1.6 %collective-permute-start.7 = (bf16[128,512]{1,0:T(8,128)(2,1)S(1)}, bf16[128,512]{1,0:T(8,128)(2,1)S(1)}, u32[]{:S(2)}, u32[]{:S(2)}) collective-permute-start(bf16[128,512]{1,0:T(8,128)(2,1)S(1)} %get-tuple-element.16), channel_id=1, source_target_pairs={{0,1},{1,0},{2,3},{3,2},{4,5},{5,4},{6,7},{7,6},{8,9},{9,8},{10,11... | collective-permute-start | bytes 393224 | tf_op jit(solution)/shard_map/ppermute | solution.py:9
  17.5 2.5 %collective-permute-start.9 = (bf16[128,512]{1,0:T(8,128)(2,1)S(1)}, bf16[128,512]{1,0:T(8,128)(2,1)S(1)}, u32[]{:S(2)}, u32[]{:S(2)}) collective-permute-start(bf16[128,512]{1,0:T(8,128)(2,1)S(1)} %get-tuple-element.17), channel_id=1, source_target_pairs={{0,3},{1,2},{2,1},{3,0},{4,7},{5,6},{6,5},{7,4},{8,11},{9,10},{10,... | collective-permute-start | bytes 393224 | tf_op jit(solution)/shard_map/ppermute | solution.py:9
  20.1 4.4 %fusion.9 = bf16[128,1792]{1,0:T(8,128)(2,1)S(1)} fusion(bf16[1,2048,1792]{2,1,0:T(8,128)(2,1)} %param.7, bf16[64,2048]{1,0:T(8,128)(2,1)S(1)} %collective-permute-done, bf16[64,2048]{1,0:T(8,128)(2,1)S(1)} %get-tuple-element.3), kind=kOutput, calls=%fused_computation.12 | convolution fusion | flops 940802048 | bytes 8323072 | tf_op jit(solution)/shard_map/dot_general | solution.py:59
  24.7 1.6 %collective-permute-start.20 = (bf16[128,1792]{1,0:T(8,128)(2,1)S(1)}, bf16[128,1792]{1,0:T(8,128)(2,1)S(1)}, u32[]{:S(2)}, u32[]{:S(2)}) collective-permute-start(bf16[128,1792]{1,0:T(8,128)(2,1)S(1)} %pad_maximum_fusion.2), channel_id=1, source_target_pairs={{0,16},{16,0},{1,17},{17,1},{2,18},{18,2},{3,19},{19,3},{4,20},{20... | collective-permute-start | bytes 1376264 | tf_op jit(solution)/shard_map/ppermute | solution.py:9
  28.3 4.8 %collective-permute-done.8 = bf16[128,512]{1,0:T(8,128)(2,1)S(1)} collective-permute-done((bf16[128,512]{1,0:T(8,128)(2,1)S(1)}, bf16[128,512]{1,0:T(8,128)(2,1)S(1)}, u32[]{:S(2)}, u32[]{:S(2)}) %collective-permute-start.8) | collective-permute-done | bytes 131104 | tf_op jit(solution)/shard_map/ppermute | solution.py:9
  33.1 1.5 %collective-permute-start.18 = (bf16[128,1024]{1,0:T(8,128)(2,1)S(1)}, bf16[128,1024]{1,0:T(8,128)(2,1)S(1)}, u32[]{:S(2)}, u32[]{:S(2)}) collective-permute-start(bf16[128,1024]{1,0:T(8,128)(2,1)S(1)} %get-tuple-element.13), channel_id=1, source_target_pairs={{0,16},{16,0},{1,17},{17,1},{2,18},{18,2},{3,19},{19,3},{4,20},{20... | collective-permute-start | bytes 786440 | tf_op jit(solution)/shard_map/ppermute | solution.py:9
  34.7 3.0 %collective-permute-done.20 = bf16[128,1792]{1,0:T(8,128)(2,1)S(1)} collective-permute-done((bf16[128,1792]{1,0:T(8,128)(2,1)S(1)}, bf16[128,1792]{1,0:T(8,128)(2,1)S(1)}, u32[]{:S(2)}, u32[]{:S(2)}) %collective-permute-start.20) | collective-permute-done | bytes 458784 | tf_op jit(solution)/shard_map/ppermute | solution.py:9
  37.8 2.5 %fusion.18 = bf16[128,2048]{1,0:T(8,128)(2,1)S(1)} fusion(bf16[128,1792]{1,0:T(8,128)(2,1)S(1)} %get-tuple-element.27, bf16[1,2048,1792]{2,1,0:T(8,128)(2,1)S(1)} %bitcast.26), kind=kOutput, calls=%fused_computation.15 | convolution fusion | flops 939786240 | bytes 8323072 | tf_op jit(solution)/shard_map/dot_general | solution.py:52
  40.3 2.4 %collective-permute-start.13 = (bf16[128,512]{1,0:T(8,128)(2,1)S(1)}, bf16[128,512]{1,0:T(8,128)(2,1)S(1)}, u32[]{:S(2)}, u32[]{:S(2)}) collective-permute-start(bf16[128,512]{1,0:T(8,128)(2,1)S(1)} %get-tuple-element.19), channel_id=1, source_target_pairs={{0,1},{1,0},{2,3},{3,2},{4,5},{5,4},{6,7},{7,6},{8,9},{9,8},{10,11... | collective-permute-start | bytes 393224 | tf_op jit(solution)/shard_map/ppermute | solution.py:9
  42.7 2.5 %collective-permute-start.15 = (bf16[128,512]{1,0:T(8,128)(2,1)S(1)}, bf16[128,512]{1,0:T(8,128)(2,1)S(1)}, u32[]{:S(2)}, u32[]{:S(2)}) collective-permute-start(bf16[128,512]{1,0:T(8,128)(2,1)S(1)} %get-tuple-element.20), channel_id=1, source_target_pairs={{0,3},{1,2},{2,1},{3,0},{4,7},{5,6},{6,5},{7,4},{8,11},{9,10},{10,... | collective-permute-start | bytes 393224 | tf_op jit(solution)/shard_map/ppermute | solution.py:9
  45.2 1.2 %collective-permute-done.13 = bf16[128,512]{1,0:T(8,128)(2,1)S(1)} collective-permute-done((bf16[128,512]{1,0:T(8,128)(2,1)S(1)}, bf16[128,512]{1,0:T(8,128)(2,1)S(1)}, u32[]{:S(2)}, u32[]{:S(2)}) %collective-permute-start.13) | collective-permute-done | bytes 131104 | tf_op jit(solution)/shard_map/ppermute | solution.py:9
  47.0 2.7 %collective-permute-done.15 = bf16[128,512]{1,0:T(8,128)(2,1)S(1)} collective-permute-done((bf16[128,512]{1,0:T(8,128)(2,1)S(1)}, bf16[128,512]{1,0:T(8,128)(2,1)S(1)}, u32[]{:S(2)}, u32[]{:S(2)}) %collective-permute-start.15) | collective-permute-done | bytes 131104 | tf_op jit(solution)/shard_map/ppermute | solution.py:9
  49.7 3.7 %collective-permute-done.14 = bf16[128,512]{1,0:T(8,128)(2,1)S(1)} collective-permute-done((bf16[128,512]{1,0:T(8,128)(2,1)S(1)}, bf16[128,512]{1,0:T(8,128)(2,1)S(1)}, u32[]{:S(2)}, u32[]{:S(2)}) %collective-permute-start.14) | collective-permute-done | bytes 131104 | tf_op jit(solution)/shard_map/ppermute | solution.py:9
  53.5 1.6 %collective-permute-start.21 = (bf16[128,1792]{1,0:T(8,128)(2,1)S(1)}, bf16[128,1792]{1,0:T(8,128)(2,1)S(1)}, u32[]{:S(2)}, u32[]{:S(2)}) collective-permute-start(bf16[128,1792]{1,0:T(8,128)(2,1)S(1)} %get-tuple-element.27), channel_id=1, source_target_pairs={{0,16},{16,0},{1,17},{17,1},{2,18},{18,2},{3,19},{19,3},{4,20},{20... | collective-permute-start | bytes 1376264 | tf_op jit(solution)/shard_map/ppermute | solution.py:9
  55.6 1.8 %collective-permute-done.5 = bf16[64,1792]{1,0:T(8,128)(2,1)S(1)} collective-permute-done((bf16[64,1792]{1,0:T(8,128)(2,1)S(1)}, bf16[64,1792]{1,0:T(8,128)(2,1)S(1)}, u32[]{:S(2)}, u32[]{:S(2)}) %collective-permute-start.5) | collective-permute-done | bytes 229408 | tf_op jit(solution)/shard_map/ppermute | solution.py:9
  58.9 1.6 %collective-permute-start.19 = (bf16[128,1024]{1,0:T(8,128)(2,1)S(1)}, bf16[128,1024]{1,0:T(8,128)(2,1)S(1)}, u32[]{:S(2)}, u32[]{:S(2)}) collective-permute-start(bf16[128,1024]{1,0:T(8,128)(2,1)S(1)} %get-tuple-element.15), channel_id=1, source_target_pairs={{0,16},{16,0},{1,17},{17,1},{2,18},{18,2},{3,19},{19,3},{4,20},{20... | collective-permute-start | bytes 786440 | tf_op jit(solution)/shard_map/ppermute | solution.py:9
  60.5 1.2 %collective-permute-done.17 = bf16[64,512]{1,0:T(8,128)(2,1)S(1)} collective-permute-done((bf16[64,512]{1,0:T(8,128)(2,1)S(1)}, bf16[64,512]{1,0:T(8,128)(2,1)S(1)}, u32[]{:S(2)}, u32[]{:S(2)}) %collective-permute-start.17) | collective-permute-done | bytes 65568 | tf_op jit(solution)/shard_map/ppermute | solution.py:9
  62.6 4.3 %collective-permute-done.21 = bf16[128,1792]{1,0:T(8,128)(2,1)S(1)} collective-permute-done((bf16[128,1792]{1,0:T(8,128)(2,1)S(1)}, bf16[128,1792]{1,0:T(8,128)(2,1)S(1)}, u32[]{:S(2)}, u32[]{:S(2)}) %collective-permute-start.21) | collective-permute-done | bytes 458784 | tf_op jit(solution)/shard_map/ppermute | solution.py:9
  67.0 5.2 %collective-permute-done.19 = bf16[128,1024]{1,0:T(8,128)(2,1)S(1)} collective-permute-done((bf16[128,1024]{1,0:T(8,128)(2,1)S(1)}, bf16[128,1024]{1,0:T(8,128)(2,1)S(1)}, u32[]{:S(2)}, u32[]{:S(2)}) %collective-permute-start.19) | collective-permute-done | bytes 262176 | tf_op jit(solution)/shard_map/ppermute | solution.py:9
  72.1 4.0 %fusion.8 = bf16[1,1024,1792]{2,1,0:T(8,128)(2,1)} fusion(bf16[512,1792]{1,0:T(8,128)(2,1)S(1)} %constant_dynamic-update-slice_fusion.4, bf16[128,1024]{1,0:T(8,128)(2,1)S(1)} %collective-permute-done.19, bf16[128,1024]{1,0:T(8,128)(2,1)S(1)} %get-tuple-element.14, bf16[128,1024]{1,0:T(8,128)(2,1)S(1)} %collective-permute-done.18, ...), kind=kOutput, calls=%fused_computation.9 | convolution fusion | flops 1885077504 | bytes 6553600 | tf_op jit(solution)/shard_map/dot_general | solution.py:77
  (63 shorter events, 9.5 us)
Async XLA Ops:
  4.3 5.8 %collective-permute-start.6 = (bf16[64,1792]{1,0:T(8,128)(2,1)}, bf16[64,1792]{1,0:T(8,128)(2,1)S(1)}, u32[]{:S(2)}, u32[]{:S(2)}) collective-permute-start(bf16[64,1792]{1,0:T(8,128)(2,1)} %get-tuple-element.10), channel_id=1, source_target_pairs={{0,4},{4,0},{8,12},{12,8},{1,5},{5,1},{9,13},{13,9},{2,6},{6,2},{1... | collective-permute-start | bytes 688136 | tf_op jit(solution)/shard_map/ppermute | solution.py:9
  5.3 19.5 %collective-permute-start.3 = (bf16[64,2048]{1,0:T(8,128)(2,1)S(1)}, bf16[64,2048]{1,0:T(8,128)(2,1)S(1)}, u32[]{:S(2)}, u32[]{:S(2)}) collective-permute-start(bf16[64,2048]{1,0:T(8,128)(2,1)S(1)} %get-tuple-element.4), channel_id=1, source_target_pairs={{0,12},{4,8},{8,4},{12,0},{1,13},{5,9},{9,5},{13,1},{2,14},{6,10},... | collective-permute-start | bytes 786440 | tf_op jit(solution)/shard_map/ppermute | solution.py:9
  7.9 16.5 %collective-permute-start.2 = (bf16[64,2048]{1,0:T(8,128)(2,1)S(1)}, bf16[64,2048]{1,0:T(8,128)(2,1)S(1)}, u32[]{:S(2)}, u32[]{:S(2)}) collective-permute-start(bf16[64,2048]{1,0:T(8,128)(2,1)S(1)} %get-tuple-element.5), channel_id=1, source_target_pairs={{0,8},{4,12},{8,0},{12,4},{1,9},{5,13},{9,1},{13,5},{2,10},{6,14},... | collective-permute-start | bytes 786440 | tf_op jit(solution)/shard_map/ppermute | solution.py:9
  7.9 9.6 %collective-permute-start = (bf16[64,2048]{1,0:T(8,128)(2,1)S(1)}, bf16[64,2048]{1,0:T(8,128)(2,1)S(1)}, u32[]{:S(2)}, u32[]{:S(2)}) collective-permute-start(bf16[64,2048]{1,0:T(8,128)(2,1)S(1)} %get-tuple-element.6), channel_id=1, source_target_pairs={{0,4},{4,0},{8,12},{12,8},{1,5},{5,1},{9,13},{13,9},{2,6},{6,2},{1... | collective-permute-start | bytes 786440 | tf_op jit(solution)/shard_map/ppermute | solution.py:9
  8.1 29.6 %collective-permute-start.12 = (bf16[64,1792]{1,0:T(8,128)(2,1)S(1)}, bf16[64,1792]{1,0:T(8,128)(2,1)S(1)}, u32[]{:S(2)}, u32[]{:S(2)}) collective-permute-start(bf16[64,1792]{1,0:T(8,128)(2,1)S(1)} %get-tuple-element.8), channel_id=1, source_target_pairs={{0,12},{4,8},{8,4},{12,0},{1,13},{5,9},{9,5},{13,1},{2,14},{6,10},... | collective-permute-start | bytes 688136 | tf_op jit(solution)/shard_map/ppermute | solution.py:9
  10.1 7.4 %copy-start.1 = (bf16[512,1792]{1,0:T(8,128)(2,1)S(1)}, bf16[512,1792]{1,0:T(8,128)(2,1)}, u32[]{:S(2)}) copy-start(bf16[512,1792]{1,0:T(8,128)(2,1)} %get-tuple-element.7) | copy-start | bytes 5505028
  15.8 11.8 %collective-permute-start.7 = (bf16[128,512]{1,0:T(8,128)(2,1)S(1)}, bf16[128,512]{1,0:T(8,128)(2,1)S(1)}, u32[]{:S(2)}, u32[]{:S(2)}) collective-permute-start(bf16[128,512]{1,0:T(8,128)(2,1)S(1)} %get-tuple-element.16), channel_id=1, source_target_pairs={{0,1},{1,0},{2,3},{3,2},{4,5},{5,4},{6,7},{7,6},{8,9},{9,8},{10,11... | collective-permute-start | bytes 393224 | tf_op jit(solution)/shard_map/ppermute | solution.py:9
  17.5 10.8 %collective-permute-start.9 = (bf16[128,512]{1,0:T(8,128)(2,1)S(1)}, bf16[128,512]{1,0:T(8,128)(2,1)S(1)}, u32[]{:S(2)}, u32[]{:S(2)}) collective-permute-start(bf16[128,512]{1,0:T(8,128)(2,1)S(1)} %get-tuple-element.17), channel_id=1, source_target_pairs={{0,3},{1,2},{2,1},{3,0},{4,7},{5,6},{6,5},{7,4},{8,11},{9,10},{10,... | collective-permute-start | bytes 393224 | tf_op jit(solution)/shard_map/ppermute | solution.py:9
  20.1 6.3 %slice-start.1 = ((s8[7340032]{0:T(1024)(128)(4,1)}), s8[3145728]{0:T(1024)(128)(4,1)S(1)}, s32[]{:S(2)}) async-start(s8[7340032]{0:T(1024)(128)(4,1)} %bitcast.25), calls=%async_computation.1 | async-start | bytes 6291456
  24.5 8.6 %collective-permute-start.8 = (bf16[128,512]{1,0:T(8,128)(2,1)S(1)}, bf16[128,512]{1,0:T(8,128)(2,1)S(1)}, u32[]{:S(2)}, u32[]{:S(2)}) collective-permute-start(bf16[128,512]{1,0:T(8,128)(2,1)S(1)} %get-tuple-element.18), channel_id=1, source_target_pairs={{0,2},{1,3},{2,0},{3,1},{4,6},{5,7},{6,4},{7,5},{8,10},{9,11},{10,... | collective-permute-start | bytes 393224 | tf_op jit(solution)/shard_map/ppermute | solution.py:9
  24.7 12.9 %collective-permute-start.20 = (bf16[128,1792]{1,0:T(8,128)(2,1)S(1)}, bf16[128,1792]{1,0:T(8,128)(2,1)S(1)}, u32[]{:S(2)}, u32[]{:S(2)}) collective-permute-start(bf16[128,1792]{1,0:T(8,128)(2,1)S(1)} %pad_maximum_fusion.2), channel_id=1, source_target_pairs={{0,16},{16,0},{1,17},{17,1},{2,18},{18,2},{3,19},{19,3},{4,20},{20... | collective-permute-start | bytes 1376264 | tf_op jit(solution)/shard_map/ppermute | solution.py:9
  27.7 10.0 %collective-permute-start.11 = (bf16[64,1792]{1,0:T(8,128)(2,1)S(1)}, bf16[64,1792]{1,0:T(8,128)(2,1)S(1)}, u32[]{:S(2)}, u32[]{:S(2)}) collective-permute-start(bf16[64,1792]{1,0:T(8,128)(2,1)S(1)} %get-tuple-element.9), channel_id=1, source_target_pairs={{0,8},{4,12},{8,0},{12,4},{1,9},{5,13},{9,1},{13,5},{2,10},{6,14},... | collective-permute-start | bytes 688136 | tf_op jit(solution)/shard_map/ppermute | solution.py:9
  28.3 25.2 %collective-permute-start.1 = (bf16[64,1792]{1,0:T(8,128)(2,1)S(1)}, bf16[64,1792]{1,0:T(8,128)(2,1)S(1)}, u32[]{:S(2)}, u32[]{:S(2)}) collective-permute-start(bf16[64,1792]{1,0:T(8,128)(2,1)S(1)} %get-tuple-element.23), channel_id=1, source_target_pairs={{0,4},{4,0},{8,12},{12,8},{1,5},{5,1},{9,13},{13,9},{2,6},{6,2},{1... | collective-permute-start | bytes 688136 | tf_op jit(solution)/shard_map/ppermute | solution.py:9
  33.1 33.8 %collective-permute-start.18 = (bf16[128,1024]{1,0:T(8,128)(2,1)S(1)}, bf16[128,1024]{1,0:T(8,128)(2,1)S(1)}, u32[]{:S(2)}, u32[]{:S(2)}) collective-permute-start(bf16[128,1024]{1,0:T(8,128)(2,1)S(1)} %get-tuple-element.13), channel_id=1, source_target_pairs={{0,16},{16,0},{1,17},{17,1},{2,18},{18,2},{3,19},{19,3},{4,20},{20... | collective-permute-start | bytes 786440 | tf_op jit(solution)/shard_map/ppermute | solution.py:9
  40.3 6.1 %collective-permute-start.13 = (bf16[128,512]{1,0:T(8,128)(2,1)S(1)}, bf16[128,512]{1,0:T(8,128)(2,1)S(1)}, u32[]{:S(2)}, u32[]{:S(2)}) collective-permute-start(bf16[128,512]{1,0:T(8,128)(2,1)S(1)} %get-tuple-element.19), channel_id=1, source_target_pairs={{0,1},{1,0},{2,3},{3,2},{4,5},{5,4},{6,7},{7,6},{8,9},{9,8},{10,11... | collective-permute-start | bytes 393224 | tf_op jit(solution)/shard_map/ppermute | solution.py:9
  42.7 6.9 %collective-permute-start.15 = (bf16[128,512]{1,0:T(8,128)(2,1)S(1)}, bf16[128,512]{1,0:T(8,128)(2,1)S(1)}, u32[]{:S(2)}, u32[]{:S(2)}) collective-permute-start(bf16[128,512]{1,0:T(8,128)(2,1)S(1)} %get-tuple-element.20), channel_id=1, source_target_pairs={{0,3},{1,2},{2,1},{3,0},{4,7},{5,6},{6,5},{7,4},{8,11},{9,10},{10,... | collective-permute-start | bytes 393224 | tf_op jit(solution)/shard_map/ppermute | solution.py:9
  45.2 8.2 %collective-permute-start.14 = (bf16[128,512]{1,0:T(8,128)(2,1)S(1)}, bf16[128,512]{1,0:T(8,128)(2,1)S(1)}, u32[]{:S(2)}, u32[]{:S(2)}) collective-permute-start(bf16[128,512]{1,0:T(8,128)(2,1)S(1)} %get-tuple-element.21), channel_id=1, source_target_pairs={{0,2},{1,3},{2,0},{3,1},{4,6},{5,7},{6,4},{7,5},{8,10},{9,11},{10,... | collective-permute-start | bytes 393224 | tf_op jit(solution)/shard_map/ppermute | solution.py:9
  46.5 8.6 %collective-permute-start.4 = (bf16[64,1792]{1,0:T(8,128)(2,1)S(1)}, bf16[64,1792]{1,0:T(8,128)(2,1)S(1)}, u32[]{:S(2)}, u32[]{:S(2)}) collective-permute-start(bf16[64,1792]{1,0:T(8,128)(2,1)S(1)} %get-tuple-element.24), channel_id=1, source_target_pairs={{0,8},{4,12},{8,0},{12,4},{1,9},{5,13},{9,1},{13,5},{2,10},{6,14},... | collective-permute-start | bytes 688136 | tf_op jit(solution)/shard_map/ppermute | solution.py:9
  49.7 7.8 %collective-permute-start.5 = (bf16[64,1792]{1,0:T(8,128)(2,1)S(1)}, bf16[64,1792]{1,0:T(8,128)(2,1)S(1)}, u32[]{:S(2)}, u32[]{:S(2)}) collective-permute-start(bf16[64,1792]{1,0:T(8,128)(2,1)S(1)} %get-tuple-element.25), channel_id=1, source_target_pairs={{0,12},{4,8},{8,4},{12,0},{1,13},{5,9},{9,5},{13,1},{2,14},{6,10},... | collective-permute-start | bytes 688136 | tf_op jit(solution)/shard_map/ppermute | solution.py:9
  53.4 5.5 %collective-permute-start.10 = (bf16[64,512]{1,0:T(8,128)(2,1)S(1)}, bf16[64,512]{1,0:T(8,128)(2,1)S(1)}, u32[]{:S(2)}, u32[]{:S(2)}) collective-permute-start(bf16[64,512]{1,0:T(8,128)(2,1)S(1)} %get-tuple-element.31), channel_id=1, source_target_pairs={{0,4},{4,0},{8,12},{12,8},{1,5},{5,1},{9,13},{13,9},{2,6},{6,2},{1... | collective-permute-start | bytes 196616 | tf_op jit(solution)/shard_map/ppermute | solution.py:9
  53.5 13.4 %collective-permute-start.21 = (bf16[128,1792]{1,0:T(8,128)(2,1)S(1)}, bf16[128,1792]{1,0:T(8,128)(2,1)S(1)}, u32[]{:S(2)}, u32[]{:S(2)}) collective-permute-start(bf16[128,1792]{1,0:T(8,128)(2,1)S(1)} %get-tuple-element.27), channel_id=1, source_target_pairs={{0,16},{16,0},{1,17},{17,1},{2,18},{18,2},{3,19},{19,3},{4,20},{20... | collective-permute-start | bytes 1376264 | tf_op jit(solution)/shard_map/ppermute | solution.py:9
  55.1 5.4 %collective-permute-start.16 = (bf16[64,512]{1,0:T(8,128)(2,1)S(1)}, bf16[64,512]{1,0:T(8,128)(2,1)S(1)}, u32[]{:S(2)}, u32[]{:S(2)}) collective-permute-start(bf16[64,512]{1,0:T(8,128)(2,1)S(1)} %get-tuple-element.32), channel_id=1, source_target_pairs={{0,8},{4,12},{8,0},{12,4},{1,9},{5,13},{9,1},{13,5},{2,10},{6,14},... | collective-permute-start | bytes 196616 | tf_op jit(solution)/shard_map/ppermute | solution.py:9
  57.4 4.3 %collective-permute-start.17 = (bf16[64,512]{1,0:T(8,128)(2,1)S(1)}, bf16[64,512]{1,0:T(8,128)(2,1)S(1)}, u32[]{:S(2)}, u32[]{:S(2)}) collective-permute-start(bf16[64,512]{1,0:T(8,128)(2,1)S(1)} %get-tuple-element.33), channel_id=1, source_target_pairs={{0,12},{4,8},{8,4},{12,0},{1,13},{5,9},{9,5},{13,1},{2,14},{6,10},... | collective-permute-start | bytes 196616 | tf_op jit(solution)/shard_map/ppermute | solution.py:9
  58.9 13.2 %collective-permute-start.19 = (bf16[128,1024]{1,0:T(8,128)(2,1)S(1)}, bf16[128,1024]{1,0:T(8,128)(2,1)S(1)}, u32[]{:S(2)}, u32[]{:S(2)}) collective-permute-start(bf16[128,1024]{1,0:T(8,128)(2,1)S(1)} %get-tuple-element.15), channel_id=1, source_target_pairs={{0,16},{16,0},{1,17},{17,1},{2,18},{18,2},{3,19},{19,3},{4,20},{20... | collective-permute-start | bytes 786440 | tf_op jit(solution)/shard_map/ppermute | solution.py:9
  (2 other events, 10.4 us)

commit v2 on v1

v2 whole, which is shorter than its diff:
```python
import functools

import jax
import jax.numpy as jnp
from jax import lax
from jax.experimental import pallas as pl
from jax.experimental.pallas import tpu as pltpu
from jax.sharding import PartitionSpec as P

VMEM = pl.BlockSpec(memory_space=pltpu.VMEM)
ANY = pl.BlockSpec(memory_space=pl.ANY)


def call(kernel, outs, ins, specs=None, scratch=(), after=(), cost=0, out_specs=None):
    def late(*refs):
        kernel(*refs[: len(ins)], *refs[len(ins) + len(after) :])

    return pl.pallas_call(
        late,
        out_shape=tuple(jax.ShapeDtypeStruct(s, d) for s, d in outs),
        in_specs=[*(specs or [VMEM] * len(ins)), *[ANY] * len(after)],
        out_specs=tuple(out_specs or [VMEM] * len(outs)),
        scratch_shapes=list(scratch),
        cost_estimate=pl.CostEstimate(flops=1000, bytes_accessed=1000 + cost, transcendentals=0),
        compiler_params=pltpu.CompilerParams(vmem_limit_bytes=24 << 20),
    )(*ins, *after)


def far(value):
    return pltpu.with_memory_space_constraint(value, pltpu.HBM)


def swap(value, axis, offset):
    size = lax.axis_size(axis)
    return lax.ppermute(value, axis, [(i, i ^ offset) for i in range(size)])


def route(routes, placement, experts, cap):
    chosen = routes == jnp.arange(placement.shape[0], dtype=jnp.int32)[None, :]
    target = jnp.sum(jnp.where(chosen, placement[None, :], 0), axis=1)
    landing = target[:, None] == jnp.arange(experts, dtype=jnp.int32)[None, :]
    counted = jnp.cumsum(landing.astype(jnp.int32), axis=0) - 1
    within = jnp.sum(jnp.where(landing, counted, 0), axis=1)
    return target, within


def slot_of(routes, placement, owner, experts, cap):
    tok = routes.shape[1]
    target = jnp.zeros((1, tok), jnp.int32)
    for j in range(experts):
        target = jnp.where(routes == j, placement[j], target)
    key = jnp.bitwise_xor(target, owner)
    landing = jnp.where(key == lax.broadcasted_iota(jnp.int32, (max(8, experts), tok), 0), 1.0, 0.0)
    earlier = lax.broadcasted_iota(jnp.int32, (tok, tok), 0) <= lax.broadcasted_iota(jnp.int32, (tok, tok), 1)
    counted = jnp.dot(
        landing.astype(jnp.bfloat16),
        jnp.where(earlier, 1.0, 0.0).astype(jnp.bfloat16),
        preferred_element_type=jnp.float32,
    )
    within = jnp.sum(landing * counted, axis=0, keepdims=True).astype(jnp.int32) - 1
    position = key * cap + within
    slots = lax.broadcasted_iota(jnp.int32, (experts * cap, tok), 0)
    return jnp.where(position == slots, 1.0, 0.0).astype(jnp.bfloat16)


def weight_copies(tensors, first, weight, held, sem):
    rows = held.shape[1]
    copies = []
    for i in range(tensors // 2):
        block = jnp.bitwise_xor(lax.axis_index("tensor"), first + 2 * i)
        start = pl.multiple_of(block * rows, rows)
        copies.append(pltpu.make_async_copy(weight.at[0, pl.ds(start, rows)], held.at[i], sem.at[i]))
    return copies


def chosen(slot, value):
    return jnp.dot(slot, value, preferred_element_type=jnp.float32).astype(jnp.bfloat16)


def pick(tensors, cap, *refs):
    routes, placement, grad, hid, weight, next_routes, next_grad, next_hid = refs[:8]
    slot_out, next_slot_out, hid_out, odd, near_g, near_h, far_g, near_pack = refs[8:16]
    routes_held, placement_held, grad_held, sem, weight_sem = refs[16:]
    copies = [
        pltpu.make_async_copy(*pair, sem.at[i])
        for i, pair in enumerate(
            ((routes, routes_held), (placement, placement_held), (grad, grad_held), (hid, hid_out))
        )
    ]
    halves = weight_copies(tensors, 1, weight, odd, weight_sem)
    for copy in copies + halves:
        copy.start()
    copies[0].wait()
    copies[1].wait()
    me = lax.axis_index("expert")
    experts = placement.shape[0]
    slot = slot_of(routes_held[...], placement_held, me, experts, cap)
    next_slot = slot_of(next_routes[...], placement_held, jnp.bitwise_xor(me, 1), experts, cap)
    slot_out[...] = slot
    next_slot_out[...] = next_slot
    copies[2].wait()
    far_g[:cap] = chosen(slot[2 * cap : 3 * cap], grad_held[...])
    far_g[cap:] = chosen(next_slot[3 * cap :], next_grad[...])
    near_g[:cap] = chosen(slot[:cap], grad_held[...])
    near_g[cap:] = chosen(next_slot[cap : 2 * cap], next_grad[...])
    copies[3].wait()
    near_h[:cap] = chosen(slot[:cap], hid_out[...])
    near_h[cap:] = chosen(next_slot[cap : 2 * cap], next_hid[...])
    cols, share = near_g.shape[1], near_h.shape[1] // 2
    near_pack[:, :cols] = near_g[...]
    near_pack[:, cols:] = near_h[:, other_share(share)]
    for copy in halves:
        copy.wait()


def pick_far(cap, slot, hid, next_slot, next_hid, out):
    out[:cap] = chosen(slot[2 * cap : 3 * cap], hid[...])
    out[cap:] = chosen(next_slot[3 * cap :], next_hid[...])


def own_share(share):
    return pl.ds(pl.multiple_of(lax.axis_index("dp") * share, share), share)


def other_share(share):
    return pl.ds(pl.multiple_of((1 - lax.axis_index("dp")) * share, share), share)


def cut_other(hid, out):
    out[...] = hid[:, other_share(out.shape[1])]


def hidden_grad(weight, grads, out):
    blocks, rows, _ = weight.shape
    for i in range(blocks):
        part = lax.dot_general(
            grads[...], weight[i], (((1,), (1,)), ((), ())), preferred_element_type=jnp.float32
        )
        out[:, i * rows : (i + 1) * rows] = part.astype(out.dtype)


def output_rows(first, weight, hids, total=None):
    blocks, rows, _ = weight.shape
    for i in range(blocks):
        block = jnp.bitwise_xor(lax.axis_index("tensor"), first + 2 * i)
        start = pl.multiple_of(block * rows, rows)
        term = jnp.dot(hids[:, pl.ds(start, rows)], weight[i], preferred_element_type=jnp.float32)
        total = term if total is None else total + term
    return total


def near_rows(tensors, weight, odd, grads, hids, even, keep, send, out, sem):
    copies = weight_copies(tensors, 0, weight, even, sem)
    for copy in copies:
        copy.start()
    hidden_grad(odd, grads, send)
    total = output_rows(1, odd, hids)
    for copy in copies:
        copy.wait()
    hidden_grad(even, grads, keep)
    out[...] = output_rows(0, even, hids, total).astype(out.dtype)


def cut_rows(total, outs):
    rows = outs[0].shape[0]
    for i, out in enumerate(outs):
        out[...] = total[i * rows : (i + 1) * rows].astype(out.dtype)


def far_grads(odd, even, grads, keep, send):
    hidden_grad(odd, grads, send)
    hidden_grad(even, grads, keep)


def far_outs(odd, even, hids, *outs):
    cut_rows(output_rows(0, even, hids, output_rows(1, odd, hids)), outs)


def fold(keep, got, *outs):
    total = keep[...] + got[...].astype(jnp.float32)
    if outs[0].dtype == jnp.float32:
        cut = outs[0].shape[1]
        outs[0][...] = total[:, :cut]
        outs[1][...] = total[:, cut:].astype(outs[1].dtype)
    else:
        cut_rows(total, outs)


def place(cap, slot, *refs):
    *rows, out, token = refs
    rows = [ref[...] if ref.shape[0] == cap else ref[i % 2 * cap : (i % 2 + 1) * cap] for i, ref in enumerate(rows)]
    out[...] = lax.dot_general(
        slot[...], jnp.concatenate(rows, axis=0), (((0,), (0,)), ((), ())), preferred_element_type=jnp.float32
    ).astype(out.dtype)
    token[...] = jnp.zeros_like(token)


def joined(grads, hids, other_g, other_h):
    g = jnp.concatenate([grads[...], other_g[...]], axis=0)
    h = jnp.concatenate([hids[:, own_share(other_h.shape[1])], other_h[...]], axis=0)
    return g, h


def outer_near(grads, hids, both, out):
    cols = grads.shape[1]
    g, h = joined(grads, hids, both.at[:, :cols], both.at[:, cols:])
    out[...] = lax.dot_general(h, g, (((0,), (0,)), ((), ())), preferred_element_type=jnp.float32)


def outer_far(near, grads, hids, other_g, other_h, out, token, held, sem):
    g, h = joined(grads, hids, other_g, other_h)
    pieces, rows, _ = held.shape
    copies = []
    for i in range(pieces):
        part = slice(i * rows, (i + 1) * rows)
        term = lax.dot_general(h[:, part], g, (((0,), (0,)), ((), ())), preferred_element_type=jnp.float32)
        held[i] = (near[part] + term).astype(held.dtype)
        copies.append(pltpu.make_async_copy(held.at[i], out.at[0, pl.ds(i * rows, rows)], sem.at[i]))
        copies[i].start()
    token[...] = jnp.zeros_like(token)
    for copy in copies:
        copy.wait()


def few(hidden, out_grad, w_down, routes, placement):
    experts = lax.axis_size("expert")
    tensors = lax.axis_size("tensor")
    tok, width = hidden.shape
    cols = out_grad.shape[1]
    cap = 2 * tok // experts
    slots = experts * cap
    share = width // 2
    column = width // tensors
    bf, f32 = jnp.bfloat16, jnp.float32
    rows = 2 * cap
    kept, cut, token = (rows, width // 2), (rows, column), ((8, 128), f32)
    part = ((tensors // 2, column, cols), bf)
    pair = ((cap, column), bf)

    routes = routes.reshape(1, tok)
    next_routes, next_grad, next_hid = (swap(x, "expert", 1) for x in (routes, out_grad, hidden))
    slot, next_slot, held, odd, near_g, near_h, far_g, near_pack = call(
        functools.partial(pick, tensors, cap),
        [
            ((slots, tok), bf),
            ((slots, tok), bf),
            ((tok, width), bf),
            part,
            ((rows, cols), bf),
            ((rows, width), bf),
            ((rows, cols), bf),
            ((rows, cols + share), bf),
        ],
        (*(far(x) for x in (routes, placement, out_grad, hidden, w_down)), next_routes, next_grad, next_hid),
        [*[ANY] * 5, *[VMEM] * 3],
        [
            pltpu.VMEM((1, tok), jnp.int32),
            pltpu.SMEM((experts,), jnp.int32),
            pltpu.VMEM((tok, cols), bf),
            pltpu.SemaphoreType.DMA((4,)),
            pltpu.SemaphoreType.DMA((tensors // 2,)),
        ],
    )
    far_g = swap(far_g, "expert", 2)
    other_near = swap(near_pack, "dp", 1)
    even, near_keep, near_send, near_out = call(
        functools.partial(near_rows, tensors),
        [part, (kept, f32), (kept, bf), ((rows, cols), bf)],
        (far(w_down), odd, near_g, near_h),
        [ANY, *[VMEM] * 3],
        [pltpu.SemaphoreType.DMA((tensors // 2,))],
    )
    near_got = swap(near_send, "tensor", 1)
    (picked,) = call(
        functools.partial(pick_far, cap), [((rows, width), bf)], (slot, held, next_slot, next_hid), after=(near_send,)
    )
    far_h = swap(picked, "expert", 2)
    far_keep, far_send = call(
        far_grads, [(kept, f32), (kept, bf)], (odd, even, far_g), after=(picked,)
    )
    far_got = swap(far_send, "tensor", 1)
    other_g = swap(far_g, "dp", 1)
    last = far_send
    if tensors > 2:
        near_keep, near_send = call(fold, [(cut, f32), (cut, bf)], (near_keep, near_got), after=(last,))
        near_got = swap(near_send, "tensor", 2)
        last = near_send
    (near_total,) = call(outer_near, [((share, cols), f32)], (near_g, near_h, other_near), after=(last,))
    last = near_total
    if tensors > 2:
        far_keep, far_send = call(fold, [(cut, f32), (cut, bf)], (far_keep, far_got), after=(last,))
        far_got = swap(far_send, "tensor", 2)
        last = far_send
    next_out = swap(near_out, "expert", 1)
    far_out = call(far_outs, [((cap, cols), bf)] * 2, (odd, even, far_h), after=(last, next_out))
    (cut_h,) = call(cut_other, [((rows, share), bf)], (far_h,), after=(far_out[0],))
    other_h = swap(cut_h, "dp", 1)
    (near_back,) = call(fold, [(cut, bf)], (near_keep, near_got), after=(cut_h,))
    next_back = swap(near_back, "expert", 1)
    far_back = call(fold, [pair, pair], (far_keep, far_got), after=(next_back, other_g))
    output, last = call(
        functools.partial(place, cap),
        [((tok, cols), bf), token],
        (slot, near_out, next_out, swap(far_out[0], "expert", 2), swap(far_out[1], "expert", 3)),
        after=(far_back[0],),
    )
    pieces = 4
    d_weight, last = call(
        outer_far,
        [((1, share, cols), bf), token],
        (near_total, far_g, far_h, other_g, other_h),
        None,
        [pltpu.VMEM((pieces, share // pieces, cols), bf), pltpu.SemaphoreType.DMA((pieces,))],
        after=(last,),
        out_specs=[ANY, VMEM],
    )
    d_hidden, _ = call(
        functools.partial(place, cap),
        [((tok, column), bf), token],
        (
            slot,
            near_back,
            next_back,
            swap(far_back[0], "expert", 2),
            swap(far_back[1], "expert", 3),
        ),
        after=(last,),
    )
    return output, d_hidden, d_weight


def many(hidden, out_grad, w_down, routes, placement):
    experts = lax.axis_size("expert")
    tok = hidden.shape[0]
    width = hidden.shape[1]
    cols = out_grad.shape[1]
    cap = 2 * tok // experts
    slots = experts * cap
    target, within = route(routes, placement, experts, cap)
    position = target * cap + within
    picker = (jnp.arange(slots, dtype=jnp.int32)[:, None] == position[None, :]).astype(jnp.bfloat16)
    send_hidden = jnp.dot(picker, hidden, preferred_element_type=jnp.float32).astype(jnp.bfloat16)
    send_grad = jnp.dot(picker, out_grad, preferred_element_type=jnp.float32).astype(jnp.bfloat16)

    def exchange(value):
        return lax.all_to_all(
            value.reshape(experts, cap, -1), "expert", split_axis=0, concat_axis=0, tiled=True
        ).reshape(slots, -1)

    slot_hidden, slot_grad = exchange(send_hidden), exchange(send_grad)
    weight = w_down[0]
    out_rows = jnp.dot(slot_hidden, weight, preferred_element_type=jnp.float32).astype(jnp.bfloat16)
    partial_value = lax.dot_general(
        slot_grad, weight, (((1,), (1,)), ((), ())), preferred_element_type=jnp.float32
    )
    hidden_grad = lax.psum_scatter(partial_value, "tensor", scatter_dimension=1, tiled=True).astype(
        jnp.bfloat16
    )

    def place(rows):
        return jnp.einsum("rt,rd->td", picker, rows, preferred_element_type=jnp.float32).astype(jnp.bfloat16)

    output, d_hidden = place(exchange(out_rows)), place(exchange(hidden_grad))
    share = width // lax.axis_size("dp")
    mine = lax.axis_index("dp") * share
    part_h = lax.dynamic_slice_in_dim(
        lax.all_gather(slot_hidden, "dp", axis=0, tiled=True), mine, share, 1
    ).reshape(-1, slots, share)
    part_g = lax.all_gather(slot_grad, "dp", axis=0, tiled=True).reshape(-1, slots, cols)
    terms = jnp.einsum("krf,krd->kfd", part_h, part_g, preferred_element_type=jnp.float32)
    rounded = lax.optimization_barrier(terms.astype(jnp.bfloat16))
    summed = jnp.sum(rounded.astype(jnp.float32), axis=0)
    return output, d_hidden, summed.astype(jnp.bfloat16)[None]


def solution(mesh):
    in_specs = (
        P(("dp", "expert"), None),
        P(("dp", "expert"), "tensor"),
        P("expert", None, "tensor"),
        P(("dp", "expert"), None),
        P(),
    )
    out_specs = (
        P(("dp", "expert"), "tensor"),
        P(("dp", "expert"), "tensor"),
        P("expert", "dp", "tensor"),
    )
    small = mesh.shape["dp"] == 2 and mesh.shape["expert"] == 4 and mesh.shape["tensor"] in (2, 4)
    shards = few if small else many
    return jax.shard_map(shards, mesh=mesh, in_specs=in_specs, out_specs=out_specs, check_vma=False)
```

time: 76.3 us -> 53.4 us (0.70)
  matrix products: 21.5 us -> 0 us
  Pallas kernels: 0 us -> 17.1 us
  waiting for transfers between devices: 27.9 us -> 17.6 us
  starting transfers between devices: 22.8 us -> 17.7 us
  other arithmetic: 1.58 us -> 0 us
  local copies, waits for them, and re-layouts: 1.32 us -> 0 us
    dot_general x9 -> x0, matrix products: 21.5 us -> none  [the longest x2 8.18 us: few(): lax.dot_general(g, weight, (((1,), (1,)), ((), ())), preferred_element_ty...]
    pallas_call x0 -> x14, Pallas kernels: none -> 17.1 us  [call(): pl.pallas_call(late, out_shape=tuple((jax.ShapeDtypeStruct(s, d) for s, d...]
    ppermute x22 -> x18, waiting for transfers between devices: 27.9 us -> 17.6 us  [swap(): return lax.ppermute(value, axis, [(i, i ^ offset) for i in range(size)])]
    ppermute x22 -> x18, starting transfers between devices: 22.8 us -> 17.7 us  [swap(): return lax.ppermute(value, axis, [(i, i ^ offset) for i in range(size)])]
    reduce_sum x2 -> x0, other arithmetic: 1.07 us -> none  [the longest x1 0.9 us: route(): target = jnp.sum(jnp.where(chosen, placement[None, :], 0), axis=1)]
    unnamed x14 -> x0, local copies, waits for them, and re-layouts: 1 us -> none
  transfers between devices with their start and end apart: 22 -> 18, of which waited for: 9 -> 6; matrix products, arithmetic and copies ran while one was open for 22% -> 0% of each run, Pallas kernels for 0% -> 26%
where the time goes in v2:
time: 53.4 us; the launch traced here: 53.2 us
  starting transfers between devices  17.7 us (33%)
  waiting for transfers between devices  17.6 us (33%)
  Pallas kernels  17.1 us (32%)
  between operations  0.78 us (1%)
    ppermute x18, starting transfers between devices, swap(): return lax.ppermute(value, axis, [(i, i ^ offset) for i in range(size)])  17.7 us
    ppermute x18, waiting for transfers between devices, swap(): return lax.ppermute(value, axis, [(i, i ^ offset) for i in range(size)])  17.6 us
    pallas_call x14, Pallas kernels, call(): pl.pallas_call(late, out_shape=tuple((jax.ShapeDtypeStruct(s, d) for s, d...  17.1 us
  transfers between devices with their start and end apart: 18, of which 6 were waited for; matrix products, arithmetic and copies ran while one was open for 0% of the time, Pallas kernels for 26%

profile of v2, /device:TPU:0, one launch (start us, length us, event | category | flops | bytes accessed | tf_op | source)
XLA Modules:
  0.0 53.2 jit_solution(5229473591169173749)
XLA Ops:
  0.6 0.5 collective-permute-start.2
  1.7 1.9 %collective-permute-done.refs_5_ = s32[1,128]{1,0:T(1,128)S(1)} collective-permute-done((s32[1,128]{1,0:T(1,128)}, s32[1,128]{1,0:T(1,128)S(1)}, u32[]{:S(2)}, u32[]{:S(2)}) %collective-permute-start) | collective-permute-done | bytes 544 | tf_op jit(solution)/shard_map/ppermute | solution.py:35
  3.6 2.4 %shard_map.76 = (bf16[256,128]{1,0:T(8,128)(2,1)S(1)}, bf16[256,128]{1,0:T(8,128)(2,1)S(1)}, bf16[128,2048]{1,0:T(8,128)(2,1)S(1)}, bf16[2,512,1792]{2,1,0:T(8,1...) custom-call(s32[1,128]{1,0:T(1,128)} %bitcast.2, ...), custom_call_target="tpu_custom_call" | custom-call | flops 1000 | bytes 1000 | tf_op jit(solution)/shard_map/pallas_call | solution.py:18
  6.0 3.0 %collective-permute-start.7 = (bf16[128,2816]{1,0:T(8,128)(2,1)S(1)}, bf16[128,2816]{1,0:T(8,128)(2,1)S(1)}, u32[]{:S(2)}, u32[]{:S(2)}) collective-permute-start(bf16[128,2816]{1,0:T(8,128)(2,1)S(1)} %get-tuple-element.42), channel_id=1, source_target_pairs={{0,16},{16,0},{1,17},{17,1},{2,18},{18,2},{3,19},{19,3},{4,20},{20... | collective-permute-start | bytes 2162696 | tf_op jit(solution)/shard_map/ppermute | solution.py:35
  9.0 1.5 %collective-permute-start.5 = (bf16[128,1792]{1,0:T(8,128)(2,1)S(1)}, bf16[128,1792]{1,0:T(8,128)(2,1)S(1)}, u32[]{:S(2)}, u32[]{:S(2)}) collective-permute-start(bf16[128,1792]{1,0:T(8,128)(2,1)S(1)} %get-tuple-element.39), channel_id=1, source_target_pairs={{0,8},{4,12},{8,0},{12,4},{1,9},{5,13},{9,1},{13,5},{2,10},{6,14},... | collective-permute-start | bytes 1376264 | tf_op jit(solution)/shard_map/ppermute | solution.py:35
  10.4 5.1 %shard_map.77 = (bf16[2,512,1792]{2,1,0:T(8,128)(2,1)S(1)}, f32[128,1024]{1,0:T(8,128)S(1)}, bf16[128,1024]{1,0:T(8,128)(2,1)S(1)}, bf16[128,1792]{1,0:T(8,128)(2,1)S(1)}) custom-call(bf16[1,2048,1792]{2,1,0:T(8,128)(2,1)} %refs_0_.1, bf16[2,512,1792]{2,1,0:T(8,128)(2,1)S(1)} %get-tuple-element.31.refs_1_.refs_0_, ...), custom_call_target="tpu_custom_call" | custom-call | flops 1000 | bytes 1000 | tf_op jit(solution)/shard_map/pallas_call | solution.py:18
  15.9 0.6 %collective-permute-start.4 = (bf16[128,2048]{1,0:T(8,128)(2,1)S(1)}, bf16[128,2048]{1,0:T(8,128)(2,1)S(1)}, u32[]{:S(2)}, u32[]{:S(2)}) collective-permute-start(bf16[128,2048]{1,0:T(8,128)(2,1)S(1)} %shard_map.78.refs_3_), channel_id=1, source_target_pairs={{0,8},{4,12},{8,0},{12,4},{1,9},{5,13},{9,1},{13,5},{2,10},{6,14},... | collective-permute-start | bytes 1572872 | tf_op jit(solution)/shard_map/ppermute | solution.py:35
  16.5 1.6 %collective-permute-start.8 = (bf16[128,1024]{1,0:T(8,128)(2,1)S(1)}, bf16[128,1024]{1,0:T(8,128)(2,1)S(1)}, u32[]{:S(2)}, u32[]{:S(2)}) collective-permute-start(bf16[128,1024]{1,0:T(8,128)(2,1)S(1)} %get-tuple-element.38.refs_4_), channel_id=1, source_target_pairs={{0,1},{1,0},{2,3},{3,2},{4,5},{5,4},{6,7},{7,6},{8,9},{9,8},{10,11... | collective-permute-start | bytes 786440 | tf_op jit(solution)/shard_map/ppermute | solution.py:35
  18.0 4.3 %collective-permute-done.5.refs_2_.refs_1_ = bf16[128,1792]{1,0:T(8,128)(2,1)S(1)} collective-permute-done((bf16[128,1792]{1,0:T(8,128)(2,1)S(1)}, bf16[128,1792]{1,0:T(8,128)(2,1)S(1)}, u32[]{:S(2)}, u32[]{:S(2)}) %collective-permute-start.5) | collective-permute-done | bytes 458784 | tf_op jit(solution)/shard_map/ppermute | solution.py:35
  22.4 2.5 %shard_map.79 = (f32[128,1024]{1,0:T(8,128)S(1)}, bf16[128,1024]{1,0:T(8,128)(2,1)S(1)}) custom-call(bf16[2,512,1792]{2,1,0:T(8,128)(2,1)S(1)} %get-tuple-element.31.refs_1_.refs_0_, bf16[2,512,1792]{2,1,0:T(8,128)(2,1)S(1)} %get-tuple-element.35.refs_1_, bf16[128,1792]{1,0:T(8,128)(2,1)S(1)} %collective-permute-done.5.refs_2_.refs_1_, ...), custom_call_target="tpu_custom_call" | custom-call | flops 1000 | bytes 1000 | tf_op jit(solution)/shard_map/pallas_call | solution.py:18
  24.8 1.7 %collective-permute-start.6 = (bf16[128,1024]{1,0:T(8,128)(2,1)S(1)}, bf16[128,1024]{1,0:T(8,128)(2,1)S(1)}, u32[]{:S(2)}, u32[]{:S(2)}) collective-permute-start(bf16[128,1024]{1,0:T(8,128)(2,1)S(1)} %get-tuple-element.41.refs_2_), channel_id=1, source_target_pairs={{0,1},{1,0},{2,3},{3,2},{4,5},{5,4},{6,7},{7,6},{8,9},{9,8},{10,11... | collective-permute-start | bytes 786440 | tf_op jit(solution)/shard_map/ppermute | solution.py:35
  26.5 0.5 collective-permute-start.14
  27.0 2.7 %collective-permute-start.12 = (bf16[128,512]{1,0:T(8,128)(2,1)S(1)}, bf16[128,512]{1,0:T(8,128)(2,1)S(1)}, u32[]{:S(2)}, u32[]{:S(2)}) collective-permute-start(bf16[128,512]{1,0:T(8,128)(2,1)S(1)} %get-tuple-element.44.refs_3_), channel_id=1, source_target_pairs={{0,2},{1,3},{2,0},{3,1},{4,6},{5,7},{6,4},{7,5},{8,10},{9,11},{10,... | collective-permute-start | bytes 393224 | tf_op jit(solution)/shard_map/ppermute | solution.py:35
  29.7 1.2 %shard_map.81.refs_2_.refs_0_ = f32[1024,1792]{1,0:T(8,128)S(1)} custom-call(bf16[128,1792]{1,0:T(8,128)(2,1)S(1)} %get-tuple-element.32.refs_2_.refs_0_, bf16[128,2048]{1,0:T(8,128)(2,1)S(1)} %get-tuple-element.33.refs_3_.refs_1_, bf16[128,2816]{1,0:T(8,128)(2,1)S(1)} %collective-permute-done.7.refs_2_, bf16[128,512]{1,0:T(8,128)(2,1)S(1)} %get-tuple-element.44.refs_3_), custom_call_target="tpu_custom_call" | custom-call | flops 1000 | bytes 1000 | tf_op jit(solution)/shard_map/pallas_call | solution.py:18
  30.9 3.2 %collective-permute-done.6.refs_1_ = bf16[128,1024]{1,0:T(8,128)(2,1)S(1)} collective-permute-done((bf16[128,1024]{1,0:T(8,128)(2,1)S(1)}, bf16[128,1024]{1,0:T(8,128)(2,1)S(1)}, u32[]{:S(2)}, u32[]{:S(2)}) %collective-permute-start.6) | collective-permute-done | bytes 262176 | tf_op jit(solution)/shard_map/ppermute | solution.py:35
  34.2 1.1 %shard_map.83 = (bf16[64,1792]{1,0:T(8,128)(2,1)S(1)}, bf16[64,1792]{1,0:T(8,128)(2,1)S(1)}) custom-call(bf16[2,512,1792]{2,1,0:T(8,128)(2,1)S(1)} %get-tuple-element.31.refs_1_.refs_0_, bf16[2,512,1792]{2,1,0:T(8,128)(2,1)S(1)} %get-tuple-element.35.refs_1_, bf16[128,2048]{1,0:T(8,128)(2,1)S(1)} %collective-permute-done.4.refs_2_.refs_0_, ...), custom_call_target="tpu_custom_call" | custom-call | flops 1000 | bytes 1000 | tf_op jit(solution)/shard_map/pallas_call | solution.py:18
  35.5 1.5 %collective-permute-start.10 = (bf16[64,1792]{1,0:T(8,128)(2,1)S(1)}, bf16[64,1792]{1,0:T(8,128)(2,1)S(1)}, u32[]{:S(2)}, u32[]{:S(2)}) collective-permute-start(bf16[64,1792]{1,0:T(8,128)(2,1)S(1)} %get-tuple-element.47), channel_id=1, source_target_pairs={{0,12},{4,8},{8,4},{12,0},{1,13},{5,9},{9,5},{13,1},{2,14},{6,10},... | collective-permute-start | bytes 688136 | tf_op jit(solution)/shard_map/ppermute | solution.py:35
  37.1 0.5 collective-permute-start.9
  37.6 1.5 %collective-permute-start.11 = (bf16[128,512]{1,0:T(8,128)(2,1)S(1)}, bf16[128,512]{1,0:T(8,128)(2,1)S(1)}, u32[]{:S(2)}, u32[]{:S(2)}) collective-permute-start(bf16[128,512]{1,0:T(8,128)(2,1)S(1)} %get-tuple-element.45.refs_3_), channel_id=1, source_target_pairs={{0,2},{1,3},{2,0},{3,1},{4,6},{5,7},{6,4},{7,5},{8,10},{9,11},{10,... | collective-permute-start | bytes 393224 | tf_op jit(solution)/shard_map/ppermute | solution.py:35
  39.1 7.5 %collective-permute-done.11.refs_1_ = bf16[128,512]{1,0:T(8,128)(2,1)S(1)} collective-permute-done((bf16[128,512]{1,0:T(8,128)(2,1)S(1)}, bf16[128,512]{1,0:T(8,128)(2,1)S(1)}, u32[]{:S(2)}, u32[]{:S(2)}) %collective-permute-start.11) | collective-permute-done | bytes 131104 | tf_op jit(solution)/shard_map/ppermute | solution.py:35
  46.6 1.6 %collective-permute-start.15 = (bf16[64,512]{1,0:T(8,128)(2,1)S(1)}, bf16[64,512]{1,0:T(8,128)(2,1)S(1)}, u32[]{:S(2)}, u32[]{:S(2)}) collective-permute-start(bf16[64,512]{1,0:T(8,128)(2,1)S(1)} %get-tuple-element.50.refs_5_), channel_id=1, source_target_pairs={{0,8},{4,12},{8,0},{12,4},{1,9},{5,13},{9,1},{13,5},{2,10},{6,14},... | collective-permute-start | bytes 196616 | tf_op jit(solution)/shard_map/ppermute | solution.py:35
  48.5 1.1 %shard_map.87 = (bf16[128,1792]{1,0:T(8,128)(2,1)}, f32[8,128]{1,0:T(8,128)S(1)}) custom-call(bf16[256,128]{1,0:T(8,128)(2,1)S(1)} %get-tuple-element.30.refs_0_, bf16[128,1792]{1,0:T(8,128)(2,1)S(1)} %get-tuple-element.34.refs_1_, bf16[128,1792]{1,0:T(8,128)(2,1)S(1)} %collective-permute-done.3.refs_4_.refs_2_, ...), custom_call_target="tpu_custom_call" | custom-call | flops 1000 | bytes 1000 | tf_op jit(solution)/shard_map/pallas_call | solution.py:18
  49.6 2.4 %shard_map.88 = (bf16[1,1024,1792]{2,1,0:T(8,128)(2,1)}, f32[8,128]{1,0:T(8,128)S(1)}) custom-call(f32[1024,1792]{1,0:T(8,128)S(1)} %shard_map.81.refs_2_.refs_0_, bf16[128,1792]{1,0:T(8,128)(2,1)S(1)} %collective-permute-done.5.refs_2_.refs_1_, bf16[128,2048]{1,0:T(8,128)(2,1)S(1)} %collective-permute-done.4.refs_2_.refs_0_, ...), custom_call_target="tpu_custom_call" | custom-call | flops 1000 | bytes 1000 | tf_op jit(solution)/shard_map/pallas_call | solution.py:18
  52.4 0.9 %shard_map.89 = (bf16[128,512]{1,0:T(8,128)(2,1)}, f32[8,128]{1,0:T(8,128)}) custom-call(bf16[256,128]{1,0:T(8,128)(2,1)S(1)} %get-tuple-element.30.refs_0_, bf16[128,512]{1,0:T(8,128)(2,1)S(1)} %shard_map.85.refs_1_, bf16[128,512]{1,0:T(8,128)(2,1)S(1)} %collective-permute-done.13.refs_2_, bf16[64,512]{1,0:T(8,128)(2,1)S(1)} %collective-permute-done.15.refs_3_, ...), custom_call_target="tpu_custom_call" | custom-call | flops 1000 | bytes 1000 | tf_op jit(solution)/shard_map/pallas_call | solution.py:18
  (26 shorter events, 1.8 us)
Async XLA Ops:
  0.6 2.9 %collective-permute-start.2 = (bf16[128,2048]{1,0:T(8,128)(2,1)}, bf16[128,2048]{1,0:T(8,128)(2,1)S(1)}, u32[]{:S(2)}, u32[]{:S(2)}) collective-permute-start(bf16[128,2048]{1,0:T(8,128)(2,1)} %refs_3_.1), channel_id=1, source_target_pairs={{0,4},{4,0},{8,12},{12,8},{1,5},{5,1},{9,13},{13,9},{2,6},{6,2},{1... | collective-permute-start | bytes 1572872 | tf_op jit(solution)/shard_map/ppermute | solution.py:35
  1.1 2.4 %collective-permute-start.1 = (bf16[128,1792]{1,0:T(8,128)(2,1)}, bf16[128,1792]{1,0:T(8,128)(2,1)S(1)}, u32[]{:S(2)}, u32[]{:S(2)}) collective-permute-start(bf16[128,1792]{1,0:T(8,128)(2,1)} %refs_2_.1), channel_id=1, source_target_pairs={{0,4},{4,0},{8,12},{12,8},{1,5},{5,1},{9,13},{13,9},{2,6},{6,2},{1... | collective-permute-start | bytes 1376264 | tf_op jit(solution)/shard_map/ppermute | solution.py:35
  1.2 2.3 %collective-permute-start = (s32[1,128]{1,0:T(1,128)}, s32[1,128]{1,0:T(1,128)S(1)}, u32[]{:S(2)}, u32[]{:S(2)}) collective-permute-start(s32[1,128]{1,0:T(1,128)} %bitcast.1), channel_id=1, source_target_pairs={{0,4},{4,0},{8,12},{12,8},{1,5},{5,1},{9,13},{13,9},{2,6},{6,2},{1... | collective-permute-start | bytes 1544 | tf_op jit(solution)/shard_map/ppermute | solution.py:35
  6.0 21.0 %collective-permute-start.7 = (bf16[128,2816]{1,0:T(8,128)(2,1)S(1)}, bf16[128,2816]{1,0:T(8,128)(2,1)S(1)}, u32[]{:S(2)}, u32[]{:S(2)}) collective-permute-start(bf16[128,2816]{1,0:T(8,128)(2,1)S(1)} %get-tuple-element.42), channel_id=1, source_target_pairs={{0,16},{16,0},{1,17},{17,1},{2,18},{18,2},{3,19},{19,3},{4,20},{20... | collective-permute-start | bytes 2162696 | tf_op jit(solution)/shard_map/ppermute | solution.py:35
  9.0 13.4 %collective-permute-start.5 = (bf16[128,1792]{1,0:T(8,128)(2,1)S(1)}, bf16[128,1792]{1,0:T(8,128)(2,1)S(1)}, u32[]{:S(2)}, u32[]{:S(2)}) collective-permute-start(bf16[128,1792]{1,0:T(8,128)(2,1)S(1)} %get-tuple-element.39), channel_id=1, source_target_pairs={{0,8},{4,12},{8,0},{12,4},{1,9},{5,13},{9,1},{13,5},{2,10},{6,14},... | collective-permute-start | bytes 1376264 | tf_op jit(solution)/shard_map/ppermute | solution.py:35
  15.9 18.3 %collective-permute-start.4 = (bf16[128,2048]{1,0:T(8,128)(2,1)S(1)}, bf16[128,2048]{1,0:T(8,128)(2,1)S(1)}, u32[]{:S(2)}, u32[]{:S(2)}) collective-permute-start(bf16[128,2048]{1,0:T(8,128)(2,1)S(1)} %shard_map.78.refs_3_), channel_id=1, source_target_pairs={{0,8},{4,12},{8,0},{12,4},{1,9},{5,13},{9,1},{13,5},{2,10},{6,14},... | collective-permute-start | bytes 1572872 | tf_op jit(solution)/shard_map/ppermute | solution.py:35
  16.5 17.7 %collective-permute-start.3 = (bf16[128,1792]{1,0:T(8,128)(2,1)S(1)}, bf16[128,1792]{1,0:T(8,128)(2,1)S(1)}, u32[]{:S(2)}, u32[]{:S(2)}) collective-permute-start(bf16[128,1792]{1,0:T(8,128)(2,1)S(1)} %get-tuple-element.34.refs_1_), channel_id=1, source_target_pairs={{0,4},{4,0},{8,12},{12,8},{1,5},{5,1},{9,13},{13,9},{2,6},{6,2},{1... | collective-permute-start | bytes 1376264 | tf_op jit(solution)/shard_map/ppermute | solution.py:35
  16.5 10.0 %collective-permute-start.8 = (bf16[128,1024]{1,0:T(8,128)(2,1)S(1)}, bf16[128,1024]{1,0:T(8,128)(2,1)S(1)}, u32[]{:S(2)}, u32[]{:S(2)}) collective-permute-start(bf16[128,1024]{1,0:T(8,128)(2,1)S(1)} %get-tuple-element.38.refs_4_), channel_id=1, source_target_pairs={{0,1},{1,0},{2,3},{3,2},{4,5},{5,4},{6,7},{7,6},{8,9},{9,8},{10,11... | collective-permute-start | bytes 786440 | tf_op jit(solution)/shard_map/ppermute | solution.py:35
  24.8 9.2 %collective-permute-start.6 = (bf16[128,1024]{1,0:T(8,128)(2,1)S(1)}, bf16[128,1024]{1,0:T(8,128)(2,1)S(1)}, u32[]{:S(2)}, u32[]{:S(2)}) collective-permute-start(bf16[128,1024]{1,0:T(8,128)(2,1)S(1)} %get-tuple-element.41.refs_2_), channel_id=1, source_target_pairs={{0,1},{1,0},{2,3},{3,2},{4,5},{5,4},{6,7},{7,6},{8,9},{9,8},{10,11... | collective-permute-start | bytes 786440 | tf_op jit(solution)/shard_map/ppermute | solution.py:35
  26.5 20.1 %collective-permute-start.14 = (bf16[128,1792]{1,0:T(8,128)(2,1)S(1)}, bf16[128,1792]{1,0:T(8,128)(2,1)S(1)}, u32[]{:S(2)}, u32[]{:S(2)}) collective-permute-start(bf16[128,1792]{1,0:T(8,128)(2,1)S(1)} %collective-permute-done.5.refs_2_.refs_1_), channel_id=1, source_target_pairs={{0,16},{16,0},{1,17},{17,1},{2,18},{18,2},{3,19},{19,3},{4,20},{20... | collective-permute-start | bytes 1376264 | tf_op jit(solution)/shard_map/ppermute | solution.py:35
  27.0 8.3 %collective-permute-start.12 = (bf16[128,512]{1,0:T(8,128)(2,1)S(1)}, bf16[128,512]{1,0:T(8,128)(2,1)S(1)}, u32[]{:S(2)}, u32[]{:S(2)}) collective-permute-start(bf16[128,512]{1,0:T(8,128)(2,1)S(1)} %get-tuple-element.44.refs_3_), channel_id=1, source_target_pairs={{0,2},{1,3},{2,0},{3,1},{4,6},{5,7},{6,4},{7,5},{8,10},{9,11},{10,... | collective-permute-start | bytes 393224 | tf_op jit(solution)/shard_map/ppermute | solution.py:35
  35.4 2.2 %collective-permute-start.13 = (bf16[128,512]{1,0:T(8,128)(2,1)S(1)}, bf16[128,512]{1,0:T(8,128)(2,1)S(1)}, u32[]{:S(2)}, u32[]{:S(2)}) collective-permute-start(bf16[128,512]{1,0:T(8,128)(2,1)S(1)} %shard_map.85.refs_1_), channel_id=1, source_target_pairs={{0,4},{4,0},{8,12},{12,8},{1,5},{5,1},{9,13},{13,9},{2,6},{6,2},{1... | collective-permute-start | bytes 393224 | tf_op jit(solution)/shard_map/ppermute | solution.py:35
  35.5 14.1 %collective-permute-start.17 = (bf16[128,1024]{1,0:T(8,128)(2,1)S(1)}, bf16[128,1024]{1,0:T(8,128)(2,1)S(1)}, u32[]{:S(2)}, u32[]{:S(2)}) collective-permute-start(bf16[128,1024]{1,0:T(8,128)(2,1)S(1)} %shard_map.84.refs_2_), channel_id=1, source_target_pairs={{0,16},{16,0},{1,17},{17,1},{2,18},{18,2},{3,19},{19,3},{4,20},{20... | collective-permute-start | bytes 786440 | tf_op jit(solution)/shard_map/ppermute | solution.py:35
  35.5 12.6 %collective-permute-start.10 = (bf16[64,1792]{1,0:T(8,128)(2,1)S(1)}, bf16[64,1792]{1,0:T(8,128)(2,1)S(1)}, u32[]{:S(2)}, u32[]{:S(2)}) collective-permute-start(bf16[64,1792]{1,0:T(8,128)(2,1)S(1)} %get-tuple-element.47), channel_id=1, source_target_pairs={{0,12},{4,8},{8,4},{12,0},{1,13},{5,9},{9,5},{13,1},{2,14},{6,10},... | collective-permute-start | bytes 688136 | tf_op jit(solution)/shard_map/ppermute | solution.py:35
  37.1 11.4 %collective-permute-start.9 = (bf16[64,1792]{1,0:T(8,128)(2,1)S(1)}, bf16[64,1792]{1,0:T(8,128)(2,1)S(1)}, u32[]{:S(2)}, u32[]{:S(2)}) collective-permute-start(bf16[64,1792]{1,0:T(8,128)(2,1)S(1)} %get-tuple-element.46.refs_1_), channel_id=1, source_target_pairs={{0,8},{4,12},{8,0},{12,4},{1,9},{5,13},{9,1},{13,5},{2,10},{6,14},... | collective-permute-start | bytes 688136 | tf_op jit(solution)/shard_map/ppermute | solution.py:35
  37.6 9.0 %collective-permute-start.11 = (bf16[128,512]{1,0:T(8,128)(2,1)S(1)}, bf16[128,512]{1,0:T(8,128)(2,1)S(1)}, u32[]{:S(2)}, u32[]{:S(2)}) collective-permute-start(bf16[128,512]{1,0:T(8,128)(2,1)S(1)} %get-tuple-element.45.refs_3_), channel_id=1, source_target_pairs={{0,2},{1,3},{2,0},{3,1},{4,6},{5,7},{6,4},{7,5},{8,10},{9,11},{10,... | collective-permute-start | bytes 393224 | tf_op jit(solution)/shard_map/ppermute | solution.py:35
  46.6 5.4 %collective-permute-start.15 = (bf16[64,512]{1,0:T(8,128)(2,1)S(1)}, bf16[64,512]{1,0:T(8,128)(2,1)S(1)}, u32[]{:S(2)}, u32[]{:S(2)}) collective-permute-start(bf16[64,512]{1,0:T(8,128)(2,1)S(1)} %get-tuple-element.50.refs_5_), channel_id=1, source_target_pairs={{0,8},{4,12},{8,0},{12,4},{1,9},{5,13},{9,1},{13,5},{2,10},{6,14},... | collective-permute-start | bytes 196616 | tf_op jit(solution)/shard_map/ppermute | solution.py:35
  48.2 4.2 %collective-permute-start.16 = (bf16[64,512]{1,0:T(8,128)(2,1)S(1)}, bf16[64,512]{1,0:T(8,128)(2,1)S(1)}, u32[]{:S(2)}, u32[]{:S(2)}) collective-permute-start(bf16[64,512]{1,0:T(8,128)(2,1)S(1)} %get-tuple-element.52), channel_id=1, source_target_pairs={{0,12},{4,8},{8,4},{12,0},{1,13},{5,9},{9,5},{13,1},{2,14},{6,10},... | collective-permute-start | bytes 196616 | tf_op jit(solution)/shard_map/ppermute | solution.py:35

commit v3 on v2

--- a/solution.py
+++ b/solution.py
@@ -11,7 +11,9 @@
 ANY = pl.BlockSpec(memory_space=pl.ANY)
 
 
-def call(kernel, outs, ins, specs=None, scratch=(), after=(), cost=0, out_specs=None):
+def call(kernel, outs, ins, specs=None, scratch=(), after=(), out_specs=None):
+    name = getattr(kernel, "func", kernel).__name__
+
     def late(*refs):
         kernel(*refs[: len(ins)], *refs[len(ins) + len(after) :])
 
@@ -21,7 +23,8 @@
         in_specs=[*(specs or [VMEM] * len(ins)), *[ANY] * len(after)],
         out_specs=tuple(out_specs or [VMEM] * len(outs)),
         scratch_shapes=list(scratch),
-        cost_estimate=pl.CostEstimate(flops=1000, bytes_accessed=1000 + cost, transcendentals=0),
+        name=name,
+        cost_estimate=pl.CostEstimate(flops=1000, bytes_accessed=1000, transcendentals=0),
         compiler_params=pltpu.CompilerParams(vmem_limit_bytes=24 << 20),
     )(*ins, *after)
 
@@ -48,7 +51,7 @@
     tok = routes.shape[1]
     target = jnp.zeros((1, tok), jnp.int32)
     for j in range(experts):
-        target = jnp.where(routes == j, placement[j], target)
+        target = jnp.where(routes == j, placement[j : j + 1, :tok], target)
     key = jnp.bitwise_xor(target, owner)
     landing = jnp.where(key == lax.broadcasted_iota(jnp.int32, (max(8, experts), tok), 0), 1.0, 0.0)
     earlier = lax.broadcasted_iota(jnp.int32, (tok, tok), 0) <= lax.broadcasted_iota(jnp.int32, (tok, tok), 1)
@@ -63,59 +66,54 @@
     return jnp.where(position == slots, 1.0, 0.0).astype(jnp.bfloat16)
 
 
-def weight_copies(tensors, first, weight, held, sem):
-    rows = held.shape[1]
-    copies = []
-    for i in range(tensors // 2):
-        block = jnp.bitwise_xor(lax.axis_index("tensor"), first + 2 * i)
-        start = pl.multiple_of(block * rows, rows)
-        copies.append(pltpu.make_async_copy(weight.at[0, pl.ds(start, rows)], held.at[i], sem.at[i]))
-    return copies
-
-
 def chosen(slot, value):
     return jnp.dot(slot, value, preferred_element_type=jnp.float32).astype(jnp.bfloat16)
 
 
-def pick(tensors, cap, *refs):
-    routes, placement, grad, hid, weight, next_routes, next_grad, next_hid = refs[:8]
-    slot_out, next_slot_out, hid_out, odd, near_g, near_h, far_g, near_pack = refs[8:16]
-    routes_held, placement_held, grad_held, sem, weight_sem = refs[16:]
+def pick_own(cap, routes, placement, grad, hid, slot_out, hid_out, near_g, near_h, far_g, table, *refs):
+    routes_held, placement_held, grad_held, sem = refs
     copies = [
         pltpu.make_async_copy(*pair, sem.at[i])
         for i, pair in enumerate(
             ((routes, routes_held), (placement, placement_held), (grad, grad_held), (hid, hid_out))
         )
     ]
-    halves = weight_copies(tensors, 1, weight, odd, weight_sem)
-    for copy in copies + halves:
+    for copy in copies:
         copy.start()
     copies[0].wait()
     copies[1].wait()
-    me = lax.axis_index("expert")
     experts = placement.shape[0]
-    slot = slot_of(routes_held[...], placement_held, me, experts, cap)
-    next_slot = slot_of(next_routes[...], placement_held, jnp.bitwise_xor(me, 1), experts, cap)
+    for j in range(experts):
+        table[j : j + 1] = jnp.full((1, table.shape[1]), placement_held[j], jnp.int32)
+    slot = slot_of(routes_held[...], table, lax.axis_index("expert"), experts, cap)
     slot_out[...] = slot
-    next_slot_out[...] = next_slot
     copies[2].wait()
-    far_g[:cap] = chosen(slot[2 * cap : 3 * cap], grad_held[...])
-    far_g[cap:] = chosen(next_slot[3 * cap :], next_grad[...])
-    near_g[:cap] = chosen(slot[:cap], grad_held[...])
-    near_g[cap:] = chosen(next_slot[cap : 2 * cap], next_grad[...])
+    far_g[...] = chosen(slot[2 * cap : 3 * cap], grad_held[...])
+    near_g[...] = chosen(slot[:cap], grad_held[...])
     copies[3].wait()
-    near_h[:cap] = chosen(slot[:cap], hid_out[...])
-    near_h[cap:] = chosen(next_slot[cap : 2 * cap], next_hid[...])
+    near_h[...] = chosen(slot[:cap], hid_out[...])
+
+
+def pick_next(cap, *refs):
+    table, routes, grad, hid, own_near_g, own_near_h, own_far_g = refs[:7]
+    slot_out, near_g, near_h, far_g, near_pack = refs[7:]
+    experts = slot_out.shape[0] // cap
+    slot = slot_of(routes[...], table, jnp.bitwise_xor(lax.axis_index("expert"), 1), experts, cap)
+    slot_out[...] = slot
+    far_g[:cap] = own_far_g[...]
+    far_g[cap:] = chosen(slot[3 * cap :], grad[...])
+    near_g[:cap] = own_near_g[...]
+    near_g[cap:] = chosen(slot[cap : 2 * cap], grad[...])
+    near_h[:cap] = own_near_h[...]
+    near_h[cap:] = chosen(slot[cap : 2 * cap], hid[...])
     cols, share = near_g.shape[1], near_h.shape[1] // 2
     near_pack[:, :cols] = near_g[...]
     near_pack[:, cols:] = near_h[:, other_share(share)]
-    for copy in halves:
-        copy.wait()
-
-
-def pick_far(cap, slot, hid, next_slot, next_hid, out):
-    out[:cap] = chosen(slot[2 * cap : 3 * cap], hid[...])
-    out[cap:] = chosen(next_slot[3 * cap :], next_hid[...])
+
+
+def pick_far(cap, slot, hid, next_slot, next_hid, own, following):
+    own[...] = chosen(slot[2 * cap : 3 * cap], hid[...])
+    following[...] = chosen(next_slot[3 * cap :], next_hid[...])
 
 
 def own_share(share):
@@ -126,39 +124,53 @@
     return pl.ds(pl.multiple_of((1 - lax.axis_index("dp")) * share, share), share)
 
 
-def cut_other(hid, out):
-    out[...] = hid[:, other_share(out.shape[1])]
-
-
-def hidden_grad(weight, grads, out):
-    blocks, rows, _ = weight.shape
-    for i in range(blocks):
-        part = lax.dot_general(
-            grads[...], weight[i], (((1,), (1,)), ((), ())), preferred_element_type=jnp.float32
-        )
-        out[:, i * rows : (i + 1) * rows] = part.astype(out.dtype)
-
-
-def output_rows(first, weight, hids, total=None):
+def cut_other(first, second, out):
+    rows = first.shape[0]
+    out[:rows] = first[:, other_share(out.shape[1])]
+    out[rows:] = second[:, other_share(out.shape[1])]
+
+
+def hidden_grad(weight, i, grads, out):
+    rows = weight.shape[1]
+    part = lax.dot_general(grads[...], weight[i], (((1,), (1,)), ((), ())), preferred_element_type=jnp.float32)
+    out[:, i * rows : (i + 1) * rows] = part.astype(out.dtype)
+
+
+def output_rows(first, weight, hids, total):
     blocks, rows, _ = weight.shape
     for i in range(blocks):
         block = jnp.bitwise_xor(lax.axis_index("tensor"), first + 2 * i)
         start = pl.multiple_of(block * rows, rows)
-        term = jnp.dot(hids[:, pl.ds(start, rows)], weight[i], preferred_element_type=jnp.float32)
+        h = jnp.concatenate([ref[:, pl.ds(start, rows)] for ref in hids], axis=0)
+        term = jnp.dot(h, weight[i], preferred_element_type=jnp.float32)
         total = term if total is None else total + term
     return total
 
 
-def near_rows(tensors, weight, odd, grads, hids, even, keep, send, out, sem):
-    copies = weight_copies(tensors, 0, weight, even, sem)
-    for copy in copies:
-        copy.start()
-    hidden_grad(odd, grads, send)
-    total = output_rows(1, odd, hids)
-    for copy in copies:
+def weight_copies(first, weight, held, sem):
+    rows = held.shape[1]
+    copies = []
+    for i in range(held.shape[0]):
+        block = jnp.bitwise_xor(lax.axis_index("tensor"), first + 2 * i)
+        start = pl.multiple_of(block * rows, rows)
+        copies.append(pltpu.make_async_copy(weight.at[0, pl.ds(start, rows)], held.at[i], sem.at[i]))
+        copies[i].start()
+    return copies
+
+
+def near_odd(weight, grads, odd, send, sem):
+    for i, copy in enumerate(weight_copies(1, weight, odd, sem)):
         copy.wait()
-    hidden_grad(even, grads, keep)
-    out[...] = output_rows(0, even, hids, total).astype(out.dtype)
+        hidden_grad(odd, i, grads, send)
+
+
+def near_even(weight, odd, grads, hids, even, keep, own, following, sem):
+    copies = weight_copies(0, weight, even, sem)
+    total = output_rows(1, odd, [hids], None)
+    for i, copy in enumerate(copies):
+        copy.wait()
+        hidden_grad(even, i, grads, keep)
+    cut_rows(output_rows(0, even, [hids], total), (own, following))
 
 
 def cut_rows(total, outs):
@@ -167,13 +179,14 @@
         out[...] = total[i * rows : (i + 1) * rows].astype(out.dtype)
 
 
-def far_grads(odd, even, grads, keep, send):
-    hidden_grad(odd, grads, send)
-    hidden_grad(even, grads, keep)
-
-
-def far_outs(odd, even, hids, *outs):
-    cut_rows(output_rows(0, even, hids, output_rows(1, odd, hids)), outs)
+def far_grads(weight, grads, out):
+    for i in range(weight.shape[0]):
+        hidden_grad(weight, i, grads, out)
+
+
+def far_outs(odd, even, first, second, *outs):
+    hids = first, second
+    cut_rows(output_rows(0, even, hids, output_rows(1, odd, hids, None)), outs)
 
 
 def fold(keep, got, *outs):
@@ -197,18 +210,19 @@
 
 def joined(grads, hids, other_g, other_h):
     g = jnp.concatenate([grads[...], other_g[...]], axis=0)
-    h = jnp.concatenate([hids[:, own_share(other_h.shape[1])], other_h[...]], axis=0)
+    part = own_share(other_h.shape[1])
+    h = jnp.concatenate([*[ref[:, part] for ref in hids], other_h[...]], axis=0)
     return g, h
 
 
 def outer_near(grads, hids, both, out):
     cols = grads.shape[1]
-    g, h = joined(grads, hids, both.at[:, :cols], both.at[:, cols:])
+    g, h = joined(grads, [hids], both.at[:, :cols], both.at[:, cols:])
     out[...] = lax.dot_general(h, g, (((0,), (0,)), ((), ())), preferred_element_type=jnp.float32)
 
 
-def outer_far(near, grads, hids, other_g, other_h, out, token, held, sem):
-    g, h = joined(grads, hids, other_g, other_h)
+def outer_far(near, grads, first, second, other_g, other_h, out, token, held, sem):
+    g, h = joined(grads, [first, second], other_g, other_h)
     pieces, rows, _ = held.shape
     copies = []
     for i in range(pieces):
@@ -234,70 +248,84 @@
     bf, f32 = jnp.bfloat16, jnp.float32
     rows = 2 * cap
     kept, cut, token = (rows, width // 2), (rows, column), ((8, 128), f32)
-    part = ((tensors // 2, column, cols), bf)
     pair = ((cap, column), bf)
 
     routes = routes.reshape(1, tok)
     next_routes, next_grad, next_hid = (swap(x, "expert", 1) for x in (routes, out_grad, hidden))
-    slot, next_slot, held, odd, near_g, near_h, far_g, near_pack = call(
-        functools.partial(pick, tensors, cap),
+    slot, held, near_g, near_h, far_g, table = call(
+        functools.partial(pick_own, cap),
         [
             ((slots, tok), bf),
+            ((tok, width), bf),
+            ((cap, cols), bf),
+            ((cap, width), bf),
+            ((cap, cols), bf),
+            ((8, 128), jnp.int32),
+        ],
+        tuple(far(x) for x in (routes, placement, out_grad, hidden)),
+        [ANY] * 4,
+        [
+            pltpu.VMEM((1, tok), jnp.int32),
+            pltpu.SMEM((experts,), jnp.int32),
+            pltpu.VMEM((tok, cols), bf),
+            pltpu.SemaphoreType.DMA((4,)),
+        ],
+    )
+    next_slot, near_g, near_h, far_g, near_pack = call(
+        functools.partial(pick_next, cap),
+        [
             ((slots, tok), bf),
-            ((tok, width), bf),
-            part,
             ((rows, cols), bf),
             ((rows, width), bf),
             ((rows, cols), bf),
             ((rows, cols + share), bf),
         ],
-        (*(far(x) for x in (routes, placement, out_grad, hidden, w_down)), next_routes, next_grad, next_hid),
-        [*[ANY] * 5, *[VMEM] * 3],
-        [
-            pltpu.VMEM((1, tok), jnp.int32),
-            pltpu.SMEM((experts,), jnp.int32),
-            pltpu.VMEM((tok, cols), bf),
-            pltpu.SemaphoreType.DMA((4,)),
-            pltpu.SemaphoreType.DMA((tensors // 2,)),
-        ],
+        (table, next_routes, next_grad, next_hid, near_g, near_h, far_g),
     )
     far_g = swap(far_g, "expert", 2)
     other_near = swap(near_pack, "dp", 1)
-    even, near_keep, near_send, near_out = call(
-        functools.partial(near_rows, tensors),
-        [part, (kept, f32), (kept, bf), ((rows, cols), bf)],
+    part = ((tensors // 2, column, cols), bf)
+    sems = [pltpu.SemaphoreType.DMA((tensors // 2,))]
+    odd, near_send = call(
+        near_odd, [part, (kept, bf)], (far(w_down), near_g), [ANY, VMEM], sems
+    )
+    near_got = swap(near_send, "tensor", 1)
+    even, near_keep, near_out, next_out = call(
+        near_even,
+        [part, (kept, f32), ((cap, cols), bf), ((cap, cols), bf)],
         (far(w_down), odd, near_g, near_h),
         [ANY, *[VMEM] * 3],
-        [pltpu.SemaphoreType.DMA((tensors // 2,))],
-    )
-    near_got = swap(near_send, "tensor", 1)
-    (picked,) = call(
-        functools.partial(pick_far, cap), [((rows, width), bf)], (slot, held, next_slot, next_hid), after=(near_send,)
-    )
-    far_h = swap(picked, "expert", 2)
-    far_keep, far_send = call(
-        far_grads, [(kept, f32), (kept, bf)], (odd, even, far_g), after=(picked,)
-    )
+        sems,
+    )
+    next_out = swap(next_out, "expert", 1)
+    picked = call(
+        functools.partial(pick_far, cap),
+        [((cap, width), bf)] * 2,
+        (slot, held, next_slot, next_hid),
+        after=(near_keep,),
+    )
+    far_h = [swap(x, "expert", 2) for x in picked]
+    (far_send,) = call(far_grads, [(kept, bf)], (odd, far_g), after=(picked[0],))
     far_got = swap(far_send, "tensor", 1)
+    (far_keep,) = call(far_grads, [(kept, f32)], (even, far_g), after=(far_send,))
     other_g = swap(far_g, "dp", 1)
-    last = far_send
+    last = far_keep
     if tensors > 2:
         near_keep, near_send = call(fold, [(cut, f32), (cut, bf)], (near_keep, near_got), after=(last,))
         near_got = swap(near_send, "tensor", 2)
         last = near_send
-    (near_total,) = call(outer_near, [((share, cols), f32)], (near_g, near_h, other_near), after=(last,))
-    last = near_total
+    far_out = call(far_outs, [((cap, cols), bf)] * 2, (odd, even, *far_h), after=(last, next_out))
+    last = far_out[0]
     if tensors > 2:
         far_keep, far_send = call(fold, [(cut, f32), (cut, bf)], (far_keep, far_got), after=(last,))
         far_got = swap(far_send, "tensor", 2)
         last = far_send
-    next_out = swap(near_out, "expert", 1)
-    far_out = call(far_outs, [((cap, cols), bf)] * 2, (odd, even, far_h), after=(last, next_out))
-    (cut_h,) = call(cut_other, [((rows, share), bf)], (far_h,), after=(far_out[0],))
+    (near_total,) = call(outer_near, [((share, cols), f32)], (near_g, near_h, other_near), after=(last,))
+    (cut_h,) = call(cut_other, [((rows, share), bf)], far_h, after=(near_total,))
     other_h = swap(cut_h, "dp", 1)
     (near_back,) = call(fold, [(cut, bf)], (near_keep, near_got), after=(cut_h,))
     next_back = swap(near_back, "expert", 1)
-    far_back = call(fold, [pair, pair], (far_keep, far_got), after=(next_back, other_g))
+    far_back = call(fold, [pair, pair], (far_keep, far_got), after=(near_back, other_g))
     output, last = call(
         functools.partial(place, cap),
         [((tok, cols), bf), token],
@@ -308,7 +336,7 @@
     d_weight, last = call(
         outer_far,
         [((1, share, cols), bf), token],
-        (near_total, far_g, far_h, other_g, other_h),
+        (near_total, far_g, *far_h, other_g, other_h),
         None,
         [pltpu.VMEM((pieces, share // pieces, cols), bf), pltpu.SemaphoreType.DMA((pieces,))],
         after=(last,),

time: 53.4 us -> 50.2 us (0.940)
  waiting for transfers between devices: 17.6 us -> 9.08 us
  starting transfers between devices: 17.7 us -> 21.8 us
  Pallas kernels: 17.1 us -> 18.4 us
    ppermute x18 -> x19, waiting for transfers between devices: 17.6 us -> 9.08 us  [swap(): return lax.ppermute(value, axis, [(i, i ^ offset) for i in range(size)])]
    ppermute x18 -> x19, starting transfers between devices: 17.7 us -> 21.8 us  [swap(): return lax.ppermute(value, axis, [(i, i ^ offset) for i in range(size)])]
    pallas_call x14 -> x17, Pallas kernels: 17.1 us -> 18.4 us  [call(): pl.pallas_call(late, out_shape=tuple((jax.ShapeDtypeStruct(s, d) for s, d...]
  transfers between devices with their start and end apart: 18 -> 19, of which waited for: 6 -> 6; matrix products, arithmetic and copies ran while one was open for 0% -> 0% of each run, Pallas kernels for 26% -> 34%
where the time goes in v3:
time: 50.2 us; the launch traced here: 50.1 us
  starting transfers between devices  21.8 us (43%)
  Pallas kernels  18.4 us (37%)
  waiting for transfers between devices  9.08 us (18%)
  between operations  0.78 us (2%)
    ppermute x19, starting transfers between devices, swap(): return lax.ppermute(value, axis, [(i, i ^ offset) for i in range(size)])  21.8 us
    pallas_call x17, Pallas kernels, call(): pl.pallas_call(late, out_shape=tuple((jax.ShapeDtypeStruct(s, d) for s, d...  18.4 us
    ppermute x19, waiting for transfers between devices, swap(): return lax.ppermute(value, axis, [(i, i ^ offset) for i in range(size)])  9.08 us
  transfers between devices with their start and end apart: 19, of which 6 were waited for; matrix products, arithmetic and copies ran while one was open for 0% of the time, Pallas kernels for 34%

profile of v3, /device:TPU:0, one launch (start us, length us, event | category | flops | bytes accessed | tf_op | source)
XLA Modules:
  0.0 50.1 jit_solution(3748322256103669425)
XLA Ops:
  1.7 1.6 %pick_own.1 = (bf16[256,128]{1,0:T(8,128)(2,1)S(1)}, bf16[128,2048]{1,0:T(8,128)(2,1)S(1)}, bf16[64,1792]{1,0:T(8,128)(2,1)S(1)}, bf16[64,2048]{1,0:T(8,128)(2,1...) custom-call(s32[1,128]{1,0:T(1,128)} %bitcast.2, s32[4]{0:T(128)} %refs_1_.1, bf16[128,1792]{1,0:T(8,128)(2,1)} %refs_2_.1, ...), custom_call_target="tpu_custom_call" | custom-call | flops 1000 | bytes 1000 | tf_op jit(solution)/shard_map/pick_own/pallas_call | solution.py:20
  4.1 2.9 %collective-permute-start.7 = (bf16[128,1792]{1,0:T(8,128)(2,1)S(1)}, bf16[128,1792]{1,0:T(8,128)(2,1)S(1)}, u32[]{:S(2)}, u32[]{:S(2)}) collective-permute-start(bf16[128,1792]{1,0:T(8,128)(2,1)S(1)} %get-tuple-element.52), channel_id=1, source_target_pairs={{0,8},{4,12},{8,0},{12,4},{1,9},{5,13},{9,1},{13,5},{2,10},{6,14},... | collective-permute-start | bytes 1376264 | tf_op jit(solution)/shard_map/ppermute | solution.py:38
  7.0 1.5 %collective-permute-start.13 = (bf16[128,2816]{1,0:T(8,128)(2,1)S(1)}, bf16[128,2816]{1,0:T(8,128)(2,1)S(1)}, u32[]{:S(2)}, u32[]{:S(2)}) collective-permute-start(bf16[128,2816]{1,0:T(8,128)(2,1)S(1)} %get-tuple-element.59), channel_id=1, source_target_pairs={{0,16},{16,0},{1,17},{17,1},{2,18},{18,2},{3,19},{19,3},{4,20},{20... | collective-permute-start | bytes 2162696 | tf_op jit(solution)/shard_map/ppermute | solution.py:38
  8.5 3.0 %near_odd.1 = (bf16[2,512,1792]{2,1,0:T(8,128)(2,1)S(1)}, bf16[128,1024]{1,0:T(8,128)(2,1)S(1)}) custom-call(bf16[1,2048,1792]{2,1,0:T(8,128)(2,1)} %refs_0_.3, bf16[128,1792]{1,0:T(8,128)(2,1)S(1)} %get-tuple-element.40.refs_1_.refs_2_.refs_0_), custom_call_target="tpu_custom_call" | custom-call | flops 1000 | bytes 1000 | tf_op jit(solution)/shard_map/near_odd/pallas_call | solution.py:20
  11.5 1.6 %collective-permute-start.6 = (bf16[128,1024]{1,0:T(8,128)(2,1)S(1)}, bf16[128,1024]{1,0:T(8,128)(2,1)S(1)}, u32[]{:S(2)}, u32[]{:S(2)}) collective-permute-start(bf16[128,1024]{1,0:T(8,128)(2,1)S(1)} %get-tuple-element.51), channel_id=1, source_target_pairs={{0,1},{1,0},{2,3},{3,2},{4,5},{5,4},{6,7},{7,6},{8,9},{9,8},{10,11... | collective-permute-start | bytes 786440 | tf_op jit(solution)/shard_map/ppermute | solution.py:38
  13.1 3.6 %near_even.1 = (bf16[2,512,1792]{2,1,0:T(8,128)(2,1)S(1)}, f32[128,1024]{1,0:T(8,128)S(1)}, bf16[64,1792]{1,0:T(8,128)(2,1)S(1)}, bf16[64,1792]{1,0:T(8,128)(2,1)S(1)}) custom-call(bf16[1,2048,1792]{2,1,0:T(8,128)(2,1)} %refs_0_.3, bf16[2,512,1792]{2,1,0:T(8,128)(2,1)S(1)} %get-tuple-element.41.refs_1_.refs_0_, ...), custom_call_target="tpu_custom_call" | custom-call | flops 1000 | bytes 1000 | tf_op jit(solution)/shard_map/near_even/pallas_call | solution.py:20
  17.2 0.6 %collective-permute-start.4 = (bf16[64,2048]{1,0:T(8,128)(2,1)S(1)}, bf16[64,2048]{1,0:T(8,128)(2,1)S(1)}, u32[]{:S(2)}, u32[]{:S(2)}) collective-permute-start(bf16[64,2048]{1,0:T(8,128)(2,1)S(1)} %get-tuple-element.49.refs_2_), channel_id=1, source_target_pairs={{0,8},{4,12},{8,0},{12,4},{1,9},{5,13},{9,1},{13,5},{2,10},{6,14},... | collective-permute-start | bytes 786440 | tf_op jit(solution)/shard_map/ppermute | solution.py:38
  17.8 1.7 %collective-permute-start.5 = (bf16[64,2048]{1,0:T(8,128)(2,1)S(1)}, bf16[64,2048]{1,0:T(8,128)(2,1)S(1)}, u32[]{:S(2)}, u32[]{:S(2)}) collective-permute-start(bf16[64,2048]{1,0:T(8,128)(2,1)S(1)} %get-tuple-element.50), channel_id=1, source_target_pairs={{0,8},{4,12},{8,0},{12,4},{1,9},{5,13},{9,1},{13,5},{2,10},{6,14},... | collective-permute-start | bytes 786440 | tf_op jit(solution)/shard_map/ppermute | solution.py:38
  19.6 1.3 %far_grads.2.refs_2_ = bf16[128,1024]{1,0:T(8,128)(2,1)S(1)} custom-call(bf16[2,512,1792]{2,1,0:T(8,128)(2,1)S(1)} %get-tuple-element.41.refs_1_.refs_0_, bf16[128,1792]{1,0:T(8,128)(2,1)S(1)} %collective-permute-done.7.refs_1_, bf16[64,2048]{1,0:T(8,128)(2,1)S(1)} %get-tuple-element.49.refs_2_), custom_call_target="tpu_custom_call" | custom-call | flops 1000 | bytes 1000 | tf_op jit(solution)/shard_map/far_grads/pallas_call | solution.py:20
  20.9 1.6 %collective-permute-start.10 = (bf16[128,1024]{1,0:T(8,128)(2,1)S(1)}, bf16[128,1024]{1,0:T(8,128)(2,1)S(1)}, u32[]{:S(2)}, u32[]{:S(2)}) collective-permute-start(bf16[128,1024]{1,0:T(8,128)(2,1)S(1)} %far_grads.2.refs_2_), channel_id=1, source_target_pairs={{0,1},{1,0},{2,3},{3,2},{4,5},{5,4},{6,7},{7,6},{8,9},{9,8},{10,11... | collective-permute-start | bytes 786440 | tf_op jit(solution)/shard_map/ppermute | solution.py:38
  22.5 2.3 %collective-permute-start.14 = (bf16[128,1792]{1,0:T(8,128)(2,1)S(1)}, bf16[128,1792]{1,0:T(8,128)(2,1)S(1)}, u32[]{:S(2)}, u32[]{:S(2)}) collective-permute-start(bf16[128,1792]{1,0:T(8,128)(2,1)S(1)} %collective-permute-done.7.refs_1_), channel_id=1, source_target_pairs={{0,16},{16,0},{1,17},{17,1},{2,18},{18,2},{3,19},{19,3},{4,20},{20... | collective-permute-start | bytes 1376264 | tf_op jit(solution)/shard_map/ppermute | solution.py:38
  24.9 1.3 %far_grads.3.refs_2_.refs_0_ = f32[128,1024]{1,0:T(8,128)S(1)} custom-call(bf16[2,512,1792]{2,1,0:T(8,128)(2,1)S(1)} %get-tuple-element.45.refs_0_.refs_1_, bf16[128,1792]{1,0:T(8,128)(2,1)S(1)} %collective-permute-done.7.refs_1_, bf16[128,1024]{1,0:T(8,128)(2,1)S(1)} %far_grads.2.refs_2_), custom_call_target="tpu_custom_call" | custom-call | flops 1000 | bytes 1000 | tf_op jit(solution)/shard_map/far_grads/pallas_call | solution.py:20
  26.3 2.6 %collective-permute-start.12 = (bf16[128,512]{1,0:T(8,128)(2,1)S(1)}, bf16[128,512]{1,0:T(8,128)(2,1)S(1)}, u32[]{:S(2)}, u32[]{:S(2)}) collective-permute-start(bf16[128,512]{1,0:T(8,128)(2,1)S(1)} %get-tuple-element.53.refs_4_), channel_id=1, source_target_pairs={{0,2},{1,3},{2,0},{3,1},{4,6},{5,7},{6,4},{7,5},{8,10},{9,11},{10,... | collective-permute-start | bytes 393224 | tf_op jit(solution)/shard_map/ppermute | solution.py:38
  28.9 2.6 %collective-permute-done.5.refs_3_.refs_1_ = bf16[64,2048]{1,0:T(8,128)(2,1)S(1)} collective-permute-done((bf16[64,2048]{1,0:T(8,128)(2,1)S(1)}, bf16[64,2048]{1,0:T(8,128)(2,1)S(1)}, u32[]{:S(2)}, u32[]{:S(2)}) %collective-permute-start.5) | collective-permute-done | bytes 262176 | tf_op jit(solution)/shard_map/ppermute | solution.py:38
  31.6 1.1 %far_outs.1 = (bf16[64,1792]{1,0:T(8,128)(2,1)S(1)}, bf16[64,1792]{1,0:T(8,128)(2,1)S(1)}) custom-call(bf16[2,512,1792]{2,1,0:T(8,128)(2,1)S(1)} %get-tuple-element.41.refs_1_.refs_0_, bf16[2,512,1792]{2,1,0:T(8,128)(2,1)S(1)} %get-tuple-element.45.refs_0_.refs_1_, bf16[64,2048]{1,0:T(8,128)(2,1)S(1)} %collective-permute-done.4.refs_2_.refs_0_, ...), custom_call_target="tpu_custom_call" | custom-call | flops 1000 | bytes 1000 | tf_op jit(solution)/shard_map/far_outs/pallas_call | solution.py:20
  32.7 0.6 %collective-permute-start.8 = (bf16[64,1792]{1,0:T(8,128)(2,1)S(1)}, bf16[64,1792]{1,0:T(8,128)(2,1)S(1)}, u32[]{:S(2)}, u32[]{:S(2)}) collective-permute-start(bf16[64,1792]{1,0:T(8,128)(2,1)S(1)} %get-tuple-element.54.refs_2_), channel_id=1, source_target_pairs={{0,8},{4,12},{8,0},{12,4},{1,9},{5,13},{9,1},{13,5},{2,10},{6,14},... | collective-permute-start | bytes 688136 | tf_op jit(solution)/shard_map/ppermute | solution.py:38
  33.4 1.2 %outer_near.1.refs_2_.refs_0_ = f32[1024,1792]{1,0:T(8,128)S(1)} custom-call(bf16[128,1792]{1,0:T(8,128)(2,1)S(1)} %get-tuple-element.40.refs_1_.refs_2_.refs_0_, bf16[128,2048]{1,0:T(8,128)(2,1)S(1)} %get-tuple-element.42.refs_3_.refs_1_, bf16[128,2816]{1,0:T(8,128)(2,1)S(1)} %collective-permute-done.13.refs_2_, bf16[128,512]{1,0:T(8,128)(2,1)S(1)} %get-tuple-element.57.refs_3_), custom_call_target="tpu_custom_call" | custom-call | flops 1000 | bytes 1000 | tf_op jit(solution)/shard_map/outer_near/pallas_call | solution.py:20
  34.6 0.6 %collective-permute-start.18 = (bf16[128,1024]{1,0:T(8,128)(2,1)S(1)}, bf16[128,1024]{1,0:T(8,128)(2,1)S(1)}, u32[]{:S(2)}, u32[]{:S(2)}) collective-permute-start(bf16[128,1024]{1,0:T(8,128)(2,1)S(1)} %cut_other.1.refs_2_), channel_id=1, source_target_pairs={{0,16},{16,0},{1,17},{17,1},{2,18},{18,2},{3,19},{19,3},{4,20},{20... | collective-permute-start | bytes 786440 | tf_op jit(solution)/shard_map/ppermute | solution.py:38
  35.2 2.6 %collective-permute-start.11 = (bf16[128,512]{1,0:T(8,128)(2,1)S(1)}, bf16[128,512]{1,0:T(8,128)(2,1)S(1)}, u32[]{:S(2)}, u32[]{:S(2)}) collective-permute-start(bf16[128,512]{1,0:T(8,128)(2,1)S(1)} %get-tuple-element.57.refs_3_), channel_id=1, source_target_pairs={{0,2},{1,3},{2,0},{3,1},{4,6},{5,7},{6,4},{7,5},{8,10},{9,11},{10,... | collective-permute-start | bytes 393224 | tf_op jit(solution)/shard_map/ppermute | solution.py:38
  37.8 5.6 %collective-permute-done.11.refs_1_ = bf16[128,512]{1,0:T(8,128)(2,1)S(1)} collective-permute-done((bf16[128,512]{1,0:T(8,128)(2,1)S(1)}, bf16[128,512]{1,0:T(8,128)(2,1)S(1)}, u32[]{:S(2)}, u32[]{:S(2)}) %collective-permute-start.11) | collective-permute-done | bytes 131104 | tf_op jit(solution)/shard_map/ppermute | solution.py:38
  43.5 1.4 %collective-permute-start.16 = (bf16[64,512]{1,0:T(8,128)(2,1)S(1)}, bf16[64,512]{1,0:T(8,128)(2,1)S(1)}, u32[]{:S(2)}, u32[]{:S(2)}) collective-permute-start(bf16[64,512]{1,0:T(8,128)(2,1)S(1)} %get-tuple-element.60.refs_5_), channel_id=1, source_target_pairs={{0,8},{4,12},{8,0},{12,4},{1,9},{5,13},{9,1},{13,5},{2,10},{6,14},... | collective-permute-start | bytes 196616 | tf_op jit(solution)/shard_map/ppermute | solution.py:38
  45.6 1.1 %place.2 = (bf16[128,1792]{1,0:T(8,128)(2,1)}, f32[8,128]{1,0:T(8,128)S(1)}) custom-call(bf16[256,128]{1,0:T(8,128)(2,1)S(1)} %get-tuple-element.35.refs_0_, bf16[64,1792]{1,0:T(8,128)(2,1)S(1)} %get-tuple-element.43.refs_1_, bf16[64,1792]{1,0:T(8,128)(2,1)S(1)} %collective-permute-done.3.refs_5_.refs_2_, ...), custom_call_target="tpu_custom_call" | custom-call | flops 1000 | bytes 1000 | tf_op jit(solution)/shard_map/place/pallas_call | solution.py:20
  46.7 2.4 %outer_far.1 = (bf16[1,1024,1792]{2,1,0:T(8,128)(2,1)}, f32[8,128]{1,0:T(8,128)S(1)}) custom-call(f32[1024,1792]{1,0:T(8,128)S(1)} %outer_near.1.refs_2_.refs_0_, bf16[128,1792]{1,0:T(8,128)(2,1)S(1)} %collective-permute-done.7.refs_1_, bf16[64,2048]{1,0:T(8,128)(2,1)S(1)} %collective-permute-done.4.refs_2_.refs_0_, ...), custom_call_target="tpu_custom_call" | custom-call | flops 1000 | bytes 1000 | tf_op jit(solution)/shard_map/outer_far/pallas_call | solution.py:20
  49.2 0.9 %place.3 = (bf16[128,512]{1,0:T(8,128)(2,1)}, f32[8,128]{1,0:T(8,128)}) custom-call(bf16[256,128]{1,0:T(8,128)(2,1)S(1)} %get-tuple-element.35.refs_0_, bf16[128,512]{1,0:T(8,128)(2,1)S(1)} %fold.6.refs_2_.refs_1_, bf16[128,512]{1,0:T(8,128)(2,1)S(1)} %collective-permute-done.15.refs_2_, bf16[64,512]{1,0:T(8,128)(2,1)S(1)} %collective-permute-done.16.refs_3_, ...), custom_call_target="tpu_custom_call" | custom-call | flops 1000 | bytes 1000 | tf_op jit(solution)/shard_map/place/pallas_call | solution.py:20
  (31 shorter events, 3.4 us)
Async XLA Ops:
  0.6 2.9 %collective-permute-start.2 = (bf16[128,2048]{1,0:T(8,128)(2,1)}, bf16[128,2048]{1,0:T(8,128)(2,1)S(1)}, u32[]{:S(2)}, u32[]{:S(2)}) collective-permute-start(bf16[128,2048]{1,0:T(8,128)(2,1)} %refs_3_.1), channel_id=1, source_target_pairs={{0,4},{4,0},{8,12},{12,8},{1,5},{5,1},{9,13},{13,9},{2,6},{6,2},{1... | collective-permute-start | bytes 1572872 | tf_op jit(solution)/shard_map/ppermute | solution.py:38
  1.1 2.4 %collective-permute-start.1 = (bf16[128,1792]{1,0:T(8,128)(2,1)}, bf16[128,1792]{1,0:T(8,128)(2,1)S(1)}, u32[]{:S(2)}, u32[]{:S(2)}) collective-permute-start(bf16[128,1792]{1,0:T(8,128)(2,1)} %refs_2_.1), channel_id=1, source_target_pairs={{0,4},{4,0},{8,12},{12,8},{1,5},{5,1},{9,13},{13,9},{2,6},{6,2},{1... | collective-permute-start | bytes 1376264 | tf_op jit(solution)/shard_map/ppermute | solution.py:38
  1.2 2.3 %collective-permute-start = (s32[1,128]{1,0:T(1,128)}, s32[1,128]{1,0:T(1,128)S(1)}, u32[]{:S(2)}, u32[]{:S(2)}) collective-permute-start(s32[1,128]{1,0:T(1,128)} %bitcast.1), channel_id=1, source_target_pairs={{0,4},{4,0},{8,12},{12,8},{1,5},{5,1},{9,13},{13,9},{2,6},{6,2},{1... | collective-permute-start | bytes 1544 | tf_op jit(solution)/shard_map/ppermute | solution.py:38
  4.1 13.7 %collective-permute-start.7 = (bf16[128,1792]{1,0:T(8,128)(2,1)S(1)}, bf16[128,1792]{1,0:T(8,128)(2,1)S(1)}, u32[]{:S(2)}, u32[]{:S(2)}) collective-permute-start(bf16[128,1792]{1,0:T(8,128)(2,1)S(1)} %get-tuple-element.52), channel_id=1, source_target_pairs={{0,8},{4,12},{8,0},{12,4},{1,9},{5,13},{9,1},{13,5},{2,10},{6,14},... | collective-permute-start | bytes 1376264 | tf_op jit(solution)/shard_map/ppermute | solution.py:38
  7.0 26.3 %collective-permute-start.13 = (bf16[128,2816]{1,0:T(8,128)(2,1)S(1)}, bf16[128,2816]{1,0:T(8,128)(2,1)S(1)}, u32[]{:S(2)}, u32[]{:S(2)}) collective-permute-start(bf16[128,2816]{1,0:T(8,128)(2,1)S(1)} %get-tuple-element.59), channel_id=1, source_target_pairs={{0,16},{16,0},{1,17},{17,1},{2,18},{18,2},{3,19},{19,3},{4,20},{20... | collective-permute-start | bytes 2162696 | tf_op jit(solution)/shard_map/ppermute | solution.py:38
  11.5 11.0 %collective-permute-start.6 = (bf16[128,1024]{1,0:T(8,128)(2,1)S(1)}, bf16[128,1024]{1,0:T(8,128)(2,1)S(1)}, u32[]{:S(2)}, u32[]{:S(2)}) collective-permute-start(bf16[128,1024]{1,0:T(8,128)(2,1)S(1)} %get-tuple-element.51), channel_id=1, source_target_pairs={{0,1},{1,0},{2,3},{3,2},{4,5},{5,4},{6,7},{7,6},{8,9},{9,8},{10,11... | collective-permute-start | bytes 786440 | tf_op jit(solution)/shard_map/ppermute | solution.py:38
  16.8 4.1 %collective-permute-start.3 = (bf16[64,1792]{1,0:T(8,128)(2,1)S(1)}, bf16[64,1792]{1,0:T(8,128)(2,1)S(1)}, u32[]{:S(2)}, u32[]{:S(2)}) collective-permute-start(bf16[64,1792]{1,0:T(8,128)(2,1)S(1)} %get-tuple-element.44), channel_id=1, source_target_pairs={{0,4},{4,0},{8,12},{12,8},{1,5},{5,1},{9,13},{13,9},{2,6},{6,2},{1... | collective-permute-start | bytes 688136 | tf_op jit(solution)/shard_map/ppermute | solution.py:38
  17.2 9.2 %collective-permute-start.4 = (bf16[64,2048]{1,0:T(8,128)(2,1)S(1)}, bf16[64,2048]{1,0:T(8,128)(2,1)S(1)}, u32[]{:S(2)}, u32[]{:S(2)}) collective-permute-start(bf16[64,2048]{1,0:T(8,128)(2,1)S(1)} %get-tuple-element.49.refs_2_), channel_id=1, source_target_pairs={{0,8},{4,12},{8,0},{12,4},{1,9},{5,13},{9,1},{13,5},{2,10},{6,14},... | collective-permute-start | bytes 786440 | tf_op jit(solution)/shard_map/ppermute | solution.py:38
  17.8 13.7 %collective-permute-start.5 = (bf16[64,2048]{1,0:T(8,128)(2,1)S(1)}, bf16[64,2048]{1,0:T(8,128)(2,1)S(1)}, u32[]{:S(2)}, u32[]{:S(2)}) collective-permute-start(bf16[64,2048]{1,0:T(8,128)(2,1)S(1)} %get-tuple-element.50), channel_id=1, source_target_pairs={{0,8},{4,12},{8,0},{12,4},{1,9},{5,13},{9,1},{13,5},{2,10},{6,14},... | collective-permute-start | bytes 786440 | tf_op jit(solution)/shard_map/ppermute | solution.py:38
  20.9 12.4 %collective-permute-start.10 = (bf16[128,1024]{1,0:T(8,128)(2,1)S(1)}, bf16[128,1024]{1,0:T(8,128)(2,1)S(1)}, u32[]{:S(2)}, u32[]{:S(2)}) collective-permute-start(bf16[128,1024]{1,0:T(8,128)(2,1)S(1)} %far_grads.2.refs_2_), channel_id=1, source_target_pairs={{0,1},{1,0},{2,3},{3,2},{4,5},{5,4},{6,7},{7,6},{8,9},{9,8},{10,11... | collective-permute-start | bytes 786440 | tf_op jit(solution)/shard_map/ppermute | solution.py:38
  22.5 20.9 %collective-permute-start.14 = (bf16[128,1792]{1,0:T(8,128)(2,1)S(1)}, bf16[128,1792]{1,0:T(8,128)(2,1)S(1)}, u32[]{:S(2)}, u32[]{:S(2)}) collective-permute-start(bf16[128,1792]{1,0:T(8,128)(2,1)S(1)} %collective-permute-done.7.refs_1_), channel_id=1, source_target_pairs={{0,16},{16,0},{1,17},{17,1},{2,18},{18,2},{3,19},{19,3},{4,20},{20... | collective-permute-start | bytes 1376264 | tf_op jit(solution)/shard_map/ppermute | solution.py:38
  26.3 11.4 %collective-permute-start.12 = (bf16[128,512]{1,0:T(8,128)(2,1)S(1)}, bf16[128,512]{1,0:T(8,128)(2,1)S(1)}, u32[]{:S(2)}, u32[]{:S(2)}) collective-permute-start(bf16[128,512]{1,0:T(8,128)(2,1)S(1)} %get-tuple-element.53.refs_4_), channel_id=1, source_target_pairs={{0,2},{1,3},{2,0},{3,1},{4,6},{5,7},{6,4},{7,5},{8,10},{9,11},{10,... | collective-permute-start | bytes 393224 | tf_op jit(solution)/shard_map/ppermute | solution.py:38
  32.7 12.2 %collective-permute-start.8 = (bf16[64,1792]{1,0:T(8,128)(2,1)S(1)}, bf16[64,1792]{1,0:T(8,128)(2,1)S(1)}, u32[]{:S(2)}, u32[]{:S(2)}) collective-permute-start(bf16[64,1792]{1,0:T(8,128)(2,1)S(1)} %get-tuple-element.54.refs_2_), channel_id=1, source_target_pairs={{0,8},{4,12},{8,0},{12,4},{1,9},{5,13},{9,1},{13,5},{2,10},{6,14},... | collective-permute-start | bytes 688136 | tf_op jit(solution)/shard_map/ppermute | solution.py:38
  34.6 12.2 %collective-permute-start.18 = (bf16[128,1024]{1,0:T(8,128)(2,1)S(1)}, bf16[128,1024]{1,0:T(8,128)(2,1)S(1)}, u32[]{:S(2)}, u32[]{:S(2)}) collective-permute-start(bf16[128,1024]{1,0:T(8,128)(2,1)S(1)} %cut_other.1.refs_2_), channel_id=1, source_target_pairs={{0,16},{16,0},{1,17},{17,1},{2,18},{18,2},{3,19},{19,3},{4,20},{20... | collective-permute-start | bytes 786440 | tf_op jit(solution)/shard_map/ppermute | solution.py:38
  35.2 8.3 %collective-permute-start.11 = (bf16[128,512]{1,0:T(8,128)(2,1)S(1)}, bf16[128,512]{1,0:T(8,128)(2,1)S(1)}, u32[]{:S(2)}, u32[]{:S(2)}) collective-permute-start(bf16[128,512]{1,0:T(8,128)(2,1)S(1)} %get-tuple-element.57.refs_3_), channel_id=1, source_target_pairs={{0,2},{1,3},{2,0},{3,1},{4,6},{5,7},{6,4},{7,5},{8,10},{9,11},{10,... | collective-permute-start | bytes 393224 | tf_op jit(solution)/shard_map/ppermute | solution.py:38
  37.8 7.9 %collective-permute-start.9 = (bf16[64,1792]{1,0:T(8,128)(2,1)S(1)}, bf16[64,1792]{1,0:T(8,128)(2,1)S(1)}, u32[]{:S(2)}, u32[]{:S(2)}) collective-permute-start(bf16[64,1792]{1,0:T(8,128)(2,1)S(1)} %get-tuple-element.55), channel_id=1, source_target_pairs={{0,12},{4,8},{8,4},{12,0},{1,13},{5,9},{9,5},{13,1},{2,14},{6,10},... | collective-permute-start | bytes 688136 | tf_op jit(solution)/shard_map/ppermute | solution.py:38
  43.4 5.7 %collective-permute-start.15 = (bf16[128,512]{1,0:T(8,128)(2,1)S(1)}, bf16[128,512]{1,0:T(8,128)(2,1)S(1)}, u32[]{:S(2)}, u32[]{:S(2)}) collective-permute-start(bf16[128,512]{1,0:T(8,128)(2,1)S(1)} %fold.6.refs_2_.refs_1_), channel_id=1, source_target_pairs={{0,4},{4,0},{8,12},{12,8},{1,5},{5,1},{9,13},{13,9},{2,6},{6,2},{1... | collective-permute-start | bytes 393224 | tf_op jit(solution)/shard_map/ppermute | solution.py:38
  43.5 5.7 %collective-permute-start.16 = (bf16[64,512]{1,0:T(8,128)(2,1)S(1)}, bf16[64,512]{1,0:T(8,128)(2,1)S(1)}, u32[]{:S(2)}, u32[]{:S(2)}) collective-permute-start(bf16[64,512]{1,0:T(8,128)(2,1)S(1)} %get-tuple-element.60.refs_5_), channel_id=1, source_target_pairs={{0,8},{4,12},{8,0},{12,4},{1,9},{5,13},{9,1},{13,5},{2,10},{6,14},... | collective-permute-start | bytes 196616 | tf_op jit(solution)/shard_map/ppermute | solution.py:38
  44.9 4.3 %collective-permute-start.17 = (bf16[64,512]{1,0:T(8,128)(2,1)S(1)}, bf16[64,512]{1,0:T(8,128)(2,1)S(1)}, u32[]{:S(2)}, u32[]{:S(2)}) collective-permute-start(bf16[64,512]{1,0:T(8,128)(2,1)S(1)} %get-tuple-element.62), channel_id=1, source_target_pairs={{0,12},{4,8},{8,4},{12,0},{1,13},{5,9},{9,5},{13,1},{2,14},{6,10},... | collective-permute-start | bytes 196616 | tf_op jit(solution)/shard_map/ppermute | solution.py:38

commit v4 on v3

--- a/solution.py
+++ b/solution.py
@@ -70,12 +70,12 @@
     return jnp.dot(slot, value, preferred_element_type=jnp.float32).astype(jnp.bfloat16)
 
 
-def pick_own(cap, routes, placement, grad, hid, slot_out, hid_out, near_g, near_h, far_g, table, *refs):
-    routes_held, placement_held, grad_held, sem = refs
+def pick_own(cap, routes, placement, grad, hid, slot_out, near_g, near_h, far_g, far_h, table, *refs):
+    routes_held, placement_held, grad_held, hid_held, sem = refs
     copies = [
         pltpu.make_async_copy(*pair, sem.at[i])
         for i, pair in enumerate(
-            ((routes, routes_held), (placement, placement_held), (grad, grad_held), (hid, hid_out))
+            ((routes, routes_held), (placement, placement_held), (grad, grad_held), (hid, hid_held))
         )
     ]
     for copy in copies:
@@ -87,35 +87,33 @@
         table[j : j + 1] = jnp.full((1, table.shape[1]), placement_held[j], jnp.int32)
     slot = slot_of(routes_held[...], table, lax.axis_index("expert"), experts, cap)
     slot_out[...] = slot
+    near, far_slots = slot[:cap], slot[2 * cap : 3 * cap]
     copies[2].wait()
-    far_g[...] = chosen(slot[2 * cap : 3 * cap], grad_held[...])
-    near_g[...] = chosen(slot[:cap], grad_held[...])
+    far_g[...] = chosen(far_slots, grad_held[...])
+    near_g[...] = chosen(near, grad_held[...])
     copies[3].wait()
-    near_h[...] = chosen(slot[:cap], hid_out[...])
+    far_h[...] = chosen(far_slots, hid_held[...])
+    near_h[...] = chosen(near, hid_held[...])
 
 
 def pick_next(cap, *refs):
-    table, routes, grad, hid, own_near_g, own_near_h, own_far_g = refs[:7]
-    slot_out, near_g, near_h, far_g, near_pack = refs[7:]
-    experts = slot_out.shape[0] // cap
-    slot = slot_of(routes[...], table, jnp.bitwise_xor(lax.axis_index("expert"), 1), experts, cap)
-    slot_out[...] = slot
-    far_g[:cap] = own_far_g[...]
-    far_g[cap:] = chosen(slot[3 * cap :], grad[...])
-    near_g[:cap] = own_near_g[...]
-    near_g[cap:] = chosen(slot[cap : 2 * cap], grad[...])
-    near_h[:cap] = own_near_h[...]
-    near_h[cap:] = chosen(slot[cap : 2 * cap], hid[...])
+    table, routes, grad, hid, own_near_g, own_near_h, own_far_g, own_far_h = refs[:8]
+    near_g, near_h, far_g, far_h, near_pack = refs[8:]
+    slot = slot_of(routes[...], table, jnp.bitwise_xor(lax.axis_index("expert"), 1), lax.axis_size("expert"), cap)
+    near, far_slots = slot[cap : 2 * cap], slot[3 * cap :]
+    for own, rows, value, out in (
+        (own_far_g, far_slots, grad, far_g),
+        (own_near_g, near, grad, near_g),
+        (own_near_h, near, hid, near_h),
+        (own_far_h, far_slots, hid, far_h),
+    ):
+        out[:cap] = own[...]
+        out[cap:] = chosen(rows, value[...])
     cols, share = near_g.shape[1], near_h.shape[1] // 2
     near_pack[:, :cols] = near_g[...]
     near_pack[:, cols:] = near_h[:, other_share(share)]
 
 
-def pick_far(cap, slot, hid, next_slot, next_hid, own, following):
-    own[...] = chosen(slot[2 * cap : 3 * cap], hid[...])
-    following[...] = chosen(next_slot[3 * cap :], next_hid[...])
-
-
 def own_share(share):
     return pl.ds(pl.multiple_of(lax.axis_index("dp") * share, share), share)
 
@@ -124,10 +122,8 @@
     return pl.ds(pl.multiple_of((1 - lax.axis_index("dp")) * share, share), share)
 
 
-def cut_other(first, second, out):
-    rows = first.shape[0]
-    out[:rows] = first[:, other_share(out.shape[1])]
-    out[rows:] = second[:, other_share(out.shape[1])]
+def cut_other(hid, out):
+    out[...] = hid[:, other_share(out.shape[1])]
 
 
 def hidden_grad(weight, i, grads, out):
@@ -141,8 +137,7 @@
     for i in range(blocks):
         block = jnp.bitwise_xor(lax.axis_index("tensor"), first + 2 * i)
         start = pl.multiple_of(block * rows, rows)
-        h = jnp.concatenate([ref[:, pl.ds(start, rows)] for ref in hids], axis=0)
-        term = jnp.dot(h, weight[i], preferred_element_type=jnp.float32)
+        term = jnp.dot(hids[:, pl.ds(start, rows)], weight[i], preferred_element_type=jnp.float32)
         total = term if total is None else total + term
     return total
 
@@ -166,17 +161,19 @@
 
 def near_even(weight, odd, grads, hids, even, keep, own, following, sem):
     copies = weight_copies(0, weight, even, sem)
-    total = output_rows(1, odd, [hids], None)
+    total = output_rows(1, odd, hids, None)
     for i, copy in enumerate(copies):
         copy.wait()
         hidden_grad(even, i, grads, keep)
-    cut_rows(output_rows(0, even, [hids], total), (own, following))
+    cut_rows(output_rows(0, even, hids, total), (own, following))
 
 
 def cut_rows(total, outs):
-    rows = outs[0].shape[0]
+    rows = min(outs[0].shape[0], total.shape[0])
     for i, out in enumerate(outs):
-        out[...] = total[i * rows : (i + 1) * rows].astype(out.dtype)
+        out[:rows] = total[i * rows : (i + 1) * rows].astype(out.dtype)
+        if out.shape[0] > rows:
+            out[rows:] = jnp.zeros((out.shape[0] - rows, out.shape[1]), out.dtype)
 
 
 def far_grads(weight, grads, out):
@@ -184,8 +181,7 @@
         hidden_grad(weight, i, grads, out)
 
 
-def far_outs(odd, even, first, second, *outs):
-    hids = first, second
+def far_outs(odd, even, hids, *outs):
     cut_rows(output_rows(0, even, hids, output_rows(1, odd, hids, None)), outs)
 
 
@@ -208,26 +204,22 @@
     token[...] = jnp.zeros_like(token)
 
 
-def joined(grads, hids, other_g, other_h):
-    g = jnp.concatenate([grads[...], other_g[...]], axis=0)
-    part = own_share(other_h.shape[1])
-    h = jnp.concatenate([*[ref[:, part] for ref in hids], other_h[...]], axis=0)
-    return g, h
-
-
-def outer_near(grads, hids, both, out):
-    cols = grads.shape[1]
-    g, h = joined(grads, [hids], both.at[:, :cols], both.at[:, cols:])
+def outer_near(grads, hids, both, far_grads, far_hids, out):
+    cols, share = grads.shape[1], out.shape[0]
+    part = own_share(share)
+    g = jnp.concatenate([grads[...], both[:, :cols], far_grads[...]], axis=0)
+    h = jnp.concatenate([hids[:, part], both[:, cols:], far_hids[:, part]], axis=0)
     out[...] = lax.dot_general(h, g, (((0,), (0,)), ((), ())), preferred_element_type=jnp.float32)
 
 
-def outer_far(near, grads, first, second, other_g, other_h, out, token, held, sem):
-    g, h = joined(grads, [first, second], other_g, other_h)
+def outer_far(near, grads, hids, out, token, held, sem):
     pieces, rows, _ = held.shape
     copies = []
     for i in range(pieces):
         part = slice(i * rows, (i + 1) * rows)
-        term = lax.dot_general(h[:, part], g, (((0,), (0,)), ((), ())), preferred_element_type=jnp.float32)
+        term = lax.dot_general(
+            hids[:, part], grads[...], (((0,), (0,)), ((), ())), preferred_element_type=jnp.float32
+        )
         held[i] = (near[part] + term).astype(held.dtype)
         copies.append(pltpu.make_async_copy(held.at[i], out.at[0, pl.ds(i * rows, rows)], sem.at[i]))
         copies[i].start()
@@ -252,36 +244,25 @@
 
     routes = routes.reshape(1, tok)
     next_routes, next_grad, next_hid = (swap(x, "expert", 1) for x in (routes, out_grad, hidden))
-    slot, held, near_g, near_h, far_g, table = call(
+    slot, near_g, near_h, far_g, far_h, table = call(
         functools.partial(pick_own, cap),
-        [
-            ((slots, tok), bf),
-            ((tok, width), bf),
-            ((cap, cols), bf),
-            ((cap, width), bf),
-            ((cap, cols), bf),
-            ((8, 128), jnp.int32),
-        ],
+        [((slots, tok), bf), *[((cap, cols), bf), ((cap, width), bf)] * 2, ((8, 128), jnp.int32)],
         tuple(far(x) for x in (routes, placement, out_grad, hidden)),
         [ANY] * 4,
         [
             pltpu.VMEM((1, tok), jnp.int32),
             pltpu.SMEM((experts,), jnp.int32),
             pltpu.VMEM((tok, cols), bf),
+            pltpu.VMEM((tok, width), bf),
             pltpu.SemaphoreType.DMA((4,)),
         ],
     )
-    next_slot, near_g, near_h, far_g, near_pack = call(
+    near_g, near_h, far_g, far_h, near_pack = call(
         functools.partial(pick_next, cap),
-        [
-            ((slots, tok), bf),
-            ((rows, cols), bf),
-            ((rows, width), bf),
-            ((rows, cols), bf),
-            ((rows, cols + share), bf),
-        ],
-        (table, next_routes, next_grad, next_hid, near_g, near_h, far_g),
-    )
+        [*[((rows, cols), bf), ((rows, width), bf)] * 2, ((rows, cols + share), bf)],
+        (table, next_routes, next_grad, next_hid, near_g, near_h, far_g, far_h),
+    )
+    far_h = swap(far_h, "expert", 2)
     far_g = swap(far_g, "expert", 2)
     other_near = swap(near_pack, "dp", 1)
     part = ((tensors // 2, column, cols), bf)
@@ -298,14 +279,7 @@
         sems,
     )
     next_out = swap(next_out, "expert", 1)
-    picked = call(
-        functools.partial(pick_far, cap),
-        [((cap, width), bf)] * 2,
-        (slot, held, next_slot, next_hid),
-        after=(near_keep,),
-    )
-    far_h = [swap(x, "expert", 2) for x in picked]
-    (far_send,) = call(far_grads, [(kept, bf)], (odd, far_g), after=(picked[0],))
+    (far_send,) = call(far_grads, [(kept, bf)], (odd, far_g), after=(near_keep,))
     far_got = swap(far_send, "tensor", 1)
     (far_keep,) = call(far_grads, [(kept, f32)], (even, far_g), after=(far_send,))
     other_g = swap(far_g, "dp", 1)
@@ -314,16 +288,16 @@
         near_keep, near_send = call(fold, [(cut, f32), (cut, bf)], (near_keep, near_got), after=(last,))
         near_got = swap(near_send, "tensor", 2)
         last = near_send
-    far_out = call(far_outs, [((cap, cols), bf)] * 2, (odd, even, *far_h), after=(last, next_out))
+    far_out = call(far_outs, [((cap, cols), bf)] * 2, (odd, even, far_h), after=(last, next_out))
     last = far_out[0]
     if tensors > 2:
-        far_keep, far_send = call(fold, [(cut, f32), (cut, bf)], (far_keep, far_got), after=(last,))
+        far_keep, far_send = call(fold, [(cut, f32), (cut, bf)], (far_keep, far_got), after=(last, other_near))
         far_got = swap(far_send, "tensor", 2)
         last = far_send
-    (near_total,) = call(outer_near, [((share, cols), f32)], (near_g, near_h, other_near), after=(last,))
-    (cut_h,) = call(cut_other, [((rows, share), bf)], far_h, after=(near_total,))
+    (cut_h,) = call(cut_other, [((rows, share), bf)], (far_h,), after=(last,))
     other_h = swap(cut_h, "dp", 1)
-    (near_back,) = call(fold, [(cut, bf)], (near_keep, near_got), after=(cut_h,))
+    (near_total,) = call(outer_near, [((share, cols), f32)], (near_g, near_h, other_near, far_g, far_h), after=(cut_h,))
+    (near_back,) = call(fold, [((rows + 16, column), bf)], (near_keep, near_got), after=(near_total,))
     next_back = swap(near_back, "expert", 1)
     far_back = call(fold, [pair, pair], (far_keep, far_got), after=(near_back, other_g))
     output, last = call(
@@ -332,11 +306,11 @@
         (slot, near_out, next_out, swap(far_out[0], "expert", 2), swap(far_out[1], "expert", 3)),
         after=(far_back[0],),
     )
-    pieces = 4
+    pieces = 8
     d_weight, last = call(
         outer_far,
         [((1, share, cols), bf), token],
-        (near_total, far_g, *far_h, other_g, other_h),
+        (near_total, other_g, other_h),
         None,
         [pltpu.VMEM((pieces, share // pieces, cols), bf), pltpu.SemaphoreType.DMA((pieces,))],
         after=(last,),

time: 50.2 us -> 47.8 us (0.952)
  waiting for transfers between devices: 9.08 us -> 5.77 us
  Pallas kernels: 18.4 us -> 19.1 us
    ppermute x19 -> x18, waiting for transfers between devices: 9.08 us -> 5.77 us  [swap(): return lax.ppermute(value, axis, [(i, i ^ offset) for i in range(size)])]
    pallas_call x17 -> x16, Pallas kernels: 18.4 us -> 19.1 us  [call(): pl.pallas_call(late, out_shape=tuple((jax.ShapeDtypeStruct(s, d) for s, d...]
    ppermute x19 -> x18, starting transfers between devices: 21.8 us -> 22 us  [swap(): return lax.ppermute(value, axis, [(i, i ^ offset) for i in range(size)])]
  transfers between devices with their start and end apart: 19 -> 18, of which waited for: 6 -> 5; matrix products, arithmetic and copies ran while one was open for 0% -> 0% of each run, Pallas kernels for 34% -> 37%
where the time goes in v4:
time: 47.8 us; the launch traced here: 47.7 us
  starting transfers between devices  22 us (46%)
  Pallas kernels  19.1 us (40%)
  waiting for transfers between devices  5.77 us (12%)
  between operations  0.78 us (2%)
    ppermute x18, starting transfers between devices, swap(): return lax.ppermute(value, axis, [(i, i ^ offset) for i in range(size)])  22 us
    pallas_call x16, Pallas kernels, call(): pl.pallas_call(late, out_shape=tuple((jax.ShapeDtypeStruct(s, d) for s, d...  19.1 us
    ppermute x18, waiting for transfers between devices, swap(): return lax.ppermute(value, axis, [(i, i ^ offset) for i in range(size)])  5.77 us
  transfers between devices with their start and end apart: 18, of which 5 were waited for; matrix products, arithmetic and copies ran while one was open for 0% of the time, Pallas kernels for 37%

profile of v4, /device:TPU:0, one launch (start us, length us, event | category | flops | bytes accessed | tf_op | source)
XLA Modules:
  0.0 47.7 jit_solution(798503592216662046)
XLA Ops:
  1.7 1.6 %pick_own.1 = (bf16[256,128]{1,0:T(8,128)(2,1)S(1)}, bf16[64,1792]{1,0:T(8,128)(2,1)S(1)}, bf16[64,2048]{1,0:T(8,128)(2,1)S(1)}, bf16[64,1792]{1,0:T(8,128)(2,1)...) custom-call(s32[1,128]{1,0:T(1,128)} %bitcast.2, s32[4]{0:T(128)} %refs_1_.1, bf16[128,1792]{1,0:T(8,128)(2,1)} %refs_2_.1, ...), custom_call_target="tpu_custom_call" | custom-call | flops 1000 | bytes 1000 | tf_op jit(solution)/shard_map/pick_own/pallas_call | solution.py:20
  4.2 2.9 %collective-permute-start.6 = (bf16[128,1792]{1,0:T(8,128)(2,1)S(1)}, bf16[128,1792]{1,0:T(8,128)(2,1)S(1)}, u32[]{:S(2)}, u32[]{:S(2)}) collective-permute-start(bf16[128,1792]{1,0:T(8,128)(2,1)S(1)} %get-tuple-element.48), channel_id=1, source_target_pairs={{0,8},{4,12},{8,0},{12,4},{1,9},{5,13},{9,1},{13,5},{2,10},{6,14},... | collective-permute-start | bytes 1376264 | tf_op jit(solution)/shard_map/ppermute | solution.py:38
  7.1 1.5 %collective-permute-start.10 = (bf16[128,2816]{1,0:T(8,128)(2,1)S(1)}, bf16[128,2816]{1,0:T(8,128)(2,1)S(1)}, u32[]{:S(2)}, u32[]{:S(2)}) collective-permute-start(bf16[128,2816]{1,0:T(8,128)(2,1)S(1)} %get-tuple-element.52), channel_id=1, source_target_pairs={{0,16},{16,0},{1,17},{17,1},{2,18},{18,2},{3,19},{19,3},{4,20},{20... | collective-permute-start | bytes 2162696 | tf_op jit(solution)/shard_map/ppermute | solution.py:38
  9.2 3.0 %near_odd.1 = (bf16[2,512,1792]{2,1,0:T(8,128)(2,1)S(1)}, bf16[128,1024]{1,0:T(8,128)(2,1)S(1)}) custom-call(bf16[1,2048,1792]{2,1,0:T(8,128)(2,1)} %refs_0_.3, bf16[128,1792]{1,0:T(8,128)(2,1)S(1)} %get-tuple-element.39.refs_1_.refs_2_.refs_0_), custom_call_target="tpu_custom_call" | custom-call | flops 1000 | bytes 1000 | tf_op jit(solution)/shard_map/near_odd/pallas_call | solution.py:20
  12.1 1.6 %collective-permute-start.5 = (bf16[128,1024]{1,0:T(8,128)(2,1)S(1)}, bf16[128,1024]{1,0:T(8,128)(2,1)S(1)}, u32[]{:S(2)}, u32[]{:S(2)}) collective-permute-start(bf16[128,1024]{1,0:T(8,128)(2,1)S(1)} %get-tuple-element.47), channel_id=1, source_target_pairs={{0,1},{1,0},{2,3},{3,2},{4,5},{5,4},{6,7},{7,6},{8,9},{9,8},{10,11... | collective-permute-start | bytes 786440 | tf_op jit(solution)/shard_map/ppermute | solution.py:38
  13.7 3.6 %near_even.1 = (bf16[2,512,1792]{2,1,0:T(8,128)(2,1)S(1)}, f32[128,1024]{1,0:T(8,128)S(1)}, bf16[64,1792]{1,0:T(8,128)(2,1)S(1)}, bf16[64,1792]{1,0:T(8,128)(2,1)S(1)}) custom-call(bf16[1,2048,1792]{2,1,0:T(8,128)(2,1)} %refs_0_.3, bf16[2,512,1792]{2,1,0:T(8,128)(2,1)S(1)} %get-tuple-element.40.refs_1_.refs_0_, ...), custom_call_target="tpu_custom_call" | custom-call | flops 1000 | bytes 1000 | tf_op jit(solution)/shard_map/near_even/pallas_call | solution.py:20
  17.5 0.9 %collective-permute-done.6.refs_1_.refs_3_ = bf16[128,1792]{1,0:T(8,128)(2,1)S(1)} collective-permute-done((bf16[128,1792]{1,0:T(8,128)(2,1)S(1)}, bf16[128,1792]{1,0:T(8,128)(2,1)S(1)}, u32[]{:S(2)}, u32[]{:S(2)}) %collective-permute-start.6) | collective-permute-done | bytes 458784 | tf_op jit(solution)/shard_map/ppermute | solution.py:38
  18.4 1.3 %far_grads.2.refs_2_ = bf16[128,1024]{1,0:T(8,128)(2,1)S(1)} custom-call(bf16[2,512,1792]{2,1,0:T(8,128)(2,1)S(1)} %get-tuple-element.40.refs_1_.refs_0_, bf16[128,1792]{1,0:T(8,128)(2,1)S(1)} %collective-permute-done.6.refs_1_.refs_3_, f32[128,1024]{1,0:T(8,128)S(1)} %get-tuple-element.46.refs_2_.refs_0_), custom_call_target="tpu_custom_call" | custom-call | flops 1000 | bytes 1000 | tf_op jit(solution)/shard_map/far_grads/pallas_call | solution.py:20
  19.7 2.2 %collective-permute-start.9 = (bf16[128,1024]{1,0:T(8,128)(2,1)S(1)}, bf16[128,1024]{1,0:T(8,128)(2,1)S(1)}, u32[]{:S(2)}, u32[]{:S(2)}) collective-permute-start(bf16[128,1024]{1,0:T(8,128)(2,1)S(1)} %far_grads.2.refs_2_), channel_id=1, source_target_pairs={{0,1},{1,0},{2,3},{3,2},{4,5},{5,4},{6,7},{7,6},{8,9},{9,8},{10,11... | collective-permute-start | bytes 786440 | tf_op jit(solution)/shard_map/ppermute | solution.py:38
  21.9 1.5 %collective-permute-start.13 = (bf16[128,1792]{1,0:T(8,128)(2,1)S(1)}, bf16[128,1792]{1,0:T(8,128)(2,1)S(1)}, u32[]{:S(2)}, u32[]{:S(2)}) collective-permute-start(bf16[128,1792]{1,0:T(8,128)(2,1)S(1)} %collective-permute-done.6.refs_1_.refs_3_), channel_id=1, source_target_pairs={{0,16},{16,0},{1,17},{17,1},{2,18},{18,2},{3,19},{19,3},{4,20},{20... | collective-permute-start | bytes 1376264 | tf_op jit(solution)/shard_map/ppermute | solution.py:38
  23.5 1.3 %far_grads.3.refs_2_.refs_0_ = f32[128,1024]{1,0:T(8,128)S(1)} custom-call(bf16[2,512,1792]{2,1,0:T(8,128)(2,1)S(1)} %get-tuple-element.44.refs_0_.refs_1_, bf16[128,1792]{1,0:T(8,128)(2,1)S(1)} %collective-permute-done.6.refs_1_.refs_3_, bf16[128,1024]{1,0:T(8,128)(2,1)S(1)} %far_grads.2.refs_2_), custom_call_target="tpu_custom_call" | custom-call | flops 1000 | bytes 1000 | tf_op jit(solution)/shard_map/far_grads/pallas_call | solution.py:20
  24.8 2.6 %collective-permute-start.12 = (bf16[128,512]{1,0:T(8,128)(2,1)S(1)}, bf16[128,512]{1,0:T(8,128)(2,1)S(1)}, u32[]{:S(2)}, u32[]{:S(2)}) collective-permute-start(bf16[128,512]{1,0:T(8,128)(2,1)S(1)} %get-tuple-element.49.refs_3_), channel_id=1, source_target_pairs={{0,2},{1,3},{2,0},{3,1},{4,6},{5,7},{6,4},{7,5},{8,10},{9,11},{10,... | collective-permute-start | bytes 393224 | tf_op jit(solution)/shard_map/ppermute | solution.py:38
  27.5 1.7 %collective-permute-done.4.refs_2_.refs_0_.refs_4_ = bf16[128,2048]{1,0:T(8,128)(2,1)S(1)} collective-permute-done((bf16[128,2048]{1,0:T(8,128)(2,1)S(1)}, bf16[128,2048]{1,0:T(8,128)(2,1)S(1)}, u32[]{:S(2)}, u32[]{:S(2)}) %collective-permute-start.4) | collective-permute-done | bytes 524320 | tf_op jit(solution)/shard_map/ppermute | solution.py:38
  29.2 1.1 %far_outs.1 = (bf16[64,1792]{1,0:T(8,128)(2,1)S(1)}, bf16[64,1792]{1,0:T(8,128)(2,1)S(1)}) custom-call(bf16[2,512,1792]{2,1,0:T(8,128)(2,1)S(1)} %get-tuple-element.40.refs_1_.refs_0_, bf16[2,512,1792]{2,1,0:T(8,128)(2,1)S(1)} %get-tuple-element.44.refs_0_.refs_1_, bf16[128,2048]{1,0:T(8,128)(2,1)S(1)} %collective-permute-done.4.refs_2_.refs_0_.refs_4_, ...), custom_call_target="tpu_custom_call" | custom-call | flops 1000 | bytes 1000 | tf_op jit(solution)/shard_map/far_outs/pallas_call | solution.py:20
  30.3 1.8 %collective-permute-start.7 = (bf16[64,1792]{1,0:T(8,128)(2,1)S(1)}, bf16[64,1792]{1,0:T(8,128)(2,1)S(1)}, u32[]{:S(2)}, u32[]{:S(2)}) collective-permute-start(bf16[64,1792]{1,0:T(8,128)(2,1)S(1)} %get-tuple-element.50.refs_2_), channel_id=1, source_target_pairs={{0,8},{4,12},{8,0},{12,4},{1,9},{5,13},{9,1},{13,5},{2,10},{6,14},... | collective-permute-start | bytes 688136 | tf_op jit(solution)/shard_map/ppermute | solution.py:38
  32.2 2.6 %collective-permute-start.11 = (bf16[128,512]{1,0:T(8,128)(2,1)S(1)}, bf16[128,512]{1,0:T(8,128)(2,1)S(1)}, u32[]{:S(2)}, u32[]{:S(2)}) collective-permute-start(bf16[128,512]{1,0:T(8,128)(2,1)S(1)} %get-tuple-element.54.refs_1_), channel_id=1, source_target_pairs={{0,2},{1,3},{2,0},{3,1},{4,6},{5,7},{6,4},{7,5},{8,10},{9,11},{10,... | collective-permute-start | bytes 393224 | tf_op jit(solution)/shard_map/ppermute | solution.py:38
  34.8 1.6 %collective-permute-start.17 = (bf16[128,1024]{1,0:T(8,128)(2,1)S(1)}, bf16[128,1024]{1,0:T(8,128)(2,1)S(1)}, u32[]{:S(2)}, u32[]{:S(2)}) collective-permute-start(bf16[128,1024]{1,0:T(8,128)(2,1)S(1)} %cut_other.1.refs_5_), channel_id=1, source_target_pairs={{0,16},{16,0},{1,17},{17,1},{2,18},{18,2},{3,19},{19,3},{4,20},{20... | collective-permute-start | bytes 786440 | tf_op jit(solution)/shard_map/ppermute | solution.py:38
  36.4 2.1 %outer_near.1.refs_2_.refs_0_ = f32[1024,1792]{1,0:T(8,128)S(1)} custom-call(bf16[128,1792]{1,0:T(8,128)(2,1)S(1)} %get-tuple-element.39.refs_1_.refs_2_.refs_0_, bf16[128,2048]{1,0:T(8,128)(2,1)S(1)} %get-tuple-element.41.refs_3_.refs_1_, bf16[128,2816]{1,0:T(8,128)(2,1)S(1)} %collective-permute-done.10.refs_3_.refs_2_, ...), custom_call_target="tpu_custom_call" | custom-call | flops 1000 | bytes 1000 | tf_op jit(solution)/shard_map/outer_near/pallas_call | solution.py:20
  38.6 1.8 %collective-permute-done.11.refs_1_ = bf16[128,512]{1,0:T(8,128)(2,1)S(1)} collective-permute-done((bf16[128,512]{1,0:T(8,128)(2,1)S(1)}, bf16[128,512]{1,0:T(8,128)(2,1)S(1)}, u32[]{:S(2)}, u32[]{:S(2)}) %collective-permute-start.11) | collective-permute-done | bytes 131104 | tf_op jit(solution)/shard_map/ppermute | solution.py:38
  41.1 1.3 %collective-permute-start.16 = (bf16[64,512]{1,0:T(8,128)(2,1)S(1)}, bf16[64,512]{1,0:T(8,128)(2,1)S(1)}, u32[]{:S(2)}, u32[]{:S(2)}) collective-permute-start(bf16[64,512]{1,0:T(8,128)(2,1)S(1)} %get-tuple-element.58), channel_id=1, source_target_pairs={{0,12},{4,8},{8,4},{12,0},{1,13},{5,9},{9,5},{13,1},{2,14},{6,10},... | collective-permute-start | bytes 196616 | tf_op jit(solution)/shard_map/ppermute | solution.py:38
  42.3 1.1 %collective-permute-done.8.refs_4_ = bf16[64,1792]{1,0:T(8,128)(2,1)S(1)} collective-permute-done((bf16[64,1792]{1,0:T(8,128)(2,1)S(1)}, bf16[64,1792]{1,0:T(8,128)(2,1)S(1)}, u32[]{:S(2)}, u32[]{:S(2)}) %collective-permute-start.8) | collective-permute-done | bytes 229408 | tf_op jit(solution)/shard_map/ppermute | solution.py:38
  43.4 1.1 %place.2 = (bf16[128,1792]{1,0:T(8,128)(2,1)}, f32[8,128]{1,0:T(8,128)S(1)}) custom-call(bf16[256,128]{1,0:T(8,128)(2,1)S(1)} %get-tuple-element.33.refs_0_, bf16[64,1792]{1,0:T(8,128)(2,1)S(1)} %get-tuple-element.42.refs_1_, bf16[64,1792]{1,0:T(8,128)(2,1)S(1)} %collective-permute-done.3.refs_4_.refs_2_, ...), custom_call_target="tpu_custom_call" | custom-call | flops 1000 | bytes 1000 | tf_op jit(solution)/shard_map/place/pallas_call | solution.py:20
  44.5 2.3 %outer_far.1 = (bf16[1,1024,1792]{2,1,0:T(8,128)(2,1)}, f32[8,128]{1,0:T(8,128)S(1)}) custom-call(f32[1024,1792]{1,0:T(8,128)S(1)} %outer_near.1.refs_2_.refs_0_, bf16[128,1792]{1,0:T(8,128)(2,1)S(1)} %collective-permute-done.13.refs_3_.refs_1_, bf16[128,1024]{1,0:T(8,128)(2,1)S(1)} %collective-permute-done.17.refs_2_, f32[8,128]{1,0:T(8,128)S(1)} %get-tuple-element.59.refs_3_), custom_call_target="tpu_custom_call" | custom-call | flops 1000 | bytes 1000 | tf_op jit(solution)/shard_map/outer_far/pallas_call | solution.py:20
  46.8 0.9 %place.3 = (bf16[128,512]{1,0:T(8,128)(2,1)}, f32[8,128]{1,0:T(8,128)}) custom-call(bf16[256,128]{1,0:T(8,128)(2,1)S(1)} %get-tuple-element.33.refs_0_, bf16[144,512]{1,0:T(8,128)(2,1)S(1)} %fold.6.refs_2_.refs_1_, bf16[144,512]{1,0:T(8,128)(2,1)S(1)} %collective-permute-done.14.refs_2_, bf16[64,512]{1,0:T(8,128)(2,1)S(1)} %collective-permute-done.15.refs_3_, ...), custom_call_target="tpu_custom_call" | custom-call | flops 1000 | bytes 1000 | tf_op jit(solution)/shard_map/place/pallas_call | solution.py:20
  (28 shorter events, 3.4 us)
Async XLA Ops:
  0.6 2.9 %collective-permute-start.2 = (bf16[128,2048]{1,0:T(8,128)(2,1)}, bf16[128,2048]{1,0:T(8,128)(2,1)S(1)}, u32[]{:S(2)}, u32[]{:S(2)}) collective-permute-start(bf16[128,2048]{1,0:T(8,128)(2,1)} %refs_3_.1), channel_id=1, source_target_pairs={{0,4},{4,0},{8,12},{12,8},{1,5},{5,1},{9,13},{13,9},{2,6},{6,2},{1... | collective-permute-start | bytes 1572872 | tf_op jit(solution)/shard_map/ppermute | solution.py:38
  1.1 2.4 %collective-permute-start.1 = (bf16[128,1792]{1,0:T(8,128)(2,1)}, bf16[128,1792]{1,0:T(8,128)(2,1)S(1)}, u32[]{:S(2)}, u32[]{:S(2)}) collective-permute-start(bf16[128,1792]{1,0:T(8,128)(2,1)} %refs_2_.1), channel_id=1, source_target_pairs={{0,4},{4,0},{8,12},{12,8},{1,5},{5,1},{9,13},{13,9},{2,6},{6,2},{1... | collective-permute-start | bytes 1376264 | tf_op jit(solution)/shard_map/ppermute | solution.py:38
  1.2 2.3 %collective-permute-start = (s32[1,128]{1,0:T(1,128)}, s32[1,128]{1,0:T(1,128)S(1)}, u32[]{:S(2)}, u32[]{:S(2)}) collective-permute-start(s32[1,128]{1,0:T(1,128)} %bitcast.1), channel_id=1, source_target_pairs={{0,4},{4,0},{8,12},{12,8},{1,5},{5,1},{9,13},{13,9},{2,6},{6,2},{1... | collective-permute-start | bytes 1544 | tf_op jit(solution)/shard_map/ppermute | solution.py:38
  4.2 14.2 %collective-permute-start.6 = (bf16[128,1792]{1,0:T(8,128)(2,1)S(1)}, bf16[128,1792]{1,0:T(8,128)(2,1)S(1)}, u32[]{:S(2)}, u32[]{:S(2)}) collective-permute-start(bf16[128,1792]{1,0:T(8,128)(2,1)S(1)} %get-tuple-element.48), channel_id=1, source_target_pairs={{0,8},{4,12},{8,0},{12,4},{1,9},{5,13},{9,1},{13,5},{2,10},{6,14},... | collective-permute-start | bytes 1376264 | tf_op jit(solution)/shard_map/ppermute | solution.py:38
  7.1 25.0 %collective-permute-start.10 = (bf16[128,2816]{1,0:T(8,128)(2,1)S(1)}, bf16[128,2816]{1,0:T(8,128)(2,1)S(1)}, u32[]{:S(2)}, u32[]{:S(2)}) collective-permute-start(bf16[128,2816]{1,0:T(8,128)(2,1)S(1)} %get-tuple-element.52), channel_id=1, source_target_pairs={{0,16},{16,0},{1,17},{17,1},{2,18},{18,2},{3,19},{19,3},{4,20},{20... | collective-permute-start | bytes 2162696 | tf_op jit(solution)/shard_map/ppermute | solution.py:38
  8.6 20.5 %collective-permute-start.4 = (bf16[128,2048]{1,0:T(8,128)(2,1)S(1)}, bf16[128,2048]{1,0:T(8,128)(2,1)S(1)}, u32[]{:S(2)}, u32[]{:S(2)}) collective-permute-start(bf16[128,2048]{1,0:T(8,128)(2,1)S(1)} %get-tuple-element.45), channel_id=1, source_target_pairs={{0,8},{4,12},{8,0},{12,4},{1,9},{5,13},{9,1},{13,5},{2,10},{6,14},... | collective-permute-start | bytes 1572872 | tf_op jit(solution)/shard_map/ppermute | solution.py:38
  12.1 9.8 %collective-permute-start.5 = (bf16[128,1024]{1,0:T(8,128)(2,1)S(1)}, bf16[128,1024]{1,0:T(8,128)(2,1)S(1)}, u32[]{:S(2)}, u32[]{:S(2)}) collective-permute-start(bf16[128,1024]{1,0:T(8,128)(2,1)S(1)} %get-tuple-element.47), channel_id=1, source_target_pairs={{0,1},{1,0},{2,3},{3,2},{4,5},{5,4},{6,7},{7,6},{8,9},{9,8},{10,11... | collective-permute-start | bytes 786440 | tf_op jit(solution)/shard_map/ppermute | solution.py:38
  17.4 7.4 %collective-permute-start.3 = (bf16[64,1792]{1,0:T(8,128)(2,1)S(1)}, bf16[64,1792]{1,0:T(8,128)(2,1)S(1)}, u32[]{:S(2)}, u32[]{:S(2)}) collective-permute-start(bf16[64,1792]{1,0:T(8,128)(2,1)S(1)} %get-tuple-element.43), channel_id=1, source_target_pairs={{0,4},{4,0},{8,12},{12,8},{1,5},{5,1},{9,13},{13,9},{2,6},{6,2},{1... | collective-permute-start | bytes 688136 | tf_op jit(solution)/shard_map/ppermute | solution.py:38
  19.7 12.4 %collective-permute-start.9 = (bf16[128,1024]{1,0:T(8,128)(2,1)S(1)}, bf16[128,1024]{1,0:T(8,128)(2,1)S(1)}, u32[]{:S(2)}, u32[]{:S(2)}) collective-permute-start(bf16[128,1024]{1,0:T(8,128)(2,1)S(1)} %far_grads.2.refs_2_), channel_id=1, source_target_pairs={{0,1},{1,0},{2,3},{3,2},{4,5},{5,4},{6,7},{7,6},{8,9},{9,8},{10,11... | collective-permute-start | bytes 786440 | tf_op jit(solution)/shard_map/ppermute | solution.py:38
  21.9 18.4 %collective-permute-start.13 = (bf16[128,1792]{1,0:T(8,128)(2,1)S(1)}, bf16[128,1792]{1,0:T(8,128)(2,1)S(1)}, u32[]{:S(2)}, u32[]{:S(2)}) collective-permute-start(bf16[128,1792]{1,0:T(8,128)(2,1)S(1)} %collective-permute-done.6.refs_1_.refs_3_), channel_id=1, source_target_pairs={{0,16},{16,0},{1,17},{17,1},{2,18},{18,2},{3,19},{19,3},{4,20},{20... | collective-permute-start | bytes 1376264 | tf_op jit(solution)/shard_map/ppermute | solution.py:38
  24.8 11.6 %collective-permute-start.12 = (bf16[128,512]{1,0:T(8,128)(2,1)S(1)}, bf16[128,512]{1,0:T(8,128)(2,1)S(1)}, u32[]{:S(2)}, u32[]{:S(2)}) collective-permute-start(bf16[128,512]{1,0:T(8,128)(2,1)S(1)} %get-tuple-element.49.refs_3_), channel_id=1, source_target_pairs={{0,2},{1,3},{2,0},{3,1},{4,6},{5,7},{6,4},{7,5},{8,10},{9,11},{10,... | collective-permute-start | bytes 393224 | tf_op jit(solution)/shard_map/ppermute | solution.py:38
  30.3 10.8 %collective-permute-start.7 = (bf16[64,1792]{1,0:T(8,128)(2,1)S(1)}, bf16[64,1792]{1,0:T(8,128)(2,1)S(1)}, u32[]{:S(2)}, u32[]{:S(2)}) collective-permute-start(bf16[64,1792]{1,0:T(8,128)(2,1)S(1)} %get-tuple-element.50.refs_2_), channel_id=1, source_target_pairs={{0,8},{4,12},{8,0},{12,4},{1,9},{5,13},{9,1},{13,5},{2,10},{6,14},... | collective-permute-start | bytes 688136 | tf_op jit(solution)/shard_map/ppermute | solution.py:38
  32.2 8.2 %collective-permute-start.11 = (bf16[128,512]{1,0:T(8,128)(2,1)S(1)}, bf16[128,512]{1,0:T(8,128)(2,1)S(1)}, u32[]{:S(2)}, u32[]{:S(2)}) collective-permute-start(bf16[128,512]{1,0:T(8,128)(2,1)S(1)} %get-tuple-element.54.refs_1_), channel_id=1, source_target_pairs={{0,2},{1,3},{2,0},{3,1},{4,6},{5,7},{6,4},{7,5},{8,10},{9,11},{10,... | collective-permute-start | bytes 393224 | tf_op jit(solution)/shard_map/ppermute | solution.py:38
  34.8 9.7 %collective-permute-start.17 = (bf16[128,1024]{1,0:T(8,128)(2,1)S(1)}, bf16[128,1024]{1,0:T(8,128)(2,1)S(1)}, u32[]{:S(2)}, u32[]{:S(2)}) collective-permute-start(bf16[128,1024]{1,0:T(8,128)(2,1)S(1)} %cut_other.1.refs_5_), channel_id=1, source_target_pairs={{0,16},{16,0},{1,17},{17,1},{2,18},{18,2},{3,19},{19,3},{4,20},{20... | collective-permute-start | bytes 786440 | tf_op jit(solution)/shard_map/ppermute | solution.py:38
  36.4 7.0 %collective-permute-start.8 = (bf16[64,1792]{1,0:T(8,128)(2,1)S(1)}, bf16[64,1792]{1,0:T(8,128)(2,1)S(1)}, u32[]{:S(2)}, u32[]{:S(2)}) collective-permute-start(bf16[64,1792]{1,0:T(8,128)(2,1)S(1)} %get-tuple-element.51), channel_id=1, source_target_pairs={{0,12},{4,8},{8,4},{12,0},{1,13},{5,9},{9,5},{13,1},{2,14},{6,10},... | collective-permute-start | bytes 688136 | tf_op jit(solution)/shard_map/ppermute | solution.py:38
  40.4 6.4 %collective-permute-start.14 = (bf16[144,512]{1,0:T(8,128)(2,1)S(1)}, bf16[144,512]{1,0:T(8,128)(2,1)S(1)}, u32[]{:S(2)}, u32[]{:S(2)}) collective-permute-start(bf16[144,512]{1,0:T(8,128)(2,1)S(1)} %fold.6.refs_2_.refs_1_), channel_id=1, source_target_pairs={{0,4},{4,0},{8,12},{12,8},{1,5},{5,1},{9,13},{13,9},{2,6},{6,2},{1... | collective-permute-start | bytes 442376 | tf_op jit(solution)/shard_map/ppermute | solution.py:38
  40.4 6.4 %collective-permute-start.15 = (bf16[64,512]{1,0:T(8,128)(2,1)S(1)}, bf16[64,512]{1,0:T(8,128)(2,1)S(1)}, u32[]{:S(2)}, u32[]{:S(2)}) collective-permute-start(bf16[64,512]{1,0:T(8,128)(2,1)S(1)} %get-tuple-element.56.refs_5_), channel_id=1, source_target_pairs={{0,8},{4,12},{8,0},{12,4},{1,9},{5,13},{9,1},{13,5},{2,10},{6,14},... | collective-permute-start | bytes 196616 | tf_op jit(solution)/shard_map/ppermute | solution.py:38
  41.1 5.7 %collective-permute-start.16 = (bf16[64,512]{1,0:T(8,128)(2,1)S(1)}, bf16[64,512]{1,0:T(8,128)(2,1)S(1)}, u32[]{:S(2)}, u32[]{:S(2)}) collective-permute-start(bf16[64,512]{1,0:T(8,128)(2,1)S(1)} %get-tuple-element.58), channel_id=1, source_target_pairs={{0,12},{4,8},{8,4},{12,0},{1,13},{5,9},{9,5},{13,1},{2,14},{6,10},... | collective-permute-start | bytes 196616 | tf_op jit(solution)/shard_map/ppermute | solution.py:38

commit v5 on v4

--- a/solution.py
+++ b/solution.py
@@ -70,12 +70,12 @@
     return jnp.dot(slot, value, preferred_element_type=jnp.float32).astype(jnp.bfloat16)
 
 
-def pick_own(cap, routes, placement, grad, hid, slot_out, near_g, near_h, far_g, far_h, table, *refs):
-    routes_held, placement_held, grad_held, hid_held, sem = refs
+def pick_own(cap, routes, placement, grad, hid, slot_out, table, grad_out, hid_out, far_g, *refs):
+    routes_held, placement_held, sem = refs
     copies = [
         pltpu.make_async_copy(*pair, sem.at[i])
         for i, pair in enumerate(
-            ((routes, routes_held), (placement, placement_held), (grad, grad_held), (hid, hid_held))
+            ((routes, routes_held), (placement, placement_held), (grad, grad_out), (hid, hid_out))
         )
     ]
     for copy in copies:
@@ -87,28 +87,27 @@
         table[j : j + 1] = jnp.full((1, table.shape[1]), placement_held[j], jnp.int32)
     slot = slot_of(routes_held[...], table, lax.axis_index("expert"), experts, cap)
     slot_out[...] = slot
-    near, far_slots = slot[:cap], slot[2 * cap : 3 * cap]
     copies[2].wait()
-    far_g[...] = chosen(far_slots, grad_held[...])
-    near_g[...] = chosen(near, grad_held[...])
+    far_g[...] = chosen(slot[2 * cap : 3 * cap], grad_out[...])
     copies[3].wait()
-    far_h[...] = chosen(far_slots, hid_held[...])
-    near_h[...] = chosen(near, hid_held[...])
-
-
-def pick_next(cap, *refs):
-    table, routes, grad, hid, own_near_g, own_near_h, own_far_g, own_far_h = refs[:8]
-    near_g, near_h, far_g, far_h, near_pack = refs[8:]
-    slot = slot_of(routes[...], table, jnp.bitwise_xor(lax.axis_index("expert"), 1), lax.axis_size("expert"), cap)
-    near, far_slots = slot[cap : 2 * cap], slot[3 * cap :]
-    for own, rows, value, out in (
-        (own_far_g, far_slots, grad, far_g),
-        (own_near_g, near, grad, near_g),
-        (own_near_h, near, hid, near_h),
-        (own_far_h, far_slots, hid, far_h),
+
+
+def pick_next(cap, table, routes, grad, own_far_g, slot_out, far_g):
+    experts = lax.axis_size("expert")
+    slot = slot_of(routes[...], table, jnp.bitwise_xor(lax.axis_index("expert"), 1), experts, cap)
+    slot_out[...] = slot
+    far_g[:cap] = own_far_g[...]
+    far_g[cap:] = chosen(slot[3 * cap :], grad[...])
+
+
+def pick_rest(cap, slot, next_slot, grad, hid, next_grad, next_hid, near_g, near_h, far_h, near_pack):
+    for own, other, value, next_value, out in (
+        (0, 1, grad, next_grad, near_g),
+        (0, 1, hid, next_hid, near_h),
+        (2, 3, hid, next_hid, far_h),
     ):
-        out[:cap] = own[...]
-        out[cap:] = chosen(rows, value[...])
+        out[:cap] = chosen(slot[own * cap : (own + 1) * cap], value[...])
+        out[cap:] = chosen(next_slot[other * cap : (other + 1) * cap], next_value[...])
     cols, share = near_g.shape[1], near_h.shape[1] // 2
     near_pack[:, :cols] = near_g[...]
     near_pack[:, cols:] = near_h[:, other_share(share)]
@@ -244,23 +243,26 @@
 
     routes = routes.reshape(1, tok)
     next_routes, next_grad, next_hid = (swap(x, "expert", 1) for x in (routes, out_grad, hidden))
-    slot, near_g, near_h, far_g, far_h, table = call(
+    slot, table, grad, hid, far_g = call(
         functools.partial(pick_own, cap),
-        [((slots, tok), bf), *[((cap, cols), bf), ((cap, width), bf)] * 2, ((8, 128), jnp.int32)],
+        [((slots, tok), bf), ((8, 128), jnp.int32), ((tok, cols), bf), ((tok, width), bf), ((cap, cols), bf)],
         tuple(far(x) for x in (routes, placement, out_grad, hidden)),
         [ANY] * 4,
         [
             pltpu.VMEM((1, tok), jnp.int32),
             pltpu.SMEM((experts,), jnp.int32),
-            pltpu.VMEM((tok, cols), bf),
-            pltpu.VMEM((tok, width), bf),
             pltpu.SemaphoreType.DMA((4,)),
         ],
     )
-    near_g, near_h, far_g, far_h, near_pack = call(
+    next_slot, far_g = call(
         functools.partial(pick_next, cap),
-        [*[((rows, cols), bf), ((rows, width), bf)] * 2, ((rows, cols + share), bf)],
-        (table, next_routes, next_grad, next_hid, near_g, near_h, far_g, far_h),
+        [((slots, tok), bf), ((rows, cols), bf)],
+        (table, next_routes, next_grad, far_g),
+    )
+    near_g, near_h, far_h, near_pack = call(
+        functools.partial(pick_rest, cap),
+        [((rows, cols), bf), ((rows, width), bf), ((rows, width), bf), ((rows, cols + share), bf)],
+        (slot, next_slot, grad, hid, next_grad, next_hid),
     )
     far_h = swap(far_h, "expert", 2)
     far_g = swap(far_g, "expert", 2)
@@ -281,13 +283,14 @@
     next_out = swap(next_out, "expert", 1)
     (far_send,) = call(far_grads, [(kept, bf)], (odd, far_g), after=(near_keep,))
     far_got = swap(far_send, "tensor", 1)
-    (far_keep,) = call(far_grads, [(kept, f32)], (even, far_g), after=(far_send,))
     other_g = swap(far_g, "dp", 1)
-    last = far_keep
+    last = far_send
     if tensors > 2:
         near_keep, near_send = call(fold, [(cut, f32), (cut, bf)], (near_keep, near_got), after=(last,))
         near_got = swap(near_send, "tensor", 2)
         last = near_send
+    (far_keep,) = call(far_grads, [(kept, f32)], (even, far_g), after=(last,))
+    last = far_keep
     far_out = call(far_outs, [((cap, cols), bf)] * 2, (odd, even, far_h), after=(last, next_out))
     last = far_out[0]
     if tensors > 2:
@@ -299,11 +302,12 @@
     (near_total,) = call(outer_near, [((share, cols), f32)], (near_g, near_h, other_near, far_g, far_h), after=(cut_h,))
     (near_back,) = call(fold, [((rows + 16, column), bf)], (near_keep, near_got), after=(near_total,))
     next_back = swap(near_back, "expert", 1)
+    back = [swap(far_out[k], "expert", 2 + k) for k in (1, 0)]
     far_back = call(fold, [pair, pair], (far_keep, far_got), after=(near_back, other_g))
     output, last = call(
         functools.partial(place, cap),
         [((tok, cols), bf), token],
-        (slot, near_out, next_out, swap(far_out[0], "expert", 2), swap(far_out[1], "expert", 3)),
+        (slot, near_out, next_out, back[1], back[0]),
         after=(far_back[0],),
     )
     pieces = 8

time: 47.8 us -> 47.6 us (level)
    pallas_call x16 -> x17, Pallas kernels: 19.1 us -> 19 us  [call(): pl.pallas_call(late, out_shape=tuple((jax.ShapeDtypeStruct(s, d) for s, d...]
  transfers between devices with their start and end apart: 18 -> 18, of which waited for: 5 -> 5; matrix products, arithmetic and copies ran while one was open for 0% -> 0% of each run, Pallas kernels for 37% -> 38%
where the time goes in v5:
time: 47.6 us; the launch traced here: 47.4 us
  starting transfers between devices  22.2 us (47%)
  Pallas kernels  19 us (40%)
  waiting for transfers between devices  5.4 us (11%)
  between operations  0.79 us (2%)
    ppermute x18, starting transfers between devices, swap(): return lax.ppermute(value, axis, [(i, i ^ offset) for i in range(size)])  22.2 us
    pallas_call x17, Pallas kernels, call(): pl.pallas_call(late, out_shape=tuple((jax.ShapeDtypeStruct(s, d) for s, d...  19 us
    ppermute x18, waiting for transfers between devices, swap(): return lax.ppermute(value, axis, [(i, i ^ offset) for i in range(size)])  5.4 us
  transfers between devices with their start and end apart: 18, of which 5 were waited for; matrix products, arithmetic and copies ran while one was open for 0% of the time, Pallas kernels for 38%

profile of v5, /device:TPU:0, one launch (start us, length us, event | category | flops | bytes accessed | tf_op | source)
XLA Modules:
  0.0 47.4 jit_solution(8785407388706572935)
XLA Ops:
  1.7 1.3 %pick_own.1 = (bf16[256,128]{1,0:T(8,128)(2,1)S(1)}, s32[8,128]{1,0:T(8,128)S(1)}, bf16[128,1792]{1,0:T(8,128)(2,1)S(1)}, bf16[128,2048]{1,0:T(8,128)(2,1)S(1)}, bf16[64,1792]{1,0:T(8,128)(2,1)S(1)}) custom-call(s32[1,128]{1,0:T(1,128)} %bitcast.2, s32[4]{0:T(128)} %refs_1_.1, bf16[128,1792]{1,0:T(8,128)(2,1)} %refs_2_.1, bf16[128,2048]{1,0:T(8,128)(2,1)} %refs_3_.1), custom_call_target="tpu_custom_call" | custom-call | flops 1000 | bytes 1000 | tf_op jit(solution)/shard_map/pick_own/pallas_call | solution.py:20
  3.9 2.9 %collective-permute-start.5 = (bf16[128,1792]{1,0:T(8,128)(2,1)S(1)}, bf16[128,1792]{1,0:T(8,128)(2,1)S(1)}, u32[]{:S(2)}, u32[]{:S(2)}) collective-permute-start(bf16[128,1792]{1,0:T(8,128)(2,1)S(1)} %get-tuple-element.46), channel_id=1, source_target_pairs={{0,8},{4,12},{8,0},{12,4},{1,9},{5,13},{9,1},{13,5},{2,10},{6,14},... | collective-permute-start | bytes 1376264 | tf_op jit(solution)/shard_map/ppermute | solution.py:38
  7.5 1.6 %collective-permute-start.10 = (bf16[128,2816]{1,0:T(8,128)(2,1)S(1)}, bf16[128,2816]{1,0:T(8,128)(2,1)S(1)}, u32[]{:S(2)}, u32[]{:S(2)}) collective-permute-start(bf16[128,2816]{1,0:T(8,128)(2,1)S(1)} %get-tuple-element.52), channel_id=1, source_target_pairs={{0,16},{16,0},{1,17},{17,1},{2,18},{18,2},{3,19},{19,3},{4,20},{20... | collective-permute-start | bytes 2162696 | tf_op jit(solution)/shard_map/ppermute | solution.py:38
  9.6 3.0 %near_odd.1 = (bf16[2,512,1792]{2,1,0:T(8,128)(2,1)S(1)}, bf16[128,1024]{1,0:T(8,128)(2,1)S(1)}) custom-call(bf16[1,2048,1792]{2,1,0:T(8,128)(2,1)} %refs_0_.3, bf16[128,1792]{1,0:T(8,128)(2,1)S(1)} %get-tuple-element.39.refs_1_.refs_2_.refs_0_), custom_call_target="tpu_custom_call" | custom-call | flops 1000 | bytes 1000 | tf_op jit(solution)/shard_map/near_odd/pallas_call | solution.py:20
  12.6 1.7 %collective-permute-start.6 = (bf16[128,1024]{1,0:T(8,128)(2,1)S(1)}, bf16[128,1024]{1,0:T(8,128)(2,1)S(1)}, u32[]{:S(2)}, u32[]{:S(2)}) collective-permute-start(bf16[128,1024]{1,0:T(8,128)(2,1)S(1)} %get-tuple-element.48), channel_id=1, source_target_pairs={{0,1},{1,0},{2,3},{3,2},{4,5},{5,4},{6,7},{7,6},{8,9},{9,8},{10,11... | collective-permute-start | bytes 786440 | tf_op jit(solution)/shard_map/ppermute | solution.py:38
  14.2 3.6 %near_even.1 = (bf16[2,512,1792]{2,1,0:T(8,128)(2,1)S(1)}, f32[128,1024]{1,0:T(8,128)S(1)}, bf16[64,1792]{1,0:T(8,128)(2,1)S(1)}, bf16[64,1792]{1,0:T(8,128)(2,1)S(1)}) custom-call(bf16[1,2048,1792]{2,1,0:T(8,128)(2,1)} %refs_0_.3, bf16[2,512,1792]{2,1,0:T(8,128)(2,1)S(1)} %get-tuple-element.40.refs_1_.refs_0_, ...), custom_call_target="tpu_custom_call" | custom-call | flops 1000 | bytes 1000 | tf_op jit(solution)/shard_map/near_even/pallas_call | solution.py:20
  18.1 1.3 %far_grads.2.refs_2_ = bf16[128,1024]{1,0:T(8,128)(2,1)S(1)} custom-call(bf16[2,512,1792]{2,1,0:T(8,128)(2,1)S(1)} %get-tuple-element.40.refs_1_.refs_0_, bf16[128,1792]{1,0:T(8,128)(2,1)S(1)} %collective-permute-done.5.refs_1_.refs_3_, f32[128,1024]{1,0:T(8,128)S(1)} %get-tuple-element.47.refs_2_.refs_0_), custom_call_target="tpu_custom_call" | custom-call | flops 1000 | bytes 1000 | tf_op jit(solution)/shard_map/far_grads/pallas_call | solution.py:20
  19.4 2.2 %collective-permute-start.9 = (bf16[128,1024]{1,0:T(8,128)(2,1)S(1)}, bf16[128,1024]{1,0:T(8,128)(2,1)S(1)}, u32[]{:S(2)}, u32[]{:S(2)}) collective-permute-start(bf16[128,1024]{1,0:T(8,128)(2,1)S(1)} %far_grads.2.refs_2_), channel_id=1, source_target_pairs={{0,1},{1,0},{2,3},{3,2},{4,5},{5,4},{6,7},{7,6},{8,9},{9,8},{10,11... | collective-permute-start | bytes 786440 | tf_op jit(solution)/shard_map/ppermute | solution.py:38
  21.7 1.5 %collective-permute-start.13 = (bf16[128,1792]{1,0:T(8,128)(2,1)S(1)}, bf16[128,1792]{1,0:T(8,128)(2,1)S(1)}, u32[]{:S(2)}, u32[]{:S(2)}) collective-permute-start(bf16[128,1792]{1,0:T(8,128)(2,1)S(1)} %collective-permute-done.5.refs_1_.refs_3_), channel_id=1, source_target_pairs={{0,16},{16,0},{1,17},{17,1},{2,18},{18,2},{3,19},{19,3},{4,20},{20... | collective-permute-start | bytes 1376264 | tf_op jit(solution)/shard_map/ppermute | solution.py:38
  23.2 2.7 %collective-permute-start.12 = (bf16[128,512]{1,0:T(8,128)(2,1)S(1)}, bf16[128,512]{1,0:T(8,128)(2,1)S(1)}, u32[]{:S(2)}, u32[]{:S(2)}) collective-permute-start(bf16[128,512]{1,0:T(8,128)(2,1)S(1)} %get-tuple-element.49.refs_2_), channel_id=1, source_target_pairs={{0,2},{1,3},{2,0},{3,1},{4,6},{5,7},{6,4},{7,5},{8,10},{9,11},{10,... | collective-permute-start | bytes 393224 | tf_op jit(solution)/shard_map/ppermute | solution.py:38
  25.9 1.3 %far_grads.3.refs_3_.refs_0_ = f32[128,1024]{1,0:T(8,128)S(1)} custom-call(bf16[2,512,1792]{2,1,0:T(8,128)(2,1)S(1)} %get-tuple-element.44.refs_0_.refs_1_, bf16[128,1792]{1,0:T(8,128)(2,1)S(1)} %collective-permute-done.5.refs_1_.refs_3_, bf16[128,512]{1,0:T(8,128)(2,1)S(1)} %get-tuple-element.49.refs_2_), custom_call_target="tpu_custom_call" | custom-call | flops 1000 | bytes 1000 | tf_op jit(solution)/shard_map/far_grads/pallas_call | solution.py:20
  27.2 1.7 %collective-permute-done.4.refs_2_.refs_0_.refs_4_ = bf16[128,2048]{1,0:T(8,128)(2,1)S(1)} collective-permute-done((bf16[128,2048]{1,0:T(8,128)(2,1)S(1)}, bf16[128,2048]{1,0:T(8,128)(2,1)S(1)}, u32[]{:S(2)}, u32[]{:S(2)}) %collective-permute-start.4) | collective-permute-done | bytes 524320 | tf_op jit(solution)/shard_map/ppermute | solution.py:38
  28.9 1.1 %far_outs.1 = (bf16[64,1792]{1,0:T(8,128)(2,1)S(1)}, bf16[64,1792]{1,0:T(8,128)(2,1)S(1)}) custom-call(bf16[2,512,1792]{2,1,0:T(8,128)(2,1)S(1)} %get-tuple-element.40.refs_1_.refs_0_, bf16[2,512,1792]{2,1,0:T(8,128)(2,1)S(1)} %get-tuple-element.44.refs_0_.refs_1_, bf16[128,2048]{1,0:T(8,128)(2,1)S(1)} %collective-permute-done.4.refs_2_.refs_0_.refs_4_, ...), custom_call_target="tpu_custom_call" | custom-call | flops 1000 | bytes 1000 | tf_op jit(solution)/shard_map/far_outs/pallas_call | solution.py:20
  30.0 1.8 %collective-permute-start.7 = (bf16[64,1792]{1,0:T(8,128)(2,1)S(1)}, bf16[64,1792]{1,0:T(8,128)(2,1)S(1)}, u32[]{:S(2)}, u32[]{:S(2)}) collective-permute-start(bf16[64,1792]{1,0:T(8,128)(2,1)S(1)} %get-tuple-element.50.refs_2_), channel_id=1, source_target_pairs={{0,8},{4,12},{8,0},{12,4},{1,9},{5,13},{9,1},{13,5},{2,10},{6,14},... | collective-permute-start | bytes 688136 | tf_op jit(solution)/shard_map/ppermute | solution.py:38
  31.9 2.7 %collective-permute-start.11 = (bf16[128,512]{1,0:T(8,128)(2,1)S(1)}, bf16[128,512]{1,0:T(8,128)(2,1)S(1)}, u32[]{:S(2)}, u32[]{:S(2)}) collective-permute-start(bf16[128,512]{1,0:T(8,128)(2,1)S(1)} %get-tuple-element.54.refs_1_), channel_id=1, source_target_pairs={{0,2},{1,3},{2,0},{3,1},{4,6},{5,7},{6,4},{7,5},{8,10},{9,11},{10,... | collective-permute-start | bytes 393224 | tf_op jit(solution)/shard_map/ppermute | solution.py:38
  34.6 1.6 %collective-permute-start.17 = (bf16[128,1024]{1,0:T(8,128)(2,1)S(1)}, bf16[128,1024]{1,0:T(8,128)(2,1)S(1)}, u32[]{:S(2)}, u32[]{:S(2)}) collective-permute-start(bf16[128,1024]{1,0:T(8,128)(2,1)S(1)} %cut_other.1.refs_5_), channel_id=1, source_target_pairs={{0,16},{16,0},{1,17},{17,1},{2,18},{18,2},{3,19},{19,3},{4,20},{20... | collective-permute-start | bytes 786440 | tf_op jit(solution)/shard_map/ppermute | solution.py:38
  36.2 2.1 %outer_near.1.refs_2_.refs_0_ = f32[1024,1792]{1,0:T(8,128)S(1)} custom-call(bf16[128,1792]{1,0:T(8,128)(2,1)S(1)} %get-tuple-element.39.refs_1_.refs_2_.refs_0_, bf16[128,2048]{1,0:T(8,128)(2,1)S(1)} %get-tuple-element.41.refs_3_.refs_1_, bf16[128,2816]{1,0:T(8,128)(2,1)S(1)} %collective-permute-done.10.refs_3_.refs_2_, ...), custom_call_target="tpu_custom_call" | custom-call | flops 1000 | bytes 1000 | tf_op jit(solution)/shard_map/outer_near/pallas_call | solution.py:20
  38.3 1.8 %collective-permute-done.11.refs_1_ = bf16[128,512]{1,0:T(8,128)(2,1)S(1)} collective-permute-done((bf16[128,512]{1,0:T(8,128)(2,1)S(1)}, bf16[128,512]{1,0:T(8,128)(2,1)S(1)}, u32[]{:S(2)}, u32[]{:S(2)}) %collective-permute-start.11) | collective-permute-done | bytes 131104 | tf_op jit(solution)/shard_map/ppermute | solution.py:38
  40.1 0.7 %collective-permute-start.15 = (bf16[64,512]{1,0:T(8,128)(2,1)S(1)}, bf16[64,512]{1,0:T(8,128)(2,1)S(1)}, u32[]{:S(2)}, u32[]{:S(2)}) collective-permute-start(bf16[64,512]{1,0:T(8,128)(2,1)S(1)} %get-tuple-element.56.refs_5_), channel_id=1, source_target_pairs={{0,8},{4,12},{8,0},{12,4},{1,9},{5,13},{9,1},{13,5},{2,10},{6,14},... | collective-permute-start | bytes 196616 | tf_op jit(solution)/shard_map/ppermute | solution.py:38
  40.8 1.3 %collective-permute-start.16 = (bf16[64,512]{1,0:T(8,128)(2,1)S(1)}, bf16[64,512]{1,0:T(8,128)(2,1)S(1)}, u32[]{:S(2)}, u32[]{:S(2)}) collective-permute-start(bf16[64,512]{1,0:T(8,128)(2,1)S(1)} %get-tuple-element.58), channel_id=1, source_target_pairs={{0,12},{4,8},{8,4},{12,0},{1,13},{5,9},{9,5},{13,1},{2,14},{6,10},... | collective-permute-start | bytes 196616 | tf_op jit(solution)/shard_map/ppermute | solution.py:38
  42.1 1.1 %collective-permute-done.8.refs_4_ = bf16[64,1792]{1,0:T(8,128)(2,1)S(1)} collective-permute-done((bf16[64,1792]{1,0:T(8,128)(2,1)S(1)}, bf16[64,1792]{1,0:T(8,128)(2,1)S(1)}, u32[]{:S(2)}, u32[]{:S(2)}) %collective-permute-start.8) | collective-permute-done | bytes 229408 | tf_op jit(solution)/shard_map/ppermute | solution.py:38
  43.2 1.1 %place.2 = (bf16[128,1792]{1,0:T(8,128)(2,1)}, f32[8,128]{1,0:T(8,128)S(1)}) custom-call(bf16[256,128]{1,0:T(8,128)(2,1)S(1)} %get-tuple-element.33.refs_0_, bf16[64,1792]{1,0:T(8,128)(2,1)S(1)} %get-tuple-element.42.refs_1_, bf16[64,1792]{1,0:T(8,128)(2,1)S(1)} %collective-permute-done.3.refs_4_.refs_2_, ...), custom_call_target="tpu_custom_call" | custom-call | flops 1000 | bytes 1000 | tf_op jit(solution)/shard_map/place/pallas_call | solution.py:20
  44.2 2.3 %outer_far.1 = (bf16[1,1024,1792]{2,1,0:T(8,128)(2,1)}, f32[8,128]{1,0:T(8,128)S(1)}) custom-call(f32[1024,1792]{1,0:T(8,128)S(1)} %outer_near.1.refs_2_.refs_0_, bf16[128,1792]{1,0:T(8,128)(2,1)S(1)} %collective-permute-done.13.refs_3_.refs_1_, bf16[128,1024]{1,0:T(8,128)(2,1)S(1)} %collective-permute-done.17.refs_2_, f32[8,128]{1,0:T(8,128)S(1)} %get-tuple-element.59.refs_3_), custom_call_target="tpu_custom_call" | custom-call | flops 1000 | bytes 1000 | tf_op jit(solution)/shard_map/outer_far/pallas_call | solution.py:20
  46.5 0.9 %place.3 = (bf16[128,512]{1,0:T(8,128)(2,1)}, f32[8,128]{1,0:T(8,128)}) custom-call(bf16[256,128]{1,0:T(8,128)(2,1)S(1)} %get-tuple-element.33.refs_0_, bf16[144,512]{1,0:T(8,128)(2,1)S(1)} %fold.6.refs_2_.refs_1_, bf16[144,512]{1,0:T(8,128)(2,1)S(1)} %collective-permute-done.14.refs_2_, bf16[64,512]{1,0:T(8,128)(2,1)S(1)} %collective-permute-done.15.refs_3_, ...), custom_call_target="tpu_custom_call" | custom-call | flops 1000 | bytes 1000 | tf_op jit(solution)/shard_map/place/pallas_call | solution.py:20
  (29 shorter events, 3.6 us)
Async XLA Ops:
  0.6 6.2 %collective-permute-start.2 = (bf16[128,2048]{1,0:T(8,128)(2,1)}, bf16[128,2048]{1,0:T(8,128)(2,1)S(1)}, u32[]{:S(2)}, u32[]{:S(2)}) collective-permute-start(bf16[128,2048]{1,0:T(8,128)(2,1)} %refs_3_.1), channel_id=1, source_target_pairs={{0,4},{4,0},{8,12},{12,8},{1,5},{5,1},{9,13},{13,9},{2,6},{6,2},{1... | collective-permute-start | bytes 1572872 | tf_op jit(solution)/shard_map/ppermute | solution.py:38
  1.1 2.4 %collective-permute-start.1 = (bf16[128,1792]{1,0:T(8,128)(2,1)}, bf16[128,1792]{1,0:T(8,128)(2,1)S(1)}, u32[]{:S(2)}, u32[]{:S(2)}) collective-permute-start(bf16[128,1792]{1,0:T(8,128)(2,1)} %refs_2_.1), channel_id=1, source_target_pairs={{0,4},{4,0},{8,12},{12,8},{1,5},{5,1},{9,13},{13,9},{2,6},{6,2},{1... | collective-permute-start | bytes 1376264 | tf_op jit(solution)/shard_map/ppermute | solution.py:38
  1.2 2.3 %collective-permute-start = (s32[1,128]{1,0:T(1,128)}, s32[1,128]{1,0:T(1,128)S(1)}, u32[]{:S(2)}, u32[]{:S(2)}) collective-permute-start(s32[1,128]{1,0:T(1,128)} %bitcast.1), channel_id=1, source_target_pairs={{0,4},{4,0},{8,12},{12,8},{1,5},{5,1},{9,13},{13,9},{2,6},{6,2},{1... | collective-permute-start | bytes 1544 | tf_op jit(solution)/shard_map/ppermute | solution.py:38
  3.9 14.2 %collective-permute-start.5 = (bf16[128,1792]{1,0:T(8,128)(2,1)S(1)}, bf16[128,1792]{1,0:T(8,128)(2,1)S(1)}, u32[]{:S(2)}, u32[]{:S(2)}) collective-permute-start(bf16[128,1792]{1,0:T(8,128)(2,1)S(1)} %get-tuple-element.46), channel_id=1, source_target_pairs={{0,8},{4,12},{8,0},{12,4},{1,9},{5,13},{9,1},{13,5},{2,10},{6,14},... | collective-permute-start | bytes 1376264 | tf_op jit(solution)/shard_map/ppermute | solution.py:38
  7.5 24.4 %collective-permute-start.10 = (bf16[128,2816]{1,0:T(8,128)(2,1)S(1)}, bf16[128,2816]{1,0:T(8,128)(2,1)S(1)}, u32[]{:S(2)}, u32[]{:S(2)}) collective-permute-start(bf16[128,2816]{1,0:T(8,128)(2,1)S(1)} %get-tuple-element.52), channel_id=1, source_target_pairs={{0,16},{16,0},{1,17},{17,1},{2,18},{18,2},{3,19},{19,3},{4,20},{20... | collective-permute-start | bytes 2162696 | tf_op jit(solution)/shard_map/ppermute | solution.py:38
  9.0 19.8 %collective-permute-start.4 = (bf16[128,2048]{1,0:T(8,128)(2,1)S(1)}, bf16[128,2048]{1,0:T(8,128)(2,1)S(1)}, u32[]{:S(2)}, u32[]{:S(2)}) collective-permute-start(bf16[128,2048]{1,0:T(8,128)(2,1)S(1)} %get-tuple-element.45), channel_id=1, source_target_pairs={{0,8},{4,12},{8,0},{12,4},{1,9},{5,13},{9,1},{13,5},{2,10},{6,14},... | collective-permute-start | bytes 1572872 | tf_op jit(solution)/shard_map/ppermute | solution.py:38
  12.6 9.1 %collective-permute-start.6 = (bf16[128,1024]{1,0:T(8,128)(2,1)S(1)}, bf16[128,1024]{1,0:T(8,128)(2,1)S(1)}, u32[]{:S(2)}, u32[]{:S(2)}) collective-permute-start(bf16[128,1024]{1,0:T(8,128)(2,1)S(1)} %get-tuple-element.48), channel_id=1, source_target_pairs={{0,1},{1,0},{2,3},{3,2},{4,5},{5,4},{6,7},{7,6},{8,9},{9,8},{10,11... | collective-permute-start | bytes 786440 | tf_op jit(solution)/shard_map/ppermute | solution.py:38
  17.9 5.4 %collective-permute-start.3 = (bf16[64,1792]{1,0:T(8,128)(2,1)S(1)}, bf16[64,1792]{1,0:T(8,128)(2,1)S(1)}, u32[]{:S(2)}, u32[]{:S(2)}) collective-permute-start(bf16[64,1792]{1,0:T(8,128)(2,1)S(1)} %get-tuple-element.43), channel_id=1, source_target_pairs={{0,4},{4,0},{8,12},{12,8},{1,5},{5,1},{9,13},{13,9},{2,6},{6,2},{1... | collective-permute-start | bytes 688136 | tf_op jit(solution)/shard_map/ppermute | solution.py:38
  19.4 12.4 %collective-permute-start.9 = (bf16[128,1024]{1,0:T(8,128)(2,1)S(1)}, bf16[128,1024]{1,0:T(8,128)(2,1)S(1)}, u32[]{:S(2)}, u32[]{:S(2)}) collective-permute-start(bf16[128,1024]{1,0:T(8,128)(2,1)S(1)} %far_grads.2.refs_2_), channel_id=1, source_target_pairs={{0,1},{1,0},{2,3},{3,2},{4,5},{5,4},{6,7},{7,6},{8,9},{9,8},{10,11... | collective-permute-start | bytes 786440 | tf_op jit(solution)/shard_map/ppermute | solution.py:38
  21.7 18.4 %collective-permute-start.13 = (bf16[128,1792]{1,0:T(8,128)(2,1)S(1)}, bf16[128,1792]{1,0:T(8,128)(2,1)S(1)}, u32[]{:S(2)}, u32[]{:S(2)}) collective-permute-start(bf16[128,1792]{1,0:T(8,128)(2,1)S(1)} %collective-permute-done.5.refs_1_.refs_3_), channel_id=1, source_target_pairs={{0,16},{16,0},{1,17},{17,1},{2,18},{18,2},{3,19},{19,3},{4,20},{20... | collective-permute-start | bytes 1376264 | tf_op jit(solution)/shard_map/ppermute | solution.py:38
  23.2 12.9 %collective-permute-start.12 = (bf16[128,512]{1,0:T(8,128)(2,1)S(1)}, bf16[128,512]{1,0:T(8,128)(2,1)S(1)}, u32[]{:S(2)}, u32[]{:S(2)}) collective-permute-start(bf16[128,512]{1,0:T(8,128)(2,1)S(1)} %get-tuple-element.49.refs_2_), channel_id=1, source_target_pairs={{0,2},{1,3},{2,0},{3,1},{4,6},{5,7},{6,4},{7,5},{8,10},{9,11},{10,... | collective-permute-start | bytes 393224 | tf_op jit(solution)/shard_map/ppermute | solution.py:38
  30.0 10.8 %collective-permute-start.7 = (bf16[64,1792]{1,0:T(8,128)(2,1)S(1)}, bf16[64,1792]{1,0:T(8,128)(2,1)S(1)}, u32[]{:S(2)}, u32[]{:S(2)}) collective-permute-start(bf16[64,1792]{1,0:T(8,128)(2,1)S(1)} %get-tuple-element.50.refs_2_), channel_id=1, source_target_pairs={{0,8},{4,12},{8,0},{12,4},{1,9},{5,13},{9,1},{13,5},{2,10},{6,14},... | collective-permute-start | bytes 688136 | tf_op jit(solution)/shard_map/ppermute | solution.py:38
  31.9 8.2 %collective-permute-start.11 = (bf16[128,512]{1,0:T(8,128)(2,1)S(1)}, bf16[128,512]{1,0:T(8,128)(2,1)S(1)}, u32[]{:S(2)}, u32[]{:S(2)}) collective-permute-start(bf16[128,512]{1,0:T(8,128)(2,1)S(1)} %get-tuple-element.54.refs_1_), channel_id=1, source_target_pairs={{0,2},{1,3},{2,0},{3,1},{4,6},{5,7},{6,4},{7,5},{8,10},{9,11},{10,... | collective-permute-start | bytes 393224 | tf_op jit(solution)/shard_map/ppermute | solution.py:38
  34.6 9.7 %collective-permute-start.17 = (bf16[128,1024]{1,0:T(8,128)(2,1)S(1)}, bf16[128,1024]{1,0:T(8,128)(2,1)S(1)}, u32[]{:S(2)}, u32[]{:S(2)}) collective-permute-start(bf16[128,1024]{1,0:T(8,128)(2,1)S(1)} %cut_other.1.refs_5_), channel_id=1, source_target_pairs={{0,16},{16,0},{1,17},{17,1},{2,18},{18,2},{3,19},{19,3},{4,20},{20... | collective-permute-start | bytes 786440 | tf_op jit(solution)/shard_map/ppermute | solution.py:38
  36.2 7.0 %collective-permute-start.8 = (bf16[64,1792]{1,0:T(8,128)(2,1)S(1)}, bf16[64,1792]{1,0:T(8,128)(2,1)S(1)}, u32[]{:S(2)}, u32[]{:S(2)}) collective-permute-start(bf16[64,1792]{1,0:T(8,128)(2,1)S(1)} %get-tuple-element.51), channel_id=1, source_target_pairs={{0,12},{4,8},{8,4},{12,0},{1,13},{5,9},{9,5},{13,1},{2,14},{6,10},... | collective-permute-start | bytes 688136 | tf_op jit(solution)/shard_map/ppermute | solution.py:38
  40.1 6.4 %collective-permute-start.14 = (bf16[144,512]{1,0:T(8,128)(2,1)S(1)}, bf16[144,512]{1,0:T(8,128)(2,1)S(1)}, u32[]{:S(2)}, u32[]{:S(2)}) collective-permute-start(bf16[144,512]{1,0:T(8,128)(2,1)S(1)} %fold.6.refs_2_.refs_1_), channel_id=1, source_target_pairs={{0,4},{4,0},{8,12},{12,8},{1,5},{5,1},{9,13},{13,9},{2,6},{6,2},{1... | collective-permute-start | bytes 442376 | tf_op jit(solution)/shard_map/ppermute | solution.py:38
  40.1 6.4 %collective-permute-start.15 = (bf16[64,512]{1,0:T(8,128)(2,1)S(1)}, bf16[64,512]{1,0:T(8,128)(2,1)S(1)}, u32[]{:S(2)}, u32[]{:S(2)}) collective-permute-start(bf16[64,512]{1,0:T(8,128)(2,1)S(1)} %get-tuple-element.56.refs_5_), channel_id=1, source_target_pairs={{0,8},{4,12},{8,0},{12,4},{1,9},{5,13},{9,1},{13,5},{2,10},{6,14},... | collective-permute-start | bytes 196616 | tf_op jit(solution)/shard_map/ppermute | solution.py:38
  40.8 5.7 %collective-permute-start.16 = (bf16[64,512]{1,0:T(8,128)(2,1)S(1)}, bf16[64,512]{1,0:T(8,128)(2,1)S(1)}, u32[]{:S(2)}, u32[]{:S(2)}) collective-permute-start(bf16[64,512]{1,0:T(8,128)(2,1)S(1)} %get-tuple-element.58), channel_id=1, source_target_pairs={{0,12},{4,8},{8,4},{12,0},{1,13},{5,9},{9,5},{13,1},{2,14},{6,10},... | collective-permute-start | bytes 196616 | tf_op jit(solution)/shard_map/ppermute | solution.py:38

commit v6 on v5

--- a/solution.py
+++ b/solution.py
@@ -152,8 +152,17 @@
     return copies
 
 
-def near_odd(weight, grads, odd, send, sem):
-    for i, copy in enumerate(weight_copies(1, weight, odd, sem)):
+def near_odd(weight, grads, slot, odd, send, slot_of_token, sem):
+    copies = weight_copies(1, weight, odd, sem)
+    tok = slot.shape[1]
+    same = lax.broadcasted_iota(jnp.int32, (tok, tok), 0) == lax.broadcasted_iota(jnp.int32, (tok, tok), 1)
+    slot_of_token[...] = lax.dot_general(
+        jnp.where(same, 1.0, 0.0).astype(jnp.bfloat16),
+        slot[...],
+        (((1,), (1,)), ((), ())),
+        preferred_element_type=jnp.float32,
+    ).astype(jnp.bfloat16)
+    for i, copy in enumerate(copies):
         copy.wait()
         hidden_grad(odd, i, grads, send)
 
@@ -197,8 +206,8 @@
 def place(cap, slot, *refs):
     *rows, out, token = refs
     rows = [ref[...] if ref.shape[0] == cap else ref[i % 2 * cap : (i % 2 + 1) * cap] for i, ref in enumerate(rows)]
-    out[...] = lax.dot_general(
-        slot[...], jnp.concatenate(rows, axis=0), (((0,), (0,)), ((), ())), preferred_element_type=jnp.float32
+    out[...] = jnp.dot(
+        slot[...], jnp.concatenate(rows, axis=0), preferred_element_type=jnp.float32
     ).astype(out.dtype)
     token[...] = jnp.zeros_like(token)
 
@@ -269,8 +278,12 @@
     other_near = swap(near_pack, "dp", 1)
     part = ((tensors // 2, column, cols), bf)
     sems = [pltpu.SemaphoreType.DMA((tensors // 2,))]
-    odd, near_send = call(
-        near_odd, [part, (kept, bf)], (far(w_down), near_g), [ANY, VMEM], sems
+    odd, near_send, placer = call(
+        near_odd,
+        [part, (kept, bf), ((tok, slots), bf)],
+        (far(w_down), near_g, slot),
+        [ANY, VMEM, VMEM],
+        sems,
     )
     near_got = swap(near_send, "tensor", 1)
     even, near_keep, near_out, next_out = call(
@@ -302,12 +315,12 @@
     (near_total,) = call(outer_near, [((share, cols), f32)], (near_g, near_h, other_near, far_g, far_h), after=(cut_h,))
     (near_back,) = call(fold, [((rows + 16, column), bf)], (near_keep, near_got), after=(near_total,))
     next_back = swap(near_back, "expert", 1)
-    back = [swap(far_out[k], "expert", 2 + k) for k in (1, 0)]
+    back = [swap(far_out[k], "expert", 2 + k) for k in (0, 1)][::-1]
     far_back = call(fold, [pair, pair], (far_keep, far_got), after=(near_back, other_g))
     output, last = call(
         functools.partial(place, cap),
         [((tok, cols), bf), token],
-        (slot, near_out, next_out, back[1], back[0]),
+        (placer, near_out, next_out, back[1], back[0]),
         after=(far_back[0],),
     )
     pieces = 8
@@ -324,7 +337,7 @@
         functools.partial(place, cap),
         [((tok, column), bf), token],
         (
-            slot,
+            placer,
             near_back,
             next_back,
             swap(far_back[0], "expert", 2),

time: 47.6 us -> 47.5 us (level)
  no operation moved by 1% of the time
where the time goes in v6:
time: 47.5 us; the launch traced here: 47.4 us
  starting transfers between devices  22.2 us (47%)
  Pallas kernels  19 us (40%)
  waiting for transfers between devices  5.37 us (11%)
  between operations  0.79 us (2%)
    ppermute x18, starting transfers between devices, swap(): return lax.ppermute(value, axis, [(i, i ^ offset) for i in range(size)])  22.2 us
    pallas_call x17, Pallas kernels, call(): pl.pallas_call(late, out_shape=tuple((jax.ShapeDtypeStruct(s, d) for s, d...  19 us
    ppermute x18, waiting for transfers between devices, swap(): return lax.ppermute(value, axis, [(i, i ^ offset) for i in range(size)])  5.37 us
  transfers between devices with their start and end apart: 18, of which 5 were waited for; matrix products, arithmetic and copies ran while one was open for 0% of the time, Pallas kernels for 38%

profile of v6, /device:TPU:0, one launch (start us, length us, event | category | flops | bytes accessed | tf_op | source)
XLA Modules:
  0.0 47.4 jit_solution(18367417461577871711)
XLA Ops:
  1.7 1.3 %pick_own.1 = (bf16[256,128]{1,0:T(8,128)(2,1)S(1)}, s32[8,128]{1,0:T(8,128)S(1)}, bf16[128,1792]{1,0:T(8,128)(2,1)S(1)}, bf16[128,2048]{1,0:T(8,128)(2,1)S(1)}, bf16[64,1792]{1,0:T(8,128)(2,1)S(1)}) custom-call(s32[1,128]{1,0:T(1,128)} %bitcast.2, s32[4]{0:T(128)} %refs_1_.1, bf16[128,1792]{1,0:T(8,128)(2,1)} %refs_2_.1, bf16[128,2048]{1,0:T(8,128)(2,1)} %refs_3_.1), custom_call_target="tpu_custom_call" | custom-call | flops 1000 | bytes 1000 | tf_op jit(solution)/shard_map/pick_own/pallas_call | solution.py:20
  3.9 2.9 %collective-permute-start.5 = (bf16[128,1792]{1,0:T(8,128)(2,1)S(1)}, bf16[128,1792]{1,0:T(8,128)(2,1)S(1)}, u32[]{:S(2)}, u32[]{:S(2)}) collective-permute-start(bf16[128,1792]{1,0:T(8,128)(2,1)S(1)} %get-tuple-element.48), channel_id=1, source_target_pairs={{0,8},{4,12},{8,0},{12,4},{1,9},{5,13},{9,1},{13,5},{2,10},{6,14},... | collective-permute-start | bytes 1376264 | tf_op jit(solution)/shard_map/ppermute | solution.py:38
  7.5 1.6 %collective-permute-start.10 = (bf16[128,2816]{1,0:T(8,128)(2,1)S(1)}, bf16[128,2816]{1,0:T(8,128)(2,1)S(1)}, u32[]{:S(2)}, u32[]{:S(2)}) collective-permute-start(bf16[128,2816]{1,0:T(8,128)(2,1)S(1)} %get-tuple-element.54), channel_id=1, source_target_pairs={{0,16},{16,0},{1,17},{17,1},{2,18},{18,2},{3,19},{19,3},{4,20},{20... | collective-permute-start | bytes 2162696 | tf_op jit(solution)/shard_map/ppermute | solution.py:38
  9.6 3.0 %near_odd.1 = (bf16[2,512,1792]{2,1,0:T(8,128)(2,1)S(1)}, bf16[128,1024]{1,0:T(8,128)(2,1)S(1)}, bf16[128,256]{1,0:T(8,128)(2,1)S(1)}) custom-call(bf16[1,2048,1792]{2,1,0:T(8,128)(2,1)} %refs_0_.3, bf16[128,1792]{1,0:T(8,128)(2,1)S(1)} %get-tuple-element.40.refs_1_.refs_2_.refs_0_, bf16[256,128]{1,0:T(8,128)(2,1)S(1)} %get-tuple-element.34.refs_0_.refs_2_), custom_call_target="tpu_custom_call" | custom-call | flops 1000 | bytes 1000 | tf_op jit(solution)/shard_map/near_odd/pallas_call | solution.py:20
  12.6 1.7 %collective-permute-start.6 = (bf16[128,1024]{1,0:T(8,128)(2,1)S(1)}, bf16[128,1024]{1,0:T(8,128)(2,1)S(1)}, u32[]{:S(2)}, u32[]{:S(2)}) collective-permute-start(bf16[128,1024]{1,0:T(8,128)(2,1)S(1)} %get-tuple-element.50), channel_id=1, source_target_pairs={{0,1},{1,0},{2,3},{3,2},{4,5},{5,4},{6,7},{7,6},{8,9},{9,8},{10,11... | collective-permute-start | bytes 786440 | tf_op jit(solution)/shard_map/ppermute | solution.py:38
  14.2 3.7 %near_even.1 = (bf16[2,512,1792]{2,1,0:T(8,128)(2,1)S(1)}, f32[128,1024]{1,0:T(8,128)S(1)}, bf16[64,1792]{1,0:T(8,128)(2,1)S(1)}, bf16[64,1792]{1,0:T(8,128)(2,1)S(1)}) custom-call(bf16[1,2048,1792]{2,1,0:T(8,128)(2,1)} %refs_0_.3, bf16[2,512,1792]{2,1,0:T(8,128)(2,1)S(1)} %get-tuple-element.42.refs_1_.refs_0_, ...), custom_call_target="tpu_custom_call" | custom-call | flops 1000 | bytes 1000 | tf_op jit(solution)/shard_map/near_even/pallas_call | solution.py:20
  18.1 1.3 %far_grads.2.refs_2_ = bf16[128,1024]{1,0:T(8,128)(2,1)S(1)} custom-call(bf16[2,512,1792]{2,1,0:T(8,128)(2,1)S(1)} %get-tuple-element.42.refs_1_.refs_0_, bf16[128,1792]{1,0:T(8,128)(2,1)S(1)} %collective-permute-done.5.refs_1_.refs_3_, f32[128,1024]{1,0:T(8,128)S(1)} %get-tuple-element.49.refs_2_.refs_0_), custom_call_target="tpu_custom_call" | custom-call | flops 1000 | bytes 1000 | tf_op jit(solution)/shard_map/far_grads/pallas_call | solution.py:20
  19.4 2.2 %collective-permute-start.9 = (bf16[128,1024]{1,0:T(8,128)(2,1)S(1)}, bf16[128,1024]{1,0:T(8,128)(2,1)S(1)}, u32[]{:S(2)}, u32[]{:S(2)}) collective-permute-start(bf16[128,1024]{1,0:T(8,128)(2,1)S(1)} %far_grads.2.refs_2_), channel_id=1, source_target_pairs={{0,1},{1,0},{2,3},{3,2},{4,5},{5,4},{6,7},{7,6},{8,9},{9,8},{10,11... | collective-permute-start | bytes 786440 | tf_op jit(solution)/shard_map/ppermute | solution.py:38
  21.7 1.5 %collective-permute-start.13 = (bf16[128,1792]{1,0:T(8,128)(2,1)S(1)}, bf16[128,1792]{1,0:T(8,128)(2,1)S(1)}, u32[]{:S(2)}, u32[]{:S(2)}) collective-permute-start(bf16[128,1792]{1,0:T(8,128)(2,1)S(1)} %collective-permute-done.5.refs_1_.refs_3_), channel_id=1, source_target_pairs={{0,16},{16,0},{1,17},{17,1},{2,18},{18,2},{3,19},{19,3},{4,20},{20... | collective-permute-start | bytes 1376264 | tf_op jit(solution)/shard_map/ppermute | solution.py:38
  23.2 2.7 %collective-permute-start.12 = (bf16[128,512]{1,0:T(8,128)(2,1)S(1)}, bf16[128,512]{1,0:T(8,128)(2,1)S(1)}, u32[]{:S(2)}, u32[]{:S(2)}) collective-permute-start(bf16[128,512]{1,0:T(8,128)(2,1)S(1)} %get-tuple-element.51.refs_2_), channel_id=1, source_target_pairs={{0,2},{1,3},{2,0},{3,1},{4,6},{5,7},{6,4},{7,5},{8,10},{9,11},{10,... | collective-permute-start | bytes 393224 | tf_op jit(solution)/shard_map/ppermute | solution.py:38
  25.9 1.3 %far_grads.3.refs_3_.refs_0_ = f32[128,1024]{1,0:T(8,128)S(1)} custom-call(bf16[2,512,1792]{2,1,0:T(8,128)(2,1)S(1)} %get-tuple-element.46.refs_0_.refs_1_, bf16[128,1792]{1,0:T(8,128)(2,1)S(1)} %collective-permute-done.5.refs_1_.refs_3_, bf16[128,512]{1,0:T(8,128)(2,1)S(1)} %get-tuple-element.51.refs_2_), custom_call_target="tpu_custom_call" | custom-call | flops 1000 | bytes 1000 | tf_op jit(solution)/shard_map/far_grads/pallas_call | solution.py:20
  27.2 1.7 %collective-permute-done.4.refs_2_.refs_0_.refs_4_ = bf16[128,2048]{1,0:T(8,128)(2,1)S(1)} collective-permute-done((bf16[128,2048]{1,0:T(8,128)(2,1)S(1)}, bf16[128,2048]{1,0:T(8,128)(2,1)S(1)}, u32[]{:S(2)}, u32[]{:S(2)}) %collective-permute-start.4) | collective-permute-done | bytes 524320 | tf_op jit(solution)/shard_map/ppermute | solution.py:38
  28.9 1.1 %far_outs.1 = (bf16[64,1792]{1,0:T(8,128)(2,1)S(1)}, bf16[64,1792]{1,0:T(8,128)(2,1)S(1)}) custom-call(bf16[2,512,1792]{2,1,0:T(8,128)(2,1)S(1)} %get-tuple-element.42.refs_1_.refs_0_, bf16[2,512,1792]{2,1,0:T(8,128)(2,1)S(1)} %get-tuple-element.46.refs_0_.refs_1_, bf16[128,2048]{1,0:T(8,128)(2,1)S(1)} %collective-permute-done.4.refs_2_.refs_0_.refs_4_, ...), custom_call_target="tpu_custom_call" | custom-call | flops 1000 | bytes 1000 | tf_op jit(solution)/shard_map/far_outs/pallas_call | solution.py:20
  30.0 1.8 %collective-permute-start.7 = (bf16[64,1792]{1,0:T(8,128)(2,1)S(1)}, bf16[64,1792]{1,0:T(8,128)(2,1)S(1)}, u32[]{:S(2)}, u32[]{:S(2)}) collective-permute-start(bf16[64,1792]{1,0:T(8,128)(2,1)S(1)} %get-tuple-element.52.refs_2_), channel_id=1, source_target_pairs={{0,8},{4,12},{8,0},{12,4},{1,9},{5,13},{9,1},{13,5},{2,10},{6,14},... | collective-permute-start | bytes 688136 | tf_op jit(solution)/shard_map/ppermute | solution.py:38
  31.9 2.7 %collective-permute-start.11 = (bf16[128,512]{1,0:T(8,128)(2,1)S(1)}, bf16[128,512]{1,0:T(8,128)(2,1)S(1)}, u32[]{:S(2)}, u32[]{:S(2)}) collective-permute-start(bf16[128,512]{1,0:T(8,128)(2,1)S(1)} %get-tuple-element.56.refs_1_), channel_id=1, source_target_pairs={{0,2},{1,3},{2,0},{3,1},{4,6},{5,7},{6,4},{7,5},{8,10},{9,11},{10,... | collective-permute-start | bytes 393224 | tf_op jit(solution)/shard_map/ppermute | solution.py:38
  34.6 1.6 %collective-permute-start.17 = (bf16[128,1024]{1,0:T(8,128)(2,1)S(1)}, bf16[128,1024]{1,0:T(8,128)(2,1)S(1)}, u32[]{:S(2)}, u32[]{:S(2)}) collective-permute-start(bf16[128,1024]{1,0:T(8,128)(2,1)S(1)} %cut_other.1.refs_5_), channel_id=1, source_target_pairs={{0,16},{16,0},{1,17},{17,1},{2,18},{18,2},{3,19},{19,3},{4,20},{20... | collective-permute-start | bytes 786440 | tf_op jit(solution)/shard_map/ppermute | solution.py:38
  36.2 2.1 %outer_near.1.refs_2_.refs_0_ = f32[1024,1792]{1,0:T(8,128)S(1)} custom-call(bf16[128,1792]{1,0:T(8,128)(2,1)S(1)} %get-tuple-element.40.refs_1_.refs_2_.refs_0_, bf16[128,2048]{1,0:T(8,128)(2,1)S(1)} %get-tuple-element.43.refs_3_.refs_1_, bf16[128,2816]{1,0:T(8,128)(2,1)S(1)} %collective-permute-done.10.refs_3_.refs_2_, ...), custom_call_target="tpu_custom_call" | custom-call | flops 1000 | bytes 1000 | tf_op jit(solution)/shard_map/outer_near/pallas_call | solution.py:20
  38.3 1.8 %collective-permute-done.11.refs_1_ = bf16[128,512]{1,0:T(8,128)(2,1)S(1)} collective-permute-done((bf16[128,512]{1,0:T(8,128)(2,1)S(1)}, bf16[128,512]{1,0:T(8,128)(2,1)S(1)}, u32[]{:S(2)}, u32[]{:S(2)}) %collective-permute-start.11) | collective-permute-done | bytes 131104 | tf_op jit(solution)/shard_map/ppermute | solution.py:38
  40.1 0.7 %collective-permute-start.15 = (bf16[64,512]{1,0:T(8,128)(2,1)S(1)}, bf16[64,512]{1,0:T(8,128)(2,1)S(1)}, u32[]{:S(2)}, u32[]{:S(2)}) collective-permute-start(bf16[64,512]{1,0:T(8,128)(2,1)S(1)} %get-tuple-element.58.refs_5_), channel_id=1, source_target_pairs={{0,8},{4,12},{8,0},{12,4},{1,9},{5,13},{9,1},{13,5},{2,10},{6,14},... | collective-permute-start | bytes 196616 | tf_op jit(solution)/shard_map/ppermute | solution.py:38
  40.8 1.3 %collective-permute-start.16 = (bf16[64,512]{1,0:T(8,128)(2,1)S(1)}, bf16[64,512]{1,0:T(8,128)(2,1)S(1)}, u32[]{:S(2)}, u32[]{:S(2)}) collective-permute-start(bf16[64,512]{1,0:T(8,128)(2,1)S(1)} %get-tuple-element.60), channel_id=1, source_target_pairs={{0,12},{4,8},{8,4},{12,0},{1,13},{5,9},{9,5},{13,1},{2,14},{6,10},... | collective-permute-start | bytes 196616 | tf_op jit(solution)/shard_map/ppermute | solution.py:38
  42.1 1.1 %collective-permute-done.8.refs_4_ = bf16[64,1792]{1,0:T(8,128)(2,1)S(1)} collective-permute-done((bf16[64,1792]{1,0:T(8,128)(2,1)S(1)}, bf16[64,1792]{1,0:T(8,128)(2,1)S(1)}, u32[]{:S(2)}, u32[]{:S(2)}) %collective-permute-start.8) | collective-permute-done | bytes 229408 | tf_op jit(solution)/shard_map/ppermute | solution.py:38
  43.2 1.1 %place.2 = (bf16[128,1792]{1,0:T(8,128)(2,1)}, f32[8,128]{1,0:T(8,128)S(1)}) custom-call(bf16[128,256]{1,0:T(8,128)(2,1)S(1)} %get-tuple-element.41.refs_0_, bf16[64,1792]{1,0:T(8,128)(2,1)S(1)} %get-tuple-element.44.refs_1_, bf16[64,1792]{1,0:T(8,128)(2,1)S(1)} %collective-permute-done.3.refs_4_.refs_2_, ...), custom_call_target="tpu_custom_call" | custom-call | flops 1000 | bytes 1000 | tf_op jit(solution)/shard_map/place/pallas_call | solution.py:20
  44.2 2.3 %outer_far.1 = (bf16[1,1024,1792]{2,1,0:T(8,128)(2,1)}, f32[8,128]{1,0:T(8,128)S(1)}) custom-call(f32[1024,1792]{1,0:T(8,128)S(1)} %outer_near.1.refs_2_.refs_0_, bf16[128,1792]{1,0:T(8,128)(2,1)S(1)} %collective-permute-done.13.refs_3_.refs_1_, bf16[128,1024]{1,0:T(8,128)(2,1)S(1)} %collective-permute-done.17.refs_2_, f32[8,128]{1,0:T(8,128)S(1)} %get-tuple-element.61.refs_3_), custom_call_target="tpu_custom_call" | custom-call | flops 1000 | bytes 1000 | tf_op jit(solution)/shard_map/outer_far/pallas_call | solution.py:20
  46.5 0.8 %place.3 = (bf16[128,512]{1,0:T(8,128)(2,1)}, f32[8,128]{1,0:T(8,128)}) custom-call(bf16[128,256]{1,0:T(8,128)(2,1)S(1)} %get-tuple-element.41.refs_0_, bf16[144,512]{1,0:T(8,128)(2,1)S(1)} %fold.6.refs_2_.refs_1_, bf16[144,512]{1,0:T(8,128)(2,1)S(1)} %collective-permute-done.14.refs_2_, bf16[64,512]{1,0:T(8,128)(2,1)S(1)} %collective-permute-done.15.refs_3_, ...), custom_call_target="tpu_custom_call" | custom-call | flops 1000 | bytes 1000 | tf_op jit(solution)/shard_map/place/pallas_call | solution.py:20
  (29 shorter events, 3.6 us)
Async XLA Ops:
  0.6 6.2 %collective-permute-start.2 = (bf16[128,2048]{1,0:T(8,128)(2,1)}, bf16[128,2048]{1,0:T(8,128)(2,1)S(1)}, u32[]{:S(2)}, u32[]{:S(2)}) collective-permute-start(bf16[128,2048]{1,0:T(8,128)(2,1)} %refs_3_.1), channel_id=1, source_target_pairs={{0,4},{4,0},{8,12},{12,8},{1,5},{5,1},{9,13},{13,9},{2,6},{6,2},{1... | collective-permute-start | bytes 1572872 | tf_op jit(solution)/shard_map/ppermute | solution.py:38
  1.1 2.4 %collective-permute-start.1 = (bf16[128,1792]{1,0:T(8,128)(2,1)}, bf16[128,1792]{1,0:T(8,128)(2,1)S(1)}, u32[]{:S(2)}, u32[]{:S(2)}) collective-permute-start(bf16[128,1792]{1,0:T(8,128)(2,1)} %refs_2_.1), channel_id=1, source_target_pairs={{0,4},{4,0},{8,12},{12,8},{1,5},{5,1},{9,13},{13,9},{2,6},{6,2},{1... | collective-permute-start | bytes 1376264 | tf_op jit(solution)/shard_map/ppermute | solution.py:38
  1.2 2.3 %collective-permute-start = (s32[1,128]{1,0:T(1,128)}, s32[1,128]{1,0:T(1,128)S(1)}, u32[]{:S(2)}, u32[]{:S(2)}) collective-permute-start(s32[1,128]{1,0:T(1,128)} %bitcast.1), channel_id=1, source_target_pairs={{0,4},{4,0},{8,12},{12,8},{1,5},{5,1},{9,13},{13,9},{2,6},{6,2},{1... | collective-permute-start | bytes 1544 | tf_op jit(solution)/shard_map/ppermute | solution.py:38
  3.9 14.2 %collective-permute-start.5 = (bf16[128,1792]{1,0:T(8,128)(2,1)S(1)}, bf16[128,1792]{1,0:T(8,128)(2,1)S(1)}, u32[]{:S(2)}, u32[]{:S(2)}) collective-permute-start(bf16[128,1792]{1,0:T(8,128)(2,1)S(1)} %get-tuple-element.48), channel_id=1, source_target_pairs={{0,8},{4,12},{8,0},{12,4},{1,9},{5,13},{9,1},{13,5},{2,10},{6,14},... | collective-permute-start | bytes 1376264 | tf_op jit(solution)/shard_map/ppermute | solution.py:38
  7.5 24.4 %collective-permute-start.10 = (bf16[128,2816]{1,0:T(8,128)(2,1)S(1)}, bf16[128,2816]{1,0:T(8,128)(2,1)S(1)}, u32[]{:S(2)}, u32[]{:S(2)}) collective-permute-start(bf16[128,2816]{1,0:T(8,128)(2,1)S(1)} %get-tuple-element.54), channel_id=1, source_target_pairs={{0,16},{16,0},{1,17},{17,1},{2,18},{18,2},{3,19},{19,3},{4,20},{20... | collective-permute-start | bytes 2162696 | tf_op jit(solution)/shard_map/ppermute | solution.py:38
  9.0 19.8 %collective-permute-start.4 = (bf16[128,2048]{1,0:T(8,128)(2,1)S(1)}, bf16[128,2048]{1,0:T(8,128)(2,1)S(1)}, u32[]{:S(2)}, u32[]{:S(2)}) collective-permute-start(bf16[128,2048]{1,0:T(8,128)(2,1)S(1)} %get-tuple-element.47), channel_id=1, source_target_pairs={{0,8},{4,12},{8,0},{12,4},{1,9},{5,13},{9,1},{13,5},{2,10},{6,14},... | collective-permute-start | bytes 1572872 | tf_op jit(solution)/shard_map/ppermute | solution.py:38
  12.6 9.1 %collective-permute-start.6 = (bf16[128,1024]{1,0:T(8,128)(2,1)S(1)}, bf16[128,1024]{1,0:T(8,128)(2,1)S(1)}, u32[]{:S(2)}, u32[]{:S(2)}) collective-permute-start(bf16[128,1024]{1,0:T(8,128)(2,1)S(1)} %get-tuple-element.50), channel_id=1, source_target_pairs={{0,1},{1,0},{2,3},{3,2},{4,5},{5,4},{6,7},{7,6},{8,9},{9,8},{10,11... | collective-permute-start | bytes 786440 | tf_op jit(solution)/shard_map/ppermute | solution.py:38
  17.9 5.4 %collective-permute-start.3 = (bf16[64,1792]{1,0:T(8,128)(2,1)S(1)}, bf16[64,1792]{1,0:T(8,128)(2,1)S(1)}, u32[]{:S(2)}, u32[]{:S(2)}) collective-permute-start(bf16[64,1792]{1,0:T(8,128)(2,1)S(1)} %get-tuple-element.45), channel_id=1, source_target_pairs={{0,4},{4,0},{8,12},{12,8},{1,5},{5,1},{9,13},{13,9},{2,6},{6,2},{1... | collective-permute-start | bytes 688136 | tf_op jit(solution)/shard_map/ppermute | solution.py:38
  19.4 12.4 %collective-permute-start.9 = (bf16[128,1024]{1,0:T(8,128)(2,1)S(1)}, bf16[128,1024]{1,0:T(8,128)(2,1)S(1)}, u32[]{:S(2)}, u32[]{:S(2)}) collective-permute-start(bf16[128,1024]{1,0:T(8,128)(2,1)S(1)} %far_grads.2.refs_2_), channel_id=1, source_target_pairs={{0,1},{1,0},{2,3},{3,2},{4,5},{5,4},{6,7},{7,6},{8,9},{9,8},{10,11... | collective-permute-start | bytes 786440 | tf_op jit(solution)/shard_map/ppermute | solution.py:38
  21.7 18.4 %collective-permute-start.13 = (bf16[128,1792]{1,0:T(8,128)(2,1)S(1)}, bf16[128,1792]{1,0:T(8,128)(2,1)S(1)}, u32[]{:S(2)}, u32[]{:S(2)}) collective-permute-start(bf16[128,1792]{1,0:T(8,128)(2,1)S(1)} %collective-permute-done.5.refs_1_.refs_3_), channel_id=1, source_target_pairs={{0,16},{16,0},{1,17},{17,1},{2,18},{18,2},{3,19},{19,3},{4,20},{20... | collective-permute-start | bytes 1376264 | tf_op jit(solution)/shard_map/ppermute | solution.py:38
  23.2 12.9 %collective-permute-start.12 = (bf16[128,512]{1,0:T(8,128)(2,1)S(1)}, bf16[128,512]{1,0:T(8,128)(2,1)S(1)}, u32[]{:S(2)}, u32[]{:S(2)}) collective-permute-start(bf16[128,512]{1,0:T(8,128)(2,1)S(1)} %get-tuple-element.51.refs_2_), channel_id=1, source_target_pairs={{0,2},{1,3},{2,0},{3,1},{4,6},{5,7},{6,4},{7,5},{8,10},{9,11},{10,... | collective-permute-start | bytes 393224 | tf_op jit(solution)/shard_map/ppermute | solution.py:38
  30.0 10.8 %collective-permute-start.7 = (bf16[64,1792]{1,0:T(8,128)(2,1)S(1)}, bf16[64,1792]{1,0:T(8,128)(2,1)S(1)}, u32[]{:S(2)}, u32[]{:S(2)}) collective-permute-start(bf16[64,1792]{1,0:T(8,128)(2,1)S(1)} %get-tuple-element.52.refs_2_), channel_id=1, source_target_pairs={{0,8},{4,12},{8,0},{12,4},{1,9},{5,13},{9,1},{13,5},{2,10},{6,14},... | collective-permute-start | bytes 688136 | tf_op jit(solution)/shard_map/ppermute | solution.py:38
  31.9 8.2 %collective-permute-start.11 = (bf16[128,512]{1,0:T(8,128)(2,1)S(1)}, bf16[128,512]{1,0:T(8,128)(2,1)S(1)}, u32[]{:S(2)}, u32[]{:S(2)}) collective-permute-start(bf16[128,512]{1,0:T(8,128)(2,1)S(1)} %get-tuple-element.56.refs_1_), channel_id=1, source_target_pairs={{0,2},{1,3},{2,0},{3,1},{4,6},{5,7},{6,4},{7,5},{8,10},{9,11},{10,... | collective-permute-start | bytes 393224 | tf_op jit(solution)/shard_map/ppermute | solution.py:38
  34.6 9.6 %collective-permute-start.17 = (bf16[128,1024]{1,0:T(8,128)(2,1)S(1)}, bf16[128,1024]{1,0:T(8,128)(2,1)S(1)}, u32[]{:S(2)}, u32[]{:S(2)}) collective-permute-start(bf16[128,1024]{1,0:T(8,128)(2,1)S(1)} %cut_other.1.refs_5_), channel_id=1, source_target_pairs={{0,16},{16,0},{1,17},{17,1},{2,18},{18,2},{3,19},{19,3},{4,20},{20... | collective-permute-start | bytes 786440 | tf_op jit(solution)/shard_map/ppermute | solution.py:38
  36.2 7.0 %collective-permute-start.8 = (bf16[64,1792]{1,0:T(8,128)(2,1)S(1)}, bf16[64,1792]{1,0:T(8,128)(2,1)S(1)}, u32[]{:S(2)}, u32[]{:S(2)}) collective-permute-start(bf16[64,1792]{1,0:T(8,128)(2,1)S(1)} %get-tuple-element.53), channel_id=1, source_target_pairs={{0,12},{4,8},{8,4},{12,0},{1,13},{5,9},{9,5},{13,1},{2,14},{6,10},... | collective-permute-start | bytes 688136 | tf_op jit(solution)/shard_map/ppermute | solution.py:38
  40.1 6.4 %collective-permute-start.14 = (bf16[144,512]{1,0:T(8,128)(2,1)S(1)}, bf16[144,512]{1,0:T(8,128)(2,1)S(1)}, u32[]{:S(2)}, u32[]{:S(2)}) collective-permute-start(bf16[144,512]{1,0:T(8,128)(2,1)S(1)} %fold.6.refs_2_.refs_1_), channel_id=1, source_target_pairs={{0,4},{4,0},{8,12},{12,8},{1,5},{5,1},{9,13},{13,9},{2,6},{6,2},{1... | collective-permute-start | bytes 442376 | tf_op jit(solution)/shard_map/ppermute | solution.py:38
  40.1 6.4 %collective-permute-start.15 = (bf16[64,512]{1,0:T(8,128)(2,1)S(1)}, bf16[64,512]{1,0:T(8,128)(2,1)S(1)}, u32[]{:S(2)}, u32[]{:S(2)}) collective-permute-start(bf16[64,512]{1,0:T(8,128)(2,1)S(1)} %get-tuple-element.58.refs_5_), channel_id=1, source_target_pairs={{0,8},{4,12},{8,0},{12,4},{1,9},{5,13},{9,1},{13,5},{2,10},{6,14},... | collective-permute-start | bytes 196616 | tf_op jit(solution)/shard_map/ppermute | solution.py:38
  40.8 5.7 %collective-permute-start.16 = (bf16[64,512]{1,0:T(8,128)(2,1)S(1)}, bf16[64,512]{1,0:T(8,128)(2,1)S(1)}, u32[]{:S(2)}, u32[]{:S(2)}) collective-permute-start(bf16[64,512]{1,0:T(8,128)(2,1)S(1)} %get-tuple-element.60), channel_id=1, source_target_pairs={{0,12},{4,8},{8,4},{12,0},{1,13},{5,9},{9,5},{13,1},{2,14},{6,10},... | collective-permute-start | bytes 196616 | tf_op jit(solution)/shard_map/ppermute | solution.py:38

commit v7 on v6

--- a/solution.py
+++ b/solution.py
@@ -204,12 +204,19 @@
 
 
 def place(cap, slot, *refs):
-    *rows, out, token = refs
+    *rows, out, token, held, sem = refs
     rows = [ref[...] if ref.shape[0] == cap else ref[i % 2 * cap : (i % 2 + 1) * cap] for i, ref in enumerate(rows)]
-    out[...] = jnp.dot(
-        slot[...], jnp.concatenate(rows, axis=0), preferred_element_type=jnp.float32
-    ).astype(out.dtype)
+    rows = jnp.concatenate(rows, axis=0)
+    pieces, _, size = held.shape
+    copies = []
+    for i in range(pieces):
+        part = slice(i * size, (i + 1) * size)
+        held[i] = jnp.dot(slot[...], rows[:, part], preferred_element_type=jnp.float32).astype(held.dtype)
+        copies.append(pltpu.make_async_copy(held.at[i], out.at[:, pl.ds(i * size, size)], sem.at[i]))
+        copies[i].start()
     token[...] = jnp.zeros_like(token)
+    for copy in copies:
+        copy.wait()
 
 
 def outer_near(grads, hids, both, far_grads, far_hids, out):
@@ -321,7 +328,10 @@
         functools.partial(place, cap),
         [((tok, cols), bf), token],
         (placer, near_out, next_out, back[1], back[0]),
+        None,
+        [pltpu.VMEM((2, tok, cols // 2), bf), pltpu.SemaphoreType.DMA((2,))],
         after=(far_back[0],),
+        out_specs=[ANY, VMEM],
     )
     pieces = 8
     d_weight, last = call(
@@ -343,7 +353,10 @@
             swap(far_back[0], "expert", 2),
             swap(far_back[1], "expert", 3),
         ),
+        None,
+        [pltpu.VMEM((2, tok, column // 2), bf), pltpu.SemaphoreType.DMA((2,))],
         after=(last,),
+        out_specs=[ANY, VMEM],
     )
     return output, d_hidden, d_weight
 

time: 47.5 us -> 48.1 us (1.013)
  Pallas kernels: 19 us -> 19.6 us
    pallas_call x17, Pallas kernels: 19 us -> 19.6 us  [call(): pl.pallas_call(late, out_shape=tuple((jax.ShapeDtypeStruct(s, d) for s, d...]
where the time goes in v7:
time: 48.1 us; the launch traced here: 47.9 us
  starting transfers between devices  22.2 us (46%)
  Pallas kernels  19.6 us (41%)
  waiting for transfers between devices  5.37 us (11%)
  between operations  0.8 us (2%)
    ppermute x18, starting transfers between devices, swap(): return lax.ppermute(value, axis, [(i, i ^ offset) for i in range(size)])  22.2 us
    pallas_call x17, Pallas kernels, call(): pl.pallas_call(late, out_shape=tuple((jax.ShapeDtypeStruct(s, d) for s, d...  19.6 us
    ppermute x18, waiting for transfers between devices, swap(): return lax.ppermute(value, axis, [(i, i ^ offset) for i in range(size)])  5.37 us
  transfers between devices with their start and end apart: 18, of which 5 were waited for; matrix products, arithmetic and copies ran while one was open for 0% of the time, Pallas kernels for 38%

profile of v7, /device:TPU:0, one launch (start us, length us, event | category | flops | bytes accessed | tf_op | source)
XLA Modules:
  0.0 47.9 jit_solution(6026975373623316133)
XLA Ops:
  1.7 1.3 %pick_own.1 = (bf16[256,128]{1,0:T(8,128)(2,1)S(1)}, s32[8,128]{1,0:T(8,128)S(1)}, bf16[128,1792]{1,0:T(8,128)(2,1)S(1)}, bf16[128,2048]{1,0:T(8,128)(2,1)S(1)}, bf16[64,1792]{1,0:T(8,128)(2,1)S(1)}) custom-call(s32[1,128]{1,0:T(1,128)} %bitcast.2, s32[4]{0:T(128)} %refs_1_.1, bf16[128,1792]{1,0:T(8,128)(2,1)} %refs_2_.1, bf16[128,2048]{1,0:T(8,128)(2,1)} %refs_3_.1), custom_call_target="tpu_custom_call" | custom-call | flops 1000 | bytes 1000 | tf_op jit(solution)/shard_map/pick_own/pallas_call | solution.py:20
  3.9 2.9 %collective-permute-start.5 = (bf16[128,1792]{1,0:T(8,128)(2,1)S(1)}, bf16[128,1792]{1,0:T(8,128)(2,1)S(1)}, u32[]{:S(2)}, u32[]{:S(2)}) collective-permute-start(bf16[128,1792]{1,0:T(8,128)(2,1)S(1)} %get-tuple-element.48), channel_id=1, source_target_pairs={{0,8},{4,12},{8,0},{12,4},{1,9},{5,13},{9,1},{13,5},{2,10},{6,14},... | collective-permute-start | bytes 1376264 | tf_op jit(solution)/shard_map/ppermute | solution.py:38
  7.5 1.6 %collective-permute-start.10 = (bf16[128,2816]{1,0:T(8,128)(2,1)S(1)}, bf16[128,2816]{1,0:T(8,128)(2,1)S(1)}, u32[]{:S(2)}, u32[]{:S(2)}) collective-permute-start(bf16[128,2816]{1,0:T(8,128)(2,1)S(1)} %get-tuple-element.54), channel_id=1, source_target_pairs={{0,16},{16,0},{1,17},{17,1},{2,18},{18,2},{3,19},{19,3},{4,20},{20... | collective-permute-start | bytes 2162696 | tf_op jit(solution)/shard_map/ppermute | solution.py:38
  9.6 3.0 %near_odd.1 = (bf16[2,512,1792]{2,1,0:T(8,128)(2,1)S(1)}, bf16[128,1024]{1,0:T(8,128)(2,1)S(1)}, bf16[128,256]{1,0:T(8,128)(2,1)S(1)}) custom-call(bf16[1,2048,1792]{2,1,0:T(8,128)(2,1)} %refs_0_.3, bf16[128,1792]{1,0:T(8,128)(2,1)S(1)} %get-tuple-element.40.refs_1_.refs_2_.refs_0_, bf16[256,128]{1,0:T(8,128)(2,1)S(1)} %get-tuple-element.34.refs_0_.refs_2_), custom_call_target="tpu_custom_call" | custom-call | flops 1000 | bytes 1000 | tf_op jit(solution)/shard_map/near_odd/pallas_call | solution.py:20
  12.6 1.7 %collective-permute-start.6 = (bf16[128,1024]{1,0:T(8,128)(2,1)S(1)}, bf16[128,1024]{1,0:T(8,128)(2,1)S(1)}, u32[]{:S(2)}, u32[]{:S(2)}) collective-permute-start(bf16[128,1024]{1,0:T(8,128)(2,1)S(1)} %get-tuple-element.50), channel_id=1, source_target_pairs={{0,1},{1,0},{2,3},{3,2},{4,5},{5,4},{6,7},{7,6},{8,9},{9,8},{10,11... | collective-permute-start | bytes 786440 | tf_op jit(solution)/shard_map/ppermute | solution.py:38
  14.2 3.7 %near_even.1 = (bf16[2,512,1792]{2,1,0:T(8,128)(2,1)S(1)}, f32[128,1024]{1,0:T(8,128)S(1)}, bf16[64,1792]{1,0:T(8,128)(2,1)S(1)}, bf16[64,1792]{1,0:T(8,128)(2,1)S(1)}) custom-call(bf16[1,2048,1792]{2,1,0:T(8,128)(2,1)} %refs_0_.3, bf16[2,512,1792]{2,1,0:T(8,128)(2,1)S(1)} %get-tuple-element.42.refs_1_.refs_0_, ...), custom_call_target="tpu_custom_call" | custom-call | flops 1000 | bytes 1000 | tf_op jit(solution)/shard_map/near_even/pallas_call | solution.py:20
  18.1 1.3 %far_grads.2.refs_2_ = bf16[128,1024]{1,0:T(8,128)(2,1)S(1)} custom-call(bf16[2,512,1792]{2,1,0:T(8,128)(2,1)S(1)} %get-tuple-element.42.refs_1_.refs_0_, bf16[128,1792]{1,0:T(8,128)(2,1)S(1)} %collective-permute-done.5.refs_1_.refs_3_, f32[128,1024]{1,0:T(8,128)S(1)} %get-tuple-element.49.refs_2_.refs_0_), custom_call_target="tpu_custom_call" | custom-call | flops 1000 | bytes 1000 | tf_op jit(solution)/shard_map/far_grads/pallas_call | solution.py:20
  19.4 2.2 %collective-permute-start.9 = (bf16[128,1024]{1,0:T(8,128)(2,1)S(1)}, bf16[128,1024]{1,0:T(8,128)(2,1)S(1)}, u32[]{:S(2)}, u32[]{:S(2)}) collective-permute-start(bf16[128,1024]{1,0:T(8,128)(2,1)S(1)} %far_grads.2.refs_2_), channel_id=1, source_target_pairs={{0,1},{1,0},{2,3},{3,2},{4,5},{5,4},{6,7},{7,6},{8,9},{9,8},{10,11... | collective-permute-start | bytes 786440 | tf_op jit(solution)/shard_map/ppermute | solution.py:38
  21.7 1.5 %collective-permute-start.13 = (bf16[128,1792]{1,0:T(8,128)(2,1)S(1)}, bf16[128,1792]{1,0:T(8,128)(2,1)S(1)}, u32[]{:S(2)}, u32[]{:S(2)}) collective-permute-start(bf16[128,1792]{1,0:T(8,128)(2,1)S(1)} %collective-permute-done.5.refs_1_.refs_3_), channel_id=1, source_target_pairs={{0,16},{16,0},{1,17},{17,1},{2,18},{18,2},{3,19},{19,3},{4,20},{20... | collective-permute-start | bytes 1376264 | tf_op jit(solution)/shard_map/ppermute | solution.py:38
  23.2 2.7 %collective-permute-start.12 = (bf16[128,512]{1,0:T(8,128)(2,1)S(1)}, bf16[128,512]{1,0:T(8,128)(2,1)S(1)}, u32[]{:S(2)}, u32[]{:S(2)}) collective-permute-start(bf16[128,512]{1,0:T(8,128)(2,1)S(1)} %get-tuple-element.51.refs_2_), channel_id=1, source_target_pairs={{0,2},{1,3},{2,0},{3,1},{4,6},{5,7},{6,4},{7,5},{8,10},{9,11},{10,... | collective-permute-start | bytes 393224 | tf_op jit(solution)/shard_map/ppermute | solution.py:38
  25.9 1.3 %far_grads.3.refs_3_.refs_0_ = f32[128,1024]{1,0:T(8,128)S(1)} custom-call(bf16[2,512,1792]{2,1,0:T(8,128)(2,1)S(1)} %get-tuple-element.46.refs_0_.refs_1_, bf16[128,1792]{1,0:T(8,128)(2,1)S(1)} %collective-permute-done.5.refs_1_.refs_3_, bf16[128,512]{1,0:T(8,128)(2,1)S(1)} %get-tuple-element.51.refs_2_), custom_call_target="tpu_custom_call" | custom-call | flops 1000 | bytes 1000 | tf_op jit(solution)/shard_map/far_grads/pallas_call | solution.py:20
  27.2 1.7 %collective-permute-done.4.refs_2_.refs_0_.refs_4_ = bf16[128,2048]{1,0:T(8,128)(2,1)S(1)} collective-permute-done((bf16[128,2048]{1,0:T(8,128)(2,1)S(1)}, bf16[128,2048]{1,0:T(8,128)(2,1)S(1)}, u32[]{:S(2)}, u32[]{:S(2)}) %collective-permute-start.4) | collective-permute-done | bytes 524320 | tf_op jit(solution)/shard_map/ppermute | solution.py:38
  28.9 1.1 %far_outs.1 = (bf16[64,1792]{1,0:T(8,128)(2,1)S(1)}, bf16[64,1792]{1,0:T(8,128)(2,1)S(1)}) custom-call(bf16[2,512,1792]{2,1,0:T(8,128)(2,1)S(1)} %get-tuple-element.42.refs_1_.refs_0_, bf16[2,512,1792]{2,1,0:T(8,128)(2,1)S(1)} %get-tuple-element.46.refs_0_.refs_1_, bf16[128,2048]{1,0:T(8,128)(2,1)S(1)} %collective-permute-done.4.refs_2_.refs_0_.refs_4_, ...), custom_call_target="tpu_custom_call" | custom-call | flops 1000 | bytes 1000 | tf_op jit(solution)/shard_map/far_outs/pallas_call | solution.py:20
  30.0 1.8 %collective-permute-start.7 = (bf16[64,1792]{1,0:T(8,128)(2,1)S(1)}, bf16[64,1792]{1,0:T(8,128)(2,1)S(1)}, u32[]{:S(2)}, u32[]{:S(2)}) collective-permute-start(bf16[64,1792]{1,0:T(8,128)(2,1)S(1)} %get-tuple-element.52.refs_2_), channel_id=1, source_target_pairs={{0,8},{4,12},{8,0},{12,4},{1,9},{5,13},{9,1},{13,5},{2,10},{6,14},... | collective-permute-start | bytes 688136 | tf_op jit(solution)/shard_map/ppermute | solution.py:38
  31.9 2.7 %collective-permute-start.11 = (bf16[128,512]{1,0:T(8,128)(2,1)S(1)}, bf16[128,512]{1,0:T(8,128)(2,1)S(1)}, u32[]{:S(2)}, u32[]{:S(2)}) collective-permute-start(bf16[128,512]{1,0:T(8,128)(2,1)S(1)} %get-tuple-element.56.refs_1_), channel_id=1, source_target_pairs={{0,2},{1,3},{2,0},{3,1},{4,6},{5,7},{6,4},{7,5},{8,10},{9,11},{10,... | collective-permute-start | bytes 393224 | tf_op jit(solution)/shard_map/ppermute | solution.py:38
  34.6 1.6 %collective-permute-start.17 = (bf16[128,1024]{1,0:T(8,128)(2,1)S(1)}, bf16[128,1024]{1,0:T(8,128)(2,1)S(1)}, u32[]{:S(2)}, u32[]{:S(2)}) collective-permute-start(bf16[128,1024]{1,0:T(8,128)(2,1)S(1)} %cut_other.1.refs_5_), channel_id=1, source_target_pairs={{0,16},{16,0},{1,17},{17,1},{2,18},{18,2},{3,19},{19,3},{4,20},{20... | collective-permute-start | bytes 786440 | tf_op jit(solution)/shard_map/ppermute | solution.py:38
  36.2 2.1 %outer_near.1.refs_2_.refs_0_ = f32[1024,1792]{1,0:T(8,128)S(1)} custom-call(bf16[128,1792]{1,0:T(8,128)(2,1)S(1)} %get-tuple-element.40.refs_1_.refs_2_.refs_0_, bf16[128,2048]{1,0:T(8,128)(2,1)S(1)} %get-tuple-element.43.refs_3_.refs_1_, bf16[128,2816]{1,0:T(8,128)(2,1)S(1)} %collective-permute-done.10.refs_3_.refs_2_, ...), custom_call_target="tpu_custom_call" | custom-call | flops 1000 | bytes 1000 | tf_op jit(solution)/shard_map/outer_near/pallas_call | solution.py:20
  38.3 1.8 %collective-permute-done.11.refs_1_ = bf16[128,512]{1,0:T(8,128)(2,1)S(1)} collective-permute-done((bf16[128,512]{1,0:T(8,128)(2,1)S(1)}, bf16[128,512]{1,0:T(8,128)(2,1)S(1)}, u32[]{:S(2)}, u32[]{:S(2)}) %collective-permute-start.11) | collective-permute-done | bytes 131104 | tf_op jit(solution)/shard_map/ppermute | solution.py:38
  40.1 0.7 %collective-permute-start.15 = (bf16[64,512]{1,0:T(8,128)(2,1)S(1)}, bf16[64,512]{1,0:T(8,128)(2,1)S(1)}, u32[]{:S(2)}, u32[]{:S(2)}) collective-permute-start(bf16[64,512]{1,0:T(8,128)(2,1)S(1)} %get-tuple-element.58.refs_5_), channel_id=1, source_target_pairs={{0,8},{4,12},{8,0},{12,4},{1,9},{5,13},{9,1},{13,5},{2,10},{6,14},... | collective-permute-start | bytes 196616 | tf_op jit(solution)/shard_map/ppermute | solution.py:38
  40.8 1.3 %collective-permute-start.16 = (bf16[64,512]{1,0:T(8,128)(2,1)S(1)}, bf16[64,512]{1,0:T(8,128)(2,1)S(1)}, u32[]{:S(2)}, u32[]{:S(2)}) collective-permute-start(bf16[64,512]{1,0:T(8,128)(2,1)S(1)} %get-tuple-element.60), channel_id=1, source_target_pairs={{0,12},{4,8},{8,4},{12,0},{1,13},{5,9},{9,5},{13,1},{2,14},{6,10},... | collective-permute-start | bytes 196616 | tf_op jit(solution)/shard_map/ppermute | solution.py:38
  42.1 1.1 %collective-permute-done.8.refs_4_ = bf16[64,1792]{1,0:T(8,128)(2,1)S(1)} collective-permute-done((bf16[64,1792]{1,0:T(8,128)(2,1)S(1)}, bf16[64,1792]{1,0:T(8,128)(2,1)S(1)}, u32[]{:S(2)}, u32[]{:S(2)}) %collective-permute-start.8) | collective-permute-done | bytes 229408 | tf_op jit(solution)/shard_map/ppermute | solution.py:38
  43.2 1.0 %place.2 = (bf16[128,1792]{1,0:T(8,128)(2,1)}, f32[8,128]{1,0:T(8,128)S(1)}) custom-call(bf16[128,256]{1,0:T(8,128)(2,1)S(1)} %get-tuple-element.41.refs_0_, bf16[64,1792]{1,0:T(8,128)(2,1)S(1)} %get-tuple-element.44.refs_1_, bf16[64,1792]{1,0:T(8,128)(2,1)S(1)} %collective-permute-done.3.refs_4_.refs_2_, ...), custom_call_target="tpu_custom_call" | custom-call | flops 1000 | bytes 1000 | tf_op jit(solution)/shard_map/place/pallas_call | solution.py:20
  44.2 2.3 %outer_far.1 = (bf16[1,1024,1792]{2,1,0:T(8,128)(2,1)}, f32[8,128]{1,0:T(8,128)S(1)}) custom-call(f32[1024,1792]{1,0:T(8,128)S(1)} %outer_near.1.refs_2_.refs_0_, bf16[128,1792]{1,0:T(8,128)(2,1)S(1)} %collective-permute-done.13.refs_3_.refs_1_, bf16[128,1024]{1,0:T(8,128)(2,1)S(1)} %collective-permute-done.17.refs_2_, f32[8,128]{1,0:T(8,128)S(1)} %get-tuple-element.61.refs_3_), custom_call_target="tpu_custom_call" | custom-call | flops 1000 | bytes 1000 | tf_op jit(solution)/shard_map/outer_far/pallas_call | solution.py:20
  46.5 1.5 %place.3 = (bf16[128,512]{1,0:T(8,128)(2,1)}, f32[8,128]{1,0:T(8,128)}) custom-call(bf16[128,256]{1,0:T(8,128)(2,1)S(1)} %get-tuple-element.41.refs_0_, bf16[144,512]{1,0:T(8,128)(2,1)S(1)} %fold.6.refs_2_.refs_1_, bf16[144,512]{1,0:T(8,128)(2,1)S(1)} %collective-permute-done.14.refs_2_, bf16[64,512]{1,0:T(8,128)(2,1)S(1)} %collective-permute-done.15.refs_3_, ...), custom_call_target="tpu_custom_call" | custom-call | flops 1000 | bytes 1000 | tf_op jit(solution)/shard_map/place/pallas_call | solution.py:20
  (29 shorter events, 3.6 us)
Async XLA Ops:
  0.6 6.2 %collective-permute-start.2 = (bf16[128,2048]{1,0:T(8,128)(2,1)}, bf16[128,2048]{1,0:T(8,128)(2,1)S(1)}, u32[]{:S(2)}, u32[]{:S(2)}) collective-permute-start(bf16[128,2048]{1,0:T(8,128)(2,1)} %refs_3_.1), channel_id=1, source_target_pairs={{0,4},{4,0},{8,12},{12,8},{1,5},{5,1},{9,13},{13,9},{2,6},{6,2},{1... | collective-permute-start | bytes 1572872 | tf_op jit(solution)/shard_map/ppermute | solution.py:38
  1.1 2.4 %collective-permute-start.1 = (bf16[128,1792]{1,0:T(8,128)(2,1)}, bf16[128,1792]{1,0:T(8,128)(2,1)S(1)}, u32[]{:S(2)}, u32[]{:S(2)}) collective-permute-start(bf16[128,1792]{1,0:T(8,128)(2,1)} %refs_2_.1), channel_id=1, source_target_pairs={{0,4},{4,0},{8,12},{12,8},{1,5},{5,1},{9,13},{13,9},{2,6},{6,2},{1... | collective-permute-start | bytes 1376264 | tf_op jit(solution)/shard_map/ppermute | solution.py:38
  1.2 2.3 %collective-permute-start = (s32[1,128]{1,0:T(1,128)}, s32[1,128]{1,0:T(1,128)S(1)}, u32[]{:S(2)}, u32[]{:S(2)}) collective-permute-start(s32[1,128]{1,0:T(1,128)} %bitcast.1), channel_id=1, source_target_pairs={{0,4},{4,0},{8,12},{12,8},{1,5},{5,1},{9,13},{13,9},{2,6},{6,2},{1... | collective-permute-start | bytes 1544 | tf_op jit(solution)/shard_map/ppermute | solution.py:38
  3.9 14.2 %collective-permute-start.5 = (bf16[128,1792]{1,0:T(8,128)(2,1)S(1)}, bf16[128,1792]{1,0:T(8,128)(2,1)S(1)}, u32[]{:S(2)}, u32[]{:S(2)}) collective-permute-start(bf16[128,1792]{1,0:T(8,128)(2,1)S(1)} %get-tuple-element.48), channel_id=1, source_target_pairs={{0,8},{4,12},{8,0},{12,4},{1,9},{5,13},{9,1},{13,5},{2,10},{6,14},... | collective-permute-start | bytes 1376264 | tf_op jit(solution)/shard_map/ppermute | solution.py:38
  7.5 24.4 %collective-permute-start.10 = (bf16[128,2816]{1,0:T(8,128)(2,1)S(1)}, bf16[128,2816]{1,0:T(8,128)(2,1)S(1)}, u32[]{:S(2)}, u32[]{:S(2)}) collective-permute-start(bf16[128,2816]{1,0:T(8,128)(2,1)S(1)} %get-tuple-element.54), channel_id=1, source_target_pairs={{0,16},{16,0},{1,17},{17,1},{2,18},{18,2},{3,19},{19,3},{4,20},{20... | collective-permute-start | bytes 2162696 | tf_op jit(solution)/shard_map/ppermute | solution.py:38
  9.0 19.8 %collective-permute-start.4 = (bf16[128,2048]{1,0:T(8,128)(2,1)S(1)}, bf16[128,2048]{1,0:T(8,128)(2,1)S(1)}, u32[]{:S(2)}, u32[]{:S(2)}) collective-permute-start(bf16[128,2048]{1,0:T(8,128)(2,1)S(1)} %get-tuple-element.47), channel_id=1, source_target_pairs={{0,8},{4,12},{8,0},{12,4},{1,9},{5,13},{9,1},{13,5},{2,10},{6,14},... | collective-permute-start | bytes 1572872 | tf_op jit(solution)/shard_map/ppermute | solution.py:38
  12.6 9.1 %collective-permute-start.6 = (bf16[128,1024]{1,0:T(8,128)(2,1)S(1)}, bf16[128,1024]{1,0:T(8,128)(2,1)S(1)}, u32[]{:S(2)}, u32[]{:S(2)}) collective-permute-start(bf16[128,1024]{1,0:T(8,128)(2,1)S(1)} %get-tuple-element.50), channel_id=1, source_target_pairs={{0,1},{1,0},{2,3},{3,2},{4,5},{5,4},{6,7},{7,6},{8,9},{9,8},{10,11... | collective-permute-start | bytes 786440 | tf_op jit(solution)/shard_map/ppermute | solution.py:38
  17.9 5.4 %collective-permute-start.3 = (bf16[64,1792]{1,0:T(8,128)(2,1)S(1)}, bf16[64,1792]{1,0:T(8,128)(2,1)S(1)}, u32[]{:S(2)}, u32[]{:S(2)}) collective-permute-start(bf16[64,1792]{1,0:T(8,128)(2,1)S(1)} %get-tuple-element.45), channel_id=1, source_target_pairs={{0,4},{4,0},{8,12},{12,8},{1,5},{5,1},{9,13},{13,9},{2,6},{6,2},{1... | collective-permute-start | bytes 688136 | tf_op jit(solution)/shard_map/ppermute | solution.py:38
  19.4 12.4 %collective-permute-start.9 = (bf16[128,1024]{1,0:T(8,128)(2,1)S(1)}, bf16[128,1024]{1,0:T(8,128)(2,1)S(1)}, u32[]{:S(2)}, u32[]{:S(2)}) collective-permute-start(bf16[128,1024]{1,0:T(8,128)(2,1)S(1)} %far_grads.2.refs_2_), channel_id=1, source_target_pairs={{0,1},{1,0},{2,3},{3,2},{4,5},{5,4},{6,7},{7,6},{8,9},{9,8},{10,11... | collective-permute-start | bytes 786440 | tf_op jit(solution)/shard_map/ppermute | solution.py:38
  21.7 18.4 %collective-permute-start.13 = (bf16[128,1792]{1,0:T(8,128)(2,1)S(1)}, bf16[128,1792]{1,0:T(8,128)(2,1)S(1)}, u32[]{:S(2)}, u32[]{:S(2)}) collective-permute-start(bf16[128,1792]{1,0:T(8,128)(2,1)S(1)} %collective-permute-done.5.refs_1_.refs_3_), channel_id=1, source_target_pairs={{0,16},{16,0},{1,17},{17,1},{2,18},{18,2},{3,19},{19,3},{4,20},{20... | collective-permute-start | bytes 1376264 | tf_op jit(solution)/shard_map/ppermute | solution.py:38
  23.2 12.9 %collective-permute-start.12 = (bf16[128,512]{1,0:T(8,128)(2,1)S(1)}, bf16[128,512]{1,0:T(8,128)(2,1)S(1)}, u32[]{:S(2)}, u32[]{:S(2)}) collective-permute-start(bf16[128,512]{1,0:T(8,128)(2,1)S(1)} %get-tuple-element.51.refs_2_), channel_id=1, source_target_pairs={{0,2},{1,3},{2,0},{3,1},{4,6},{5,7},{6,4},{7,5},{8,10},{9,11},{10,... | collective-permute-start | bytes 393224 | tf_op jit(solution)/shard_map/ppermute | solution.py:38
  30.0 10.8 %collective-permute-start.7 = (bf16[64,1792]{1,0:T(8,128)(2,1)S(1)}, bf16[64,1792]{1,0:T(8,128)(2,1)S(1)}, u32[]{:S(2)}, u32[]{:S(2)}) collective-permute-start(bf16[64,1792]{1,0:T(8,128)(2,1)S(1)} %get-tuple-element.52.refs_2_), channel_id=1, source_target_pairs={{0,8},{4,12},{8,0},{12,4},{1,9},{5,13},{9,1},{13,5},{2,10},{6,14},... | collective-permute-start | bytes 688136 | tf_op jit(solution)/shard_map/ppermute | solution.py:38
  31.9 8.2 %collective-permute-start.11 = (bf16[128,512]{1,0:T(8,128)(2,1)S(1)}, bf16[128,512]{1,0:T(8,128)(2,1)S(1)}, u32[]{:S(2)}, u32[]{:S(2)}) collective-permute-start(bf16[128,512]{1,0:T(8,128)(2,1)S(1)} %get-tuple-element.56.refs_1_), channel_id=1, source_target_pairs={{0,2},{1,3},{2,0},{3,1},{4,6},{5,7},{6,4},{7,5},{8,10},{9,11},{10,... | collective-permute-start | bytes 393224 | tf_op jit(solution)/shard_map/ppermute | solution.py:38
  34.6 9.6 %collective-permute-start.17 = (bf16[128,1024]{1,0:T(8,128)(2,1)S(1)}, bf16[128,1024]{1,0:T(8,128)(2,1)S(1)}, u32[]{:S(2)}, u32[]{:S(2)}) collective-permute-start(bf16[128,1024]{1,0:T(8,128)(2,1)S(1)} %cut_other.1.refs_5_), channel_id=1, source_target_pairs={{0,16},{16,0},{1,17},{17,1},{2,18},{18,2},{3,19},{19,3},{4,20},{20... | collective-permute-start | bytes 786440 | tf_op jit(solution)/shard_map/ppermute | solution.py:38
  36.2 7.0 %collective-permute-start.8 = (bf16[64,1792]{1,0:T(8,128)(2,1)S(1)}, bf16[64,1792]{1,0:T(8,128)(2,1)S(1)}, u32[]{:S(2)}, u32[]{:S(2)}) collective-permute-start(bf16[64,1792]{1,0:T(8,128)(2,1)S(1)} %get-tuple-element.53), channel_id=1, source_target_pairs={{0,12},{4,8},{8,4},{12,0},{1,13},{5,9},{9,5},{13,1},{2,14},{6,10},... | collective-permute-start | bytes 688136 | tf_op jit(solution)/shard_map/ppermute | solution.py:38
  40.1 6.4 %collective-permute-start.14 = (bf16[144,512]{1,0:T(8,128)(2,1)S(1)}, bf16[144,512]{1,0:T(8,128)(2,1)S(1)}, u32[]{:S(2)}, u32[]{:S(2)}) collective-permute-start(bf16[144,512]{1,0:T(8,128)(2,1)S(1)} %fold.6.refs_2_.refs_1_), channel_id=1, source_target_pairs={{0,4},{4,0},{8,12},{12,8},{1,5},{5,1},{9,13},{13,9},{2,6},{6,2},{1... | collective-permute-start | bytes 442376 | tf_op jit(solution)/shard_map/ppermute | solution.py:38
  40.1 6.3 %collective-permute-start.15 = (bf16[64,512]{1,0:T(8,128)(2,1)S(1)}, bf16[64,512]{1,0:T(8,128)(2,1)S(1)}, u32[]{:S(2)}, u32[]{:S(2)}) collective-permute-start(bf16[64,512]{1,0:T(8,128)(2,1)S(1)} %get-tuple-element.58.refs_5_), channel_id=1, source_target_pairs={{0,8},{4,12},{8,0},{12,4},{1,9},{5,13},{9,1},{13,5},{2,10},{6,14},... | collective-permute-start | bytes 196616 | tf_op jit(solution)/shard_map/ppermute | solution.py:38
  40.8 5.7 %collective-permute-start.16 = (bf16[64,512]{1,0:T(8,128)(2,1)S(1)}, bf16[64,512]{1,0:T(8,128)(2,1)S(1)}, u32[]{:S(2)}, u32[]{:S(2)}) collective-permute-start(bf16[64,512]{1,0:T(8,128)(2,1)S(1)} %get-tuple-element.60), channel_id=1, source_target_pairs={{0,12},{4,8},{8,4},{12,0},{1,13},{5,9},{9,5},{13,1},{2,14},{6,10},... | collective-permute-start | bytes 196616 | tf_op jit(solution)/shard_map/ppermute | solution.py:38
